TPU v7x, 32 devices: a whole 2x2x4 slice. The times are simulated.
32 devices in a mesh: dp: 8 (over z, y), tp: 4 (over x, core).
Axes of the slice: x: 2, y: 2, z: 4, core: 2. Of those that a mesh axis runs over, the one named last changes fastest.
Arguments:
- tokens: bfloat16 [8192, 1536], P('dp'), may hold values from -6 to 6
- text: bfloat16 [2048, 4096], P('dp'), may hold values from -6 to 6
- cond: bfloat16 [8, 1024], P('dp'), may hold values from -6 to 6
- frames: int32 [8], P('dp'), may hold values from 4 to 16, as said below
- w_query: bfloat16 [1536, 1536], P('dp', 'tp'), may hold values from -0.15625 to 0.15625
- w_key: bfloat16 [1536, 1536], P('dp', 'tp'), may hold values from -0.15625 to 0.15625
- w_value: bfloat16 [1536, 1536], P('dp', 'tp'), may hold values from -0.15625 to 0.15625
- w_out: bfloat16 [1536, 1536], P('tp', 'dp'), may hold values from -2.5 to 2.5
- w_text_key: bfloat16 [4096, 1536], P('dp', 'tp'), may hold values from -0.09375 to 0.09375
- w_text_value: bfloat16 [4096, 1536], P('dp', 'tp'), may hold values from -0.09375 to 0.09375
- w_gate: bfloat16 [1536, 4096], P('dp', 'tp'), may hold values from -0.15625 to 0.15625
- w_up: bfloat16 [1536, 4096], P('dp', 'tp'), may hold values from -0.15625 to 0.15625
- w_down: bfloat16 [4096, 1536], P('tp', 'dp'), may hold values from -0.09375 to 0.09375
- w_ada: bfloat16 [1024, 6144], P('dp'), may hold values from -0.1875 to 0.1875
- ada_bias: bfloat16 [6144], P('dp'), may hold values from -3 to 3
- norm_one: bfloat16 [1536], P('dp'), may hold values from 0.5 to 1.5
- norm_two: bfloat16 [1536], P('dp'), may hold values from 0.5 to 1.5
- query_gain: bfloat16 [1536], P('tp'), may hold values from 0.5 to 1.5
- key_gain: bfloat16 [1536], P('tp'), may hold values from 0.5 to 1.5
- text_key_gain: bfloat16 [1536], P('tp'), may hold values from 0.5 to 1.5
- cross_gate: bfloat16 [24], P('tp'), may hold values from -1.5 to 1.5
- cotangent: bfloat16 [8192, 1536], P('dp'), may hold values from -6 to 6
Outputs:
- block_out: bfloat16 [8192, 1536], P('dp')
- grad_tokens: bfloat16 [8192, 1536], P('dp')
- grad_query: float32 [1536, 1536], P('dp', 'tp')
- grad_key: float32 [1536, 1536], P('dp', 'tp')
- grad_value: float32 [1536, 1536], P('dp', 'tp')
- grad_out: float32 [1536, 1536], P('tp', 'dp')
- grad_text_key: float32 [4096, 1536], P('dp', 'tp')
- grad_text_value: float32 [4096, 1536], P('dp', 'tp')
- grad_gate: float32 [1536, 4096], P('dp', 'tp')
- grad_up: float32 [1536, 4096], P('dp', 'tp')
- grad_down: float32 [4096, 1536], P('tp', 'dp')
- grad_ada: float32 [1024, 6144], P('dp')
- grad_ada_bias: float32 [6144], P('dp')
- grad_norm_one: float32 [1536], P('dp')
- grad_norm_two: float32 [1536], P('dp')
- grad_query_gain: float32 [1536], P('tp')
- grad_key_gain: float32 [1536], P('tp')
- grad_text_key_gain: float32 [1536], P('tp')
- grad_cross_gate: float32 [24], P('tp')
Inputs may be any that keep to these rules, and one draw needn't show every extreme that they name: Clip c has frames[c] frames of 64 tokens, the last of each frame being its nextframe token, and occupies the first frames[c] * 64 of its 1024 slots. Every draw has a clip of 16 frames and one of 4 frames.
All inputs are finite; a program needn't handle non-finite values.
Results may differ from a plain program's by a relative error of at most 0.019.
Values may be sent and summed in bfloat16 or wider, within the bound.
A program may use at most 256 MiB of HBM per device.

v0:
```python
import jax
import jax.numpy as jnp
from jax import lax
from jax.sharding import PartitionSpec as P

HEAD = 64
FRAME_TOK = 64


EPS = 1e-06
ROPE_BASE = 10000.0
MASKED = -1e30


def exact_dot(left, right):
    return jnp.dot(left, right, precision=lax.Precision.HIGHEST, preferred_element_type=jnp.float32)


def rope_flat(row_count, width):
    lane = jnp.arange(width, dtype=jnp.int32)
    within = lane % HEAD
    quarter = HEAD // 4
    which = within // quarter
    offset = within % quarter
    freqs = ROPE_BASE ** (-offset.astype(jnp.float32) / quarter)
    row_index = jnp.arange(row_count, dtype=jnp.int32)
    frame_pos = (row_index // FRAME_TOK).astype(jnp.float32)
    place_pos = (row_index % FRAME_TOK).astype(jnp.float32)
    position = jnp.where(which[None, :] < 2, frame_pos[:, None], place_pos[:, None])
    angles = position * freqs[None, :]
    source = lane - within + (which ^ 1) * quarter + offset
    signs = jnp.where(which % 2 == 0, -1.0, 1.0).astype(jnp.float32)
    turner = (lane[:, None] == source[None, :]).astype(jnp.float32) * signs[None, :]
    return (jnp.cos(angles), jnp.sin(angles), turner)


def rotate_flat(value, cosine_table, sine_table, turner):
    return value * cosine_table + exact_dot(value, turner) * sine_table


def rotate_flat_back(grad, cosine_table, sine_table, turner):
    return grad * cosine_table + exact_dot(grad * sine_table, turner.T)


def rms_parts(value):
    inverse = lax.rsqrt(jnp.mean(value * value, axis=-1, keepdims=True) + EPS)
    return (inverse, value * inverse)


def rms_back(inverse, normed, grad):
    return inverse * (grad - normed * jnp.mean(grad * normed, axis=-1, keepdims=True))


def head_norm(value, segment):
    inverse = lax.rsqrt(exact_dot(value * value, segment) / HEAD + EPS)
    inverse_wide = exact_dot(inverse, segment.T)
    return (inverse_wide, value * inverse_wide)


def head_norm_back(inverse_wide, normed, grad, segment):
    average = exact_dot(exact_dot(grad * normed, segment) / HEAD, segment.T)
    return inverse_wide * (grad - normed * average)


def to_heads(value):
    return value.reshape(value.shape[0], -1, HEAD).transpose(1, 0, 2)


def from_heads(value):
    return value.transpose(1, 0, 2).reshape(value.shape[1], -1)


def attend(query_block, keys, values, key_valid, score_scale):
    scores = (
        jnp.einsum("hqd,hkd->hqk", query_block, keys, preferred_element_type=jnp.float32)
        * score_scale
    )
    if key_valid is not None:
        scores = jnp.where(key_valid, scores, MASKED)
    maximum = jnp.max(scores, axis=-1, keepdims=True)
    expo = jnp.exp(scores - maximum)
    denominator = jnp.sum(expo, axis=-1, keepdims=True)
    probability = (expo / denominator).astype(jnp.bfloat16)
    outputs = jnp.einsum("hqk,hkd->hqd", probability, values, preferred_element_type=jnp.float32)
    return (outputs, maximum + jnp.log(denominator))


def attend_back(query_block, keys, values, key_valid, score_scale, log_total, grad_outputs):
    scores = (
        jnp.einsum("hqd,hkd->hqk", query_block, keys, preferred_element_type=jnp.float32)
        * score_scale
    )
    if key_valid is not None:
        scores = jnp.where(key_valid, scores, MASKED)
    probability = jnp.exp(scores - log_total)
    grad_values = jnp.einsum(
        "hqk,hqd->hkd",
        probability.astype(jnp.bfloat16),
        grad_outputs,
        preferred_element_type=jnp.float32,
    )
    grad_probs = jnp.einsum(
        "hqd,hkd->hqk", grad_outputs, values, preferred_element_type=jnp.float32
    )
    grad_scores = probability * (
        grad_probs - jnp.sum(probability * grad_probs, axis=-1, keepdims=True)
    )
    grad_scores = grad_scores.astype(jnp.bfloat16)
    grad_query = (
        jnp.einsum("hqk,hkd->hqd", grad_scores, keys, preferred_element_type=jnp.float32)
        * score_scale
    )
    grad_keys = (
        jnp.einsum("hqk,hqd->hkd", grad_scores, query_block, preferred_element_type=jnp.float32)
        * score_scale
    )
    return (grad_query, grad_keys, grad_values)


def fetch(
    w_query,
    w_key,
    w_value,
    w_out,
    w_text_key,
    w_text_value,
    w_gate,
    w_up,
    w_down,
    ada_bias,
    norm_one,
    norm_two,
):
    return (
        lax.all_gather(w_query, "dp", axis=0, tiled=True),
        lax.all_gather(w_key, "dp", axis=0, tiled=True),
        lax.all_gather(w_value, "dp", axis=0, tiled=True),
        lax.all_gather(w_out, "dp", axis=1, tiled=True),
        lax.all_gather(w_text_key, "dp", axis=0, tiled=True),
        lax.all_gather(w_text_value, "dp", axis=0, tiled=True),
        lax.all_gather(w_gate, "dp", axis=0, tiled=True),
        lax.all_gather(w_up, "dp", axis=0, tiled=True),
        lax.all_gather(w_down, "dp", axis=1, tiled=True),
        lax.all_gather(ada_bias, "dp", axis=0, tiled=True),
        lax.all_gather(norm_one, "dp", axis=0, tiled=True),
        lax.all_gather(norm_two, "dp", axis=0, tiled=True),
    )


def on_device(
    tokens,
    text,
    cond,
    frames,
    w_query,
    w_key,
    w_value,
    w_out,
    w_text_key,
    w_text_value,
    w_gate,
    w_up,
    w_down,
    w_ada,
    ada_bias,
    norm_one,
    norm_two,
    query_gain,
    key_gain,
    text_key_gain,
    cross_gate,
    cotangent,
):
    row_count = tokens.shape[0]
    text_count = text.shape[0]
    fetched = fetch(
        w_query,
        w_key,
        w_value,
        w_out,
        w_text_key,
        w_text_value,
        w_gate,
        w_up,
        w_down,
        ada_bias,
        norm_one,
        norm_two,
    )
    (
        full_query,
        full_key,
        full_value,
        full_out,
        full_text_key,
        full_text_value,
        full_gate,
        full_up,
        full_down,
        bias_full,
        gain_one,
        gain_two,
    ) = fetched
    local_cols = full_query.shape[1]
    heads_here = local_cols // HEAD
    segment = (
        jnp.arange(local_cols, dtype=jnp.int32)[:, None] // HEAD
        == jnp.arange(heads_here, dtype=jnp.int32)[None, :]
    ).astype(jnp.float32)
    token_values = tokens.astype(jnp.float32)
    activated = jax.nn.silu(cond.astype(jnp.float32)).astype(jnp.bfloat16)
    ada_full = lax.all_gather(w_ada, "dp", axis=0, tiled=True)
    modulation = jnp.dot(activated, ada_full, preferred_element_type=jnp.float32)
    modulation = modulation[0] + bias_full.astype(jnp.float32)
    scale_attn, gate_attn, scale_ffn, gate_ffn = jnp.split(modulation, 4)
    row_index = jnp.arange(row_count, dtype=jnp.int32)
    length = frames[0] * FRAME_TOK
    row_valid = row_index < length
    live_rows = row_valid.astype(jnp.float32)[:, None]
    key_valid = row_valid[None, None, :]
    inv_one, hat_one = rms_parts(token_values)
    mult_one = gain_one.astype(jnp.float32) * (1.0 + scale_attn)
    h_one = (hat_one * mult_one).astype(jnp.bfloat16)
    query_pre = jnp.dot(h_one, full_query, preferred_element_type=jnp.float32)
    key_pre = jnp.dot(h_one, full_key, preferred_element_type=jnp.float32)
    values = to_heads(
        jnp.dot(h_one, full_value, preferred_element_type=jnp.float32).astype(jnp.bfloat16)
    )
    qgain = query_gain.astype(jnp.float32)
    kgain = key_gain.astype(jnp.float32)
    kygain = text_key_gain.astype(jnp.float32)
    inv_query, hat_query = head_norm(query_pre, segment)
    inv_key, hat_key = head_norm(key_pre, segment)
    query_norm = hat_query * qgain
    cosine_table, sine_table, turner = rope_flat(row_count, local_cols)
    query_rot = to_heads(
        rotate_flat(query_norm, cosine_table, sine_table, turner).astype(jnp.bfloat16)
    )
    key_rot = to_heads(
        rotate_flat(hat_key * kgain, cosine_table, sine_table, turner).astype(jnp.bfloat16)
    )
    query_text = to_heads(query_norm.astype(jnp.bfloat16))
    text_pre = jnp.dot(text, full_text_key, preferred_element_type=jnp.float32)
    inv_text, hat_text = head_norm(text_pre, segment)
    text_keys = to_heads((hat_text * kygain).astype(jnp.bfloat16))
    text_values = to_heads(
        jnp.dot(text, full_text_value, preferred_element_type=jnp.float32).astype(jnp.bfloat16)
    )
    score_scale = HEAD ** (-0.5)
    block_rows = min(512, row_count)
    self_parts, self_totals, text_parts, text_totals = ([], [], [], [])
    for start_row in range(0, row_count, block_rows):
        self_block, self_total = attend(
            query_rot[:, start_row : start_row + block_rows],
            key_rot,
            values,
            key_valid,
            score_scale,
        )
        text_block, text_total = attend(
            query_text[:, start_row : start_row + block_rows],
            text_keys,
            text_values,
            None,
            score_scale,
        )
        self_parts.append(self_block)
        self_totals.append(self_total)
        text_parts.append(text_block)
        text_totals.append(text_total)
    self_outs = from_heads(jnp.concatenate(self_parts, axis=1))
    text_outs = from_heads(jnp.concatenate(text_parts, axis=1))
    gate_tanh = jnp.tanh(cross_gate.astype(jnp.float32))
    gate_wide = jnp.repeat(gate_tanh, HEAD)
    mixed = (self_outs + gate_wide[None, :] * text_outs).astype(jnp.bfloat16)
    attn_sum = lax.psum(
        jnp.dot(mixed, full_out, preferred_element_type=jnp.float32).astype(jnp.bfloat16), "tp"
    ).astype(jnp.float32)
    tanh_attn = jnp.tanh(gate_attn)
    hidden_state = token_values + live_rows * tanh_attn * attn_sum
    inv_two, hat_two = rms_parts(hidden_state)
    mult_two = gain_two.astype(jnp.float32) * (1.0 + scale_ffn)
    h_two = (hat_two * mult_two).astype(jnp.bfloat16)
    gate_pre = jnp.dot(h_two, full_gate, preferred_element_type=jnp.float32)
    up_pre = jnp.dot(h_two, full_up, preferred_element_type=jnp.float32)
    logistic = jax.nn.sigmoid(gate_pre)
    swish = gate_pre * logistic
    hidden_units = (swish * up_pre).astype(jnp.bfloat16)
    ffn_sum = lax.psum(
        jnp.dot(hidden_units, full_down, preferred_element_type=jnp.float32).astype(jnp.bfloat16),
        "tp",
    ).astype(jnp.float32)
    tanh_ffn = jnp.tanh(gate_ffn)
    result = hidden_state + live_rows * tanh_ffn * ffn_sum
    grad_result = cotangent.astype(jnp.float32)
    grad_ffn = (live_rows * tanh_ffn * grad_result).astype(jnp.bfloat16)
    grad_gate_ffn = jnp.sum(live_rows * ffn_sum * grad_result, axis=0) * (1.0 - tanh_ffn * tanh_ffn)
    grad_hidden = jnp.dot(grad_ffn, full_down.T, preferred_element_type=jnp.float32)
    grad_gate_pre = (grad_hidden * up_pre * logistic * (1.0 + gate_pre * (1.0 - logistic))).astype(
        jnp.bfloat16
    )
    grad_up_pre = (grad_hidden * swish).astype(jnp.bfloat16)
    g_down = jnp.dot(hidden_units.T, grad_ffn, preferred_element_type=jnp.float32)
    g_gate = jnp.dot(h_two.T, grad_gate_pre, preferred_element_type=jnp.float32)
    g_up = jnp.dot(h_two.T, grad_up_pre, preferred_element_type=jnp.float32)
    grad_n_two = lax.psum(
        (
            jnp.dot(grad_gate_pre, full_gate.T, preferred_element_type=jnp.float32)
            + jnp.dot(grad_up_pre, full_up.T, preferred_element_type=jnp.float32)
        ).astype(jnp.bfloat16),
        "tp",
    ).astype(jnp.float32)
    g_norm_two = jnp.sum(grad_n_two * hat_two * (1.0 + scale_ffn), axis=0)
    grad_scale_ffn = jnp.sum(grad_n_two * hat_two * gain_two.astype(jnp.float32), axis=0)
    grad_state = grad_result + rms_back(inv_two, hat_two, grad_n_two * mult_two)
    grad_attn = (live_rows * tanh_attn * grad_state).astype(jnp.bfloat16)
    grad_gate_attn = jnp.sum(live_rows * attn_sum * grad_state, axis=0) * (
        1.0 - tanh_attn * tanh_attn
    )
    grad_mixed = jnp.dot(grad_attn, full_out.T, preferred_element_type=jnp.float32)
    g_out = jnp.dot(mixed.T, grad_attn, preferred_element_type=jnp.float32)
    column_cross = jnp.sum(grad_mixed * text_outs, axis=0)
    g_cross_gate = exact_dot(column_cross[None, :], segment)[0] * (1.0 - gate_tanh * gate_tanh)
    grad_self = to_heads(grad_mixed.astype(jnp.bfloat16))
    grad_text = to_heads((grad_mixed * gate_wide[None, :]).astype(jnp.bfloat16))
    grad_query_rot_parts, grad_query_text_parts = ([], [])
    grad_key_rot = jnp.zeros((heads_here, row_count, HEAD), jnp.float32)
    grad_values = jnp.zeros((heads_here, row_count, HEAD), jnp.float32)
    grad_text_keys = jnp.zeros((heads_here, text_count, HEAD), jnp.float32)
    grad_text_values = jnp.zeros((heads_here, text_count, HEAD), jnp.float32)
    for block_number, start_row in enumerate(range(0, row_count, block_rows)):
        rows_here = slice(start_row, start_row + block_rows)
        query_grad, key_grad, value_grad = attend_back(
            query_rot[:, rows_here],
            key_rot,
            values,
            key_valid,
            score_scale,
            self_totals[block_number],
            grad_self[:, rows_here],
        )
        grad_query_rot_parts.append(query_grad)
        grad_key_rot = grad_key_rot + key_grad
        grad_values = grad_values + value_grad
        query_grad, key_grad, value_grad = attend_back(
            query_text[:, rows_here],
            text_keys,
            text_values,
            None,
            score_scale,
            text_totals[block_number],
            grad_text[:, rows_here],
        )
        grad_query_text_parts.append(query_grad)
        grad_text_keys = grad_text_keys + key_grad
        grad_text_values = grad_text_values + value_grad
    grad_query_norm = rotate_flat_back(
        from_heads(jnp.concatenate(grad_query_rot_parts, axis=1)), cosine_table, sine_table, turner
    ) + from_heads(jnp.concatenate(grad_query_text_parts, axis=1))
    grad_key_norm = rotate_flat_back(from_heads(grad_key_rot), cosine_table, sine_table, turner)
    grad_text_flat = from_heads(grad_text_keys)
    g_query_gain = jnp.sum(grad_query_norm * hat_query, axis=0)
    g_key_gain = jnp.sum(grad_key_norm * hat_key, axis=0)
    g_text_gain = jnp.sum(grad_text_flat * hat_text, axis=0)
    grad_query_pre = head_norm_back(inv_query, hat_query, grad_query_norm * qgain, segment).astype(
        jnp.bfloat16
    )
    grad_key_pre = head_norm_back(inv_key, hat_key, grad_key_norm * kgain, segment).astype(
        jnp.bfloat16
    )
    grad_value_pre = from_heads(grad_values).astype(jnp.bfloat16)
    grad_text_pre = head_norm_back(inv_text, hat_text, grad_text_flat * kygain, segment).astype(
        jnp.bfloat16
    )
    grad_text_vals = from_heads(grad_text_values).astype(jnp.bfloat16)
    g_query = jnp.dot(h_one.T, grad_query_pre, preferred_element_type=jnp.float32)
    g_key = jnp.dot(h_one.T, grad_key_pre, preferred_element_type=jnp.float32)
    g_value = jnp.dot(h_one.T, grad_value_pre, preferred_element_type=jnp.float32)
    g_text_key = jnp.dot(text.T, grad_text_pre, preferred_element_type=jnp.float32)
    g_text_value = jnp.dot(text.T, grad_text_vals, preferred_element_type=jnp.float32)
    grad_n_one = lax.psum(
        (
            jnp.dot(grad_query_pre, full_query.T, preferred_element_type=jnp.float32)
            + jnp.dot(grad_key_pre, full_key.T, preferred_element_type=jnp.float32)
            + jnp.dot(grad_value_pre, full_value.T, preferred_element_type=jnp.float32)
        ).astype(jnp.bfloat16),
        "tp",
    ).astype(jnp.float32)
    g_norm_one = jnp.sum(grad_n_one * hat_one * (1.0 + scale_attn), axis=0)
    grad_scale_attn = jnp.sum(grad_n_one * hat_one * gain_one.astype(jnp.float32), axis=0)
    grad_input = grad_state + rms_back(inv_one, hat_one, grad_n_one * mult_one)
    grad_mod = jnp.concatenate([grad_scale_attn, grad_gate_attn, grad_scale_ffn, grad_gate_ffn])[
        None, :
    ]
    ada_local = activated.astype(jnp.float32).reshape(-1, 1) * grad_mod
    g_ada = lax.psum_scatter(ada_local, "dp", scatter_dimension=0, tiled=True)
    summed = (
        lax.psum_scatter(g_query, "dp", scatter_dimension=0, tiled=True),
        lax.psum_scatter(g_key, "dp", scatter_dimension=0, tiled=True),
        lax.psum_scatter(g_value, "dp", scatter_dimension=0, tiled=True),
        lax.psum_scatter(g_out, "dp", scatter_dimension=1, tiled=True),
        lax.psum_scatter(g_text_key, "dp", scatter_dimension=0, tiled=True),
        lax.psum_scatter(g_text_value, "dp", scatter_dimension=0, tiled=True),
        lax.psum_scatter(g_gate, "dp", scatter_dimension=0, tiled=True),
        lax.psum_scatter(g_up, "dp", scatter_dimension=0, tiled=True),
        lax.psum_scatter(g_down, "dp", scatter_dimension=1, tiled=True),
        lax.psum_scatter(grad_mod[0], "dp", scatter_dimension=0, tiled=True),
        lax.psum_scatter(g_norm_one, "dp", scatter_dimension=0, tiled=True),
        lax.psum_scatter(g_norm_two, "dp", scatter_dimension=0, tiled=True),
    )
    small_sums = lax.psum((g_query_gain, g_key_gain, g_text_gain, g_cross_gate), "dp")
    return (
        result.astype(jnp.bfloat16),
        grad_input.astype(jnp.bfloat16),
        summed[0],
        summed[1],
        summed[2],
        summed[3],
        summed[4],
        summed[5],
        summed[6],
        summed[7],
        summed[8],
        g_ada,
        summed[9],
        summed[10],
        summed[11],
        small_sums[0],
        small_sums[1],
        small_sums[2],
        small_sums[3],
    )


def solution(mesh):
    placed = (
        P("dp", None),
        P("dp", None),
        P("dp", None),
        P("dp"),
        P("dp", "tp"),
        P("dp", "tp"),
        P("dp", "tp"),
        P("tp", "dp"),
        P("dp", "tp"),
        P("dp", "tp"),
        P("dp", "tp"),
        P("dp", "tp"),
        P("tp", "dp"),
        P("dp", None),
        P("dp"),
        P("dp"),
        P("dp"),
        P("tp"),
        P("tp"),
        P("tp"),
        P("tp"),
        P("dp", None),
    )
    return jax.shard_map(
        on_device,
        mesh=mesh,
        in_specs=placed,
        out_specs=(
            P("dp", None),
            P("dp", None),
            P("dp", "tp"),
            P("dp", "tp"),
            P("dp", "tp"),
            P("tp", "dp"),
            P("dp", "tp"),
            P("dp", "tp"),
            P("dp", "tp"),
            P("dp", "tp"),
            P("tp", "dp"),
            P("dp", None),
            P("dp"),
            P("dp"),
            P("dp"),
            P("tp"),
            P("tp"),
            P("tp"),
            P("tp"),
        ),
        check_vma=False,
    )
```

profile of v0, /device:TPU:0, one launch (start us, length us, event | category | flops | bytes accessed | tf_op | source)
XLA Modules:
  0.0 2385.8 jit_solution(2681223203793855277)
XLA Ops:
  19.0 32.5 %all-gather = bf16[8,1,768]{2,1,0:T(2,128)(2,1)S(1)} all-gather(bf16[1,1,768]{2,1,0:T(2,128)(2,1)S(1)} %reshape.336), channel_id=1, replica_groups=mesh['dp'=8,'tp'=4] {'dp'}, dimensions={0}, use_global_device_ids=true | all-gather | bytes 13824 | tf_op jit(solution)/shard_map/all_gather | solution.py:144
  53.2 22.2 all-reduce.6
  78.8 57.4 %all-gather.20.cloned.1.call-done = bf16[4096,384]{1,0:T(8,128)(2,1)} async-done(((bf16[512,384]{1,0:T(8,128)(2,1)}), bf16[4096,384]{1,0:T(8,128)(2,1)}) %all-gather.20.cloned.1.call-update) | async-done | bytes 3145744 | tf_op jit(solution)/shard_map/all_gather | solution.py:139
  141.3 172.1 %all-gather.12.cloned.1.call-done = bf16[1024,6144]{1,0:T(8,128)(2,1)} async-done(((bf16[128,6144]{1,0:T(8,128)(2,1)}), bf16[1024,6144]{1,0:T(8,128)(2,1)}) %all-gather.12.cloned.1.call-update) | async-done | bytes 12582928 | tf_op jit(solution)/shard_map/all_gather | solution.py:212
  320.4 34.3 %all-gather.14.cloned.1.call-done = bf16[1536,384]{1,0:T(8,128)(2,1)} async-done(((bf16[192,384]{1,0:T(8,128)(2,1)}), bf16[1536,384]{1,0:T(8,128)(2,1)}) %all-gather.14.cloned.1.call-update) | async-done | bytes 1179664 | tf_op jit(solution)/shard_map/all_gather | solution.py:135
  366.5 30.2 %all-gather.16.cloned.1.call-done = bf16[1536,384]{1,0:T(8,128)(2,1)} async-done(((bf16[192,384]{1,0:T(8,128)(2,1)}), bf16[1536,384]{1,0:T(8,128)(2,1)}) %all-gather.16.cloned.1.call-update) | async-done | bytes 1179664 | tf_op jit(solution)/shard_map/all_gather | solution.py:136
  462.7 17.8 all-gather.24.cloned.1.call-done
  487.4 65.2 %all-reduce.12.cloned.1.call-done = bf16[1024,1536]{1,0:T(8,128)(2,1)} async-done(((bf16[1024,1536]{1,0:T(8,128)(2,1)}), bf16[1024,1536]{1,0:T(8,128)(2,1)}) %all-reduce.12.cloned.1.call-update) | async-done | bytes 3145744 | tf_op jit(solution)/shard_map/psum | solution.py:276
  560.6 54.8 %all-gather.28.cloned.1.call-done = bf16[1536,1024]{1,0:T(8,128)(2,1)} async-done(((bf16[192,1024]{1,0:T(8,128)(2,1)}), bf16[1536,1024]{1,0:T(8,128)(2,1)}) %all-gather.28.cloned.1.call-update) | async-done | bytes 3145744 | tf_op jit(solution)/shard_map/all_gather | solution.py:142
  623.7 52.9 %all-gather.26.cloned.1.call-done = bf16[1536,1024]{1,0:T(8,128)(2,1)} async-done(((bf16[192,1024]{1,0:T(8,128)(2,1)}), bf16[1536,1024]{1,0:T(8,128)(2,1)}) %all-gather.26.cloned.1.call-update) | async-done | bytes 3145744 | tf_op jit(solution)/shard_map/all_gather | solution.py:141
  684.9 52.9 %all-gather.30.cloned.1.call-done = bf16[1024,1536]{0,1:T(8,128)(2,1)} async-done(((bf16[1024,192]{0,1:T(8,128)(2,1)}), bf16[1024,1536]{0,1:T(8,128)(2,1)}) %all-gather.30.cloned.1.call-update) | async-done | bytes 3145744 | tf_op jit(solution)/shard_map/all_gather | solution.py:143
  762.1 117.8 %all-reduce.16.cloned.1.call-done = (bf16[1024,1536]{1,0:T(8,128)(2,1)}, bf16[1024,1536]{1,0:T(8,128)(2,1)}) async-done(((bf16[1024,1536]{1,0:T(8,128)(2,1)}, bf16[1024,1536]{1,0:T(8,128)(2,1)}), (bf16[1024,1536]{1,0:T(8,128)(2,1)}, bf16[1024,1536]{1,0:T(8,128)(2,1)})) %all-reduce.16.cloned.1.call-update) | async-done | bytes 6291472 | tf_op jit(solution)/shard_map/psum | solution.py:289
  912.6 20.6 multiply_reduce_fusion.1
  1099.9 41.0 %all-reduce.5 = (f32[6144]{0:T(1024)S(1)}, f32[1536]{0:T(1024)S(1)}, f32[1536]{0:T(1024)S(1)}, f32[384]{0:T(512)}, f32[384]{0:T(512)}, /*index=5*/f32[384]{0:T(512)}, f32[6]{0:T(128)}) all-reduce(f32[6144]{0:T(1024)S(1)} %pad_maximum_fusion.4, f32[1536]{0:T(1024)S(1)} %get-tuple-element.79, ...), channel_id=12, replica_groups=mesh['dp'=8,'tp'=4] {'dp'}, use_global_device_ids=true, to_apply=%region_34.35.clone | all-reduce | flops 10374 | bytes 82992
  1149.6 49.3 %reduce-scatter.19.cloned.1.call-done = f32[512,384]{0,1:T(8,128)} async-done(((f32[4096,384]{0,1:T(8,128)}), f32[512,384]{0,1:T(8,128)}) %reduce-scatter.19.cloned.1.call-update) | async-done | bytes 786448 | tf_op jit(solution)/shard_map/reduce_scatter | solution.py:402
  1201.2 118.7 %reduce-scatter.21.cloned.1.call-done = f32[512,384]{0,1:T(8,128)} async-done(((f32[4096,384]{0,1:T(8,128)}), f32[512,384]{0,1:T(8,128)}) %reduce-scatter.21.cloned.1.call-update) | async-done | bytes 786448 | tf_op jit(solution)/shard_map/reduce_scatter | solution.py:403
  1322.2 69.8 %reduce-scatter.17.cloned.1.call-done = f32[384,192]{0,1:T(8,128)} async-done(((f32[384,1536]{0,1:T(8,128)}), f32[384,192]{0,1:T(8,128)}) %reduce-scatter.17.cloned.1.call-update) | async-done | bytes 294928 | tf_op jit(solution)/shard_map/reduce_scatter | solution.py:401
  1392.0 71.9 %reduce-scatter.15.cloned.1.call-done = f32[192,384]{1,0:T(8,128)} async-done(((f32[1536,384]{1,0:T(8,128)}), f32[192,384]{1,0:T(8,128)}) %reduce-scatter.15.cloned.1.call-update) | async-done | bytes 294928 | tf_op jit(solution)/shard_map/reduce_scatter | solution.py:400
  1463.9 71.9 %reduce-scatter.13.cloned.1.call-done = f32[192,384]{1,0:T(8,128)} async-done(((f32[1536,384]{1,0:T(8,128)}), f32[192,384]{1,0:T(8,128)}) %reduce-scatter.13.cloned.1.call-update) | async-done | bytes 294928 | tf_op jit(solution)/shard_map/reduce_scatter | solution.py:399
  1535.8 72.1 %reduce-scatter.11.cloned.1.call-done = f32[192,384]{1,0:T(8,128)} async-done(((f32[1536,384]{1,0:T(8,128)}), f32[192,384]{1,0:T(8,128)}) %reduce-scatter.11.cloned.1.call-update) | async-done | bytes 294928 | tf_op jit(solution)/shard_map/reduce_scatter | solution.py:398
  1608.0 121.1 %reduce-scatter.27.cloned.1.call-done = f32[1024,192]{0,1:T(8,128)} async-done(((f32[1024,1536]{0,1:T(8,128)}), f32[1024,192]{0,1:T(8,128)}) %reduce-scatter.27.cloned.1.call-update) | async-done | bytes 786448 | tf_op jit(solution)/shard_map/reduce_scatter | solution.py:406
  1729.0 121.3 %reduce-scatter.25.cloned.1.call-done = f32[192,1024]{1,0:T(8,128)} async-done(((f32[1536,1024]{1,0:T(8,128)}), f32[192,1024]{1,0:T(8,128)}) %reduce-scatter.25.cloned.1.call-update) | async-done | bytes 786448 | tf_op jit(solution)/shard_map/reduce_scatter | solution.py:405
  1850.4 121.3 %reduce-scatter.23.cloned.1.call-done = f32[192,1024]{1,0:T(8,128)} async-done(((f32[1536,1024]{1,0:T(8,128)}), f32[192,1024]{1,0:T(8,128)}) %reduce-scatter.23.cloned.1.call-update) | async-done | bytes 786448 | tf_op jit(solution)/shard_map/reduce_scatter | solution.py:404
  1971.7 407.4 %reduce-scatter.29.cloned.1.call-done = f32[128,6144]{1,0:T(8,128)} async-done(((f32[1024,6144]{1,0:T(8,128)}), f32[128,6144]{1,0:T(8,128)}) %reduce-scatter.29.cloned.1.call-update) | async-done | bytes 3145744 | tf_op jit(solution)/shard_map/reduce_scatter | solution.py:396
  (409 shorter events, 370.6 us)
Async XLA Ops:
  7.2 68.2 %all-gather.22.cloned.1.call-start = ((), (), s32[]{:S(2)}) async-start(), calls=%async_computation.15 | async-start | bytes 3538944 | tf_op jit(solution)/shard_map/all_gather | solution.py:140
  8.0 128.2 %all-gather.20.cloned.1.call-start = ((), (), s32[]{:S(2)}) async-start(), calls=%async_computation.14 | async-start | bytes 3538944 | tf_op jit(solution)/shard_map/all_gather | solution.py:139
  8.7 304.7 %all-gather.12.cloned.1.call-start = ((), (), s32[]{:S(2)}) async-start(), calls=%async_computation.10 | async-start | bytes 14155776 | tf_op jit(solution)/shard_map/all_gather | solution.py:212
  9.5 345.3 %all-gather.14.cloned.1.call-start = ((), (), s32[]{:S(2)}) async-start(), calls=%async_computation.11 | async-start | bytes 1327104 | tf_op jit(solution)/shard_map/all_gather | solution.py:135
  10.0 386.6 %all-gather.16.cloned.1.call-start = ((), (), s32[]{:S(2)}) async-start(), calls=%async_computation.12 | async-start | bytes 1327104 | tf_op jit(solution)/shard_map/all_gather | solution.py:136
  10.6 435.1 %all-gather.18.cloned.1.call-start = ((), (), s32[]{:S(2)}) async-start(), calls=%async_computation.13 | async-start | bytes 1327104 | tf_op jit(solution)/shard_map/all_gather | solution.py:137
  11.2 469.3 %all-gather.24.cloned.1.call-start = ((), (), s32[]{:S(2)}) async-start(), calls=%async_computation.16 | async-start | bytes 1327104 | tf_op jit(solution)/shard_map/all_gather | solution.py:138
  11.9 540.7 %all-reduce.12.cloned.1.call-start = ((), (), s32[]{:S(2)}) async-start(), calls=%async_computation.17 | async-start | bytes 6291456 | tf_op jit(solution)/shard_map/psum | solution.py:276
  19.0 426.7 %copy-start.65 = (f32[1024]{0:T(1024)}, f32[1024]{0:T(1024)S(1)}, u32[]{:S(2)}) copy-start(f32[1024]{0:T(1024)S(1)} %add_rsqrt_fusion.1) | copy-start | bytes 12292
  485.3 130.2 %all-gather.28.cloned.1.call-start = ((), (), s32[]{:S(2)}) async-start(), calls=%async_computation.19 | async-start | bytes 3538944 | tf_op jit(solution)/shard_map/all_gather | solution.py:142
  486.0 190.6 %all-gather.26.cloned.1.call-start = ((), (), s32[]{:S(2)}) async-start(), calls=%async_computation.18 | async-start | bytes 3538944 | tf_op jit(solution)/shard_map/all_gather | solution.py:141
  486.6 251.3 %all-gather.30.cloned.1.call-start = ((), (), s32[]{:S(2)}) async-start(), calls=%async_computation.20 | async-start | bytes 3538944 | tf_op jit(solution)/shard_map/all_gather | solution.py:143
  487.4 392.6 %all-reduce.16.cloned.1.call-start = ((), (), s32[]{:S(2)}) async-start(), calls=%async_computation.32 | async-start | bytes 12582912 | tf_op jit(solution)/shard_map/psum | solution.py:289
  761.4 320.2 %all-reduce.14.cloned.1.call-start = ((), (), s32[]{:S(2)}) async-start(), calls=%async_computation.21 | async-start | bytes 6291456 | tf_op jit(solution)/shard_map/psum | solution.py:381
  1006.9 192.0 %reduce-scatter.19.cloned.1.call-start = ((), (), s32[]{:S(2)}) async-start(), calls=%async_computation.26 | async-start | bytes 7077888 | tf_op jit(solution)/shard_map/reduce_scatter | solution.py:402
  1020.7 299.2 %reduce-scatter.21.cloned.1.call-start = ((), (), s32[]{:S(2)}) async-start(), calls=%async_computation.27 | async-start | bytes 7077888 | tf_op jit(solution)/shard_map/reduce_scatter | solution.py:403
  1029.1 362.8 %reduce-scatter.17.cloned.1.call-start = ((), (), s32[]{:S(2)}) async-start(), calls=%async_computation.25 | async-start | bytes 2654208 | tf_op jit(solution)/shard_map/reduce_scatter | solution.py:401
  1036.5 427.4 %reduce-scatter.15.cloned.1.call-start = ((), (), s32[]{:S(2)}) async-start(), calls=%async_computation.24 | async-start | bytes 2654208 | tf_op jit(solution)/shard_map/reduce_scatter | solution.py:400
  1042.3 493.5 %reduce-scatter.13.cloned.1.call-start = ((), (), s32[]{:S(2)}) async-start(), calls=%async_computation.23 | async-start | bytes 2654208 | tf_op jit(solution)/shard_map/reduce_scatter | solution.py:399
  1048.1 559.9 %reduce-scatter.11.cloned.1.call-start = ((), (), s32[]{:S(2)}) async-start(), calls=%async_computation.22 | async-start | bytes 2654208 | tf_op jit(solution)/shard_map/reduce_scatter | solution.py:398
  1054.2 674.9 %reduce-scatter.27.cloned.1.call-start = ((), (), s32[]{:S(2)}) async-start(), calls=%async_computation.30 | async-start | bytes 7077888 | tf_op jit(solution)/shard_map/reduce_scatter | solution.py:406
  1063.0 787.4 %reduce-scatter.25.cloned.1.call-start = ((), (), s32[]{:S(2)}) async-start(), calls=%async_computation.29 | async-start | bytes 7077888 | tf_op jit(solution)/shard_map/reduce_scatter | solution.py:405
  1071.8 899.8 %reduce-scatter.23.cloned.1.call-start = ((), (), s32[]{:S(2)}) async-start(), calls=%async_computation.28 | async-start | bytes 7077888 | tf_op jit(solution)/shard_map/reduce_scatter | solution.py:404
  1080.8 1298.3 %reduce-scatter.29.cloned.1.call-start = ((), (), s32[]{:S(2)}) async-start(), calls=%async_computation.31 | async-start | bytes 28311552 | tf_op jit(solution)/shard_map/reduce_scatter | solution.py:396
  (112 other events, 6559.0 us)
Sparse Core Ops, SparseCore 0:
  10.3 64.4 all-gather.21
  76.9 59.2 all-gather.19
  138.4 175.0 all-gather.11
  315.5 39.2 all-gather.13
  356.8 39.8 all-gather.15
  398.7 39.8 all-gather.17
  440.7 39.6 all-gather.23
  485.4 67.1 all-reduce.11
  554.8 60.5 all-gather.27
  617.5 59.0 all-gather.25
  678.8 59.0 all-gather.29
  761.5 118.3 all-reduce.15
  1007.1 68.6 all-reduce.13
  1079.2 119.6 reduce-scatter.18
  1202.4 117.5 reduce-scatter.20
  1323.8 68.0 reduce-scatter.16
  1395.9 67.9 reduce-scatter.14
  1467.8 67.9 reduce-scatter.12
  1539.9 68.0 reduce-scatter.10
  1612.0 117.0 reduce-scatter.26
  1733.2 117.1 reduce-scatter.24
  1854.5 117.0 reduce-scatter.22
  1976.1 402.8 reduce-scatter.28
where the time goes:
time: 2390 us
  waiting for transfers between devices  1890 us (79%)
  matrix products  267 us (11%)
  blocking collectives  95.6 us (4%)
  other arithmetic  87 us (4%)
  local copies, waits for them, and re-layouts  28.7 us (1%)
    reduce_scatter x1, waiting for transfers between devices, on_device(): g_ada = lax.psum_scatter(ada_local, 'dp', scatter_dimension=0, tiled=True)  407 us
    all_gather x1, waiting for transfers between devices, on_device(): ada_full = lax.all_gather(w_ada, 'dp', axis=0, tiled=True)  172 us
    reduce_scatter x1, waiting for transfers between devices, on_device(): lax.psum_scatter(g_up, 'dp', scatter_dimension=0, tiled=True)  121 us
    reduce_scatter x1, waiting for transfers between devices, on_device(): lax.psum_scatter(g_gate, 'dp', scatter_dimension=0, tiled=True)  121 us
    reduce_scatter x1, waiting for transfers between devices, on_device(): lax.psum_scatter(g_down, 'dp', scatter_dimension=1, tiled=True)  121 us
    reduce_scatter x1, waiting for transfers between devices, on_device(): lax.psum_scatter(g_text_value, 'dp', scatter_dimension=0, tiled=True)  119 us
    psum x1, waiting for transfers between devices, on_device(): lax.psum(jnp.dot(hidden_units, full_down, preferred_element_type=jnp.floa...  118 us
    reduce_scatter x1, waiting for transfers between devices, on_device(): lax.psum_scatter(g_query, 'dp', scatter_dimension=0, tiled=True)  72.1 us
  transfers between devices with their start and end apart: 23, of which 20 were waited for; matrix products, arithmetic and copies ran while one was open for 9% of the time, Pallas kernels for 0%

commit v1 on v0

--- a/solution.py
+++ b/solution.py
@@ -1,6 +1,10 @@
+import functools
+
 import jax
 import jax.numpy as jnp
 from jax import lax
+from jax.experimental import pallas as pl
+from jax.experimental.pallas import tpu as pltpu
 from jax.sharding import PartitionSpec as P
 
 HEAD = 64
@@ -117,34 +121,448 @@
     return (grad_query, grad_keys, grad_values)
 
 
-def fetch(
-    w_query,
-    w_key,
-    w_value,
-    w_out,
-    w_text_key,
-    w_text_value,
-    w_gate,
-    w_up,
-    w_down,
-    ada_bias,
-    norm_one,
-    norm_two,
-):
-    return (
-        lax.all_gather(w_query, "dp", axis=0, tiled=True),
-        lax.all_gather(w_key, "dp", axis=0, tiled=True),
-        lax.all_gather(w_value, "dp", axis=0, tiled=True),
-        lax.all_gather(w_out, "dp", axis=1, tiled=True),
-        lax.all_gather(w_text_key, "dp", axis=0, tiled=True),
-        lax.all_gather(w_text_value, "dp", axis=0, tiled=True),
-        lax.all_gather(w_gate, "dp", axis=0, tiled=True),
-        lax.all_gather(w_up, "dp", axis=0, tiled=True),
-        lax.all_gather(w_down, "dp", axis=1, tiled=True),
-        lax.all_gather(ada_bias, "dp", axis=0, tiled=True),
-        lax.all_gather(norm_one, "dp", axis=0, tiled=True),
-        lax.all_gather(norm_two, "dp", axis=0, tiled=True),
-    )
+MESH = pl.DeviceIdType.MESH
+VMEM_LIMIT = 60 * 2**20
+GRID = 8
+LINE = 4
+
+
+def remote(src, dst, send, recv, **where):
+    return pltpu.make_async_remote_copy(
+        src_ref=src, dst_ref=dst, send_sem=send, recv_sem=recv, device_id=where, device_id_type=MESH
+    )
+
+
+def greet(axis, others):
+    barrier = pltpu.get_barrier_semaphore()
+    for other in others:
+        pl.semaphore_signal(barrier, inc=1, device_id={axis: other}, device_id_type=MESH)
+    pl.semaphore_wait(barrier, len(others))
+
+
+def add_rows(out_ref, first, *others):
+    rows = out_ref.shape[0]
+
+    def step(i, carry):
+        here = pl.ds(pl.multiple_of(i * 16, 16), 16)
+        total = first[here, :].astype(jnp.float32)
+        for other in others:
+            total = total + other[here, :].astype(jnp.float32)
+        out_ref[here, :] = total.astype(out_ref.dtype)
+        return carry
+
+    lax.fori_loop(0, rows // 16, step, 0)
+
+
+def gather_kernel(chunks, n_in, n_out, *refs):
+    shards, refs = refs[:n_in], refs[n_in:]
+    cond_ref, small_ref, ada_ref = refs[:3]
+    fulls, refs = refs[3 : 3 + n_out], refs[3 + n_out :]
+    mod_ref, smalls_ref, act_ref = refs[:3]
+    (conds, part, parts, up_s, up_r, dn_s, dn_r, y_s, y_r, own_sem, c_s, c_r, m_s, m_r, p_s, p_r) = refs[3:]
+    me = lax.axis_index("dp")
+    z, y = me // 2, lax.rem(me, 2)
+    count = len(chunks)
+    peers = [lax.rem(me + step, GRID) for step in range(1, GRID)]
+    sources = [lax.rem(me + GRID - step, GRID) for step in range(1, GRID)]
+    greet("dp", peers)
+
+    def own(c):
+        at, row, rows, col, cols = chunks[c][:5]
+        return shards[at].at[pl.ds(row, rows), pl.ds(col, cols)]
+
+    def place(c, origin):
+        _, row, rows, _, cols, out, depth, out_col = chunks[c]
+        start = pl.multiple_of(origin * depth + row, 16)
+        return fulls[out].at[pl.ds(start, rows), pl.ds(out_col, cols)]
+
+    def up(c, hop):
+        origin = me - 2 * hop
+        src = own(c) if hop == 0 else place(c, origin)
+        return remote(src, place(c, origin), up_s.at[c, hop], up_r.at[c, hop], dp=me + 2)
+
+    def down(c, hop):
+        origin = me + 2 * hop
+        src = own(c) if hop == 0 else place(c, origin)
+        return remote(src, place(c, origin), dn_s.at[c, hop], dn_r.at[c, hop], dp=me - 2)
+
+    def across(c, line):
+        origin = 2 * line + y
+        return remote(place(c, origin), place(c, origin), y_s.at[c, line], y_r.at[c, line], dp=me + 1 - 2 * y)
+
+    def across_own(c):
+        return remote(own(c), place(c, me), y_s.at[c, z], y_r.at[c, z], dp=me + 1 - 2 * y)
+
+    def came_up(c, hop):
+        origin = me - 2 * (hop + 1)
+        return remote(place(c, origin), place(c, origin), up_s.at[c, hop], up_r.at[c, hop], dp=me)
+
+    def came_down(c, hop):
+        origin = me + 2 * (hop + 1)
+        return remote(place(c, origin), place(c, origin), dn_s.at[c, hop], dn_r.at[c, hop], dp=me)
+
+    def came_across(c, line):
+        origin = 2 * line + 1 - y
+        return remote(place(c, origin), place(c, origin), y_s.at[c, line], y_r.at[c, line], dp=me)
+
+    def local(c):
+        return pltpu.make_async_copy(own(c), place(c, me), own_sem.at[c])
+
+    def pump(t):
+        if t < count:
+            pl.when(z < LINE - 1)(lambda: up(t, 0).start())
+            pl.when(z > 0)(lambda: down(t, 0).start())
+            across_own(t).start()
+            local(t).start()
+        for hop in range(LINE - 1):
+            c = t - 1 - hop
+            if not 0 <= c < count:
+                continue
+
+            @pl.when(z - 1 - hop >= 0)
+            def _():
+                came_up(c, hop).wait_recv()
+                if hop < LINE - 2:
+                    pl.when(z < LINE - 1)(lambda: up(c, hop + 1).start())
+                across(c, z - 1 - hop).start()
+
+            @pl.when(z + 1 + hop <= LINE - 1)
+            def _():
+                came_down(c, hop).wait_recv()
+                if hop < LINE - 2:
+                    pl.when(z > 0)(lambda: down(c, hop + 1).start())
+                across(c, z + 1 + hop).start()
+
+    pump(0)
+    for step in range(1, GRID):
+        there = peers[step - 1]
+        remote(cond_ref.at[there], conds.at[me], c_s.at[step - 1], c_r.at[step - 1], dp=there).start()
+        remote(small_ref, smalls_ref.at[me], m_s.at[step - 1], m_r.at[step - 1], dp=there).start()
+    conds[pl.ds(me, 1)] = cond_ref[pl.ds(me, 1)]
+    smalls_ref[pl.ds(me, 1)] = small_ref[...][None]
+    pump(1)
+    for step in range(1, GRID):
+        here = sources[step - 1]
+        remote(conds.at[here], conds.at[here], c_s.at[step - 1], c_r.at[step - 1], dp=me).wait_recv()
+    cond = jnp.concatenate([conds[i] for i in range(GRID)], axis=0)
+    act = (cond * (1.0 / (1.0 + jnp.exp(-cond)))).astype(jnp.bfloat16)
+    act_ref[...] = act.astype(jnp.float32)
+    width = ada_ref.shape[1] // 4
+    for i in range(4):
+        cols = pl.ds(i * width, width)
+        product = jnp.dot(act, ada_ref[:, cols], preferred_element_type=jnp.float32)
+        for j in range(GRID):
+            part[j, :, cols] = product[j : j + 1, :]
+    for step in range(1, GRID):
+        there = peers[step - 1]
+        remote(part.at[there], parts.at[me], p_s.at[step - 1], p_r.at[step - 1], dp=there).start()
+    parts[pl.ds(me, 1)] = part[pl.ds(me, 1)]
+    pump(2)
+    for step in range(1, GRID):
+        here = sources[step - 1]
+        remote(parts.at[here], parts.at[here], p_s.at[step - 1], p_r.at[step - 1], dp=me).wait_recv()
+    mod_ref[...] = sum(parts[i] for i in range(GRID))
+    for t in range(3, count + LINE):
+        pump(t)
+    for c in range(count):
+        for line in range(LINE):
+            came_across(c, line).wait_recv()
+        local(c).wait()
+        for hop in range(LINE - 1):
+            pl.when((z < LINE - 1) & (z - hop >= 0))(lambda: up(c, hop).wait_send())
+            pl.when((z > 0) & (z + hop <= LINE - 1))(lambda: down(c, hop).wait_send())
+        for line in range(LINE):
+            across(c, line).wait_send()
+    for step in range(1, GRID):
+        here, there = sources[step - 1], peers[step - 1]
+        remote(small_ref, smalls_ref.at[here], m_s.at[step - 1], m_r.at[step - 1], dp=me).wait_recv()
+        remote(cond_ref.at[there], conds.at[me], c_s.at[step - 1], c_r.at[step - 1], dp=there).wait_send()
+        remote(small_ref, smalls_ref.at[me], m_s.at[step - 1], m_r.at[step - 1], dp=there).wait_send()
+        remote(part.at[there], parts.at[me], p_s.at[step - 1], p_r.at[step - 1], dp=there).wait_send()
+
+
+def gather_all(shards, groups, cond, small, w_ada):
+    chunks, outs = [], []
+    for at, group in enumerate(groups):
+        col = 0
+        depth = shards[group[0]].shape[0]
+        for member in group:
+            wide = shards[member].shape[1]
+            tall = min(256, depth)
+            step = 384 if wide % 384 == 0 else 512
+            for row in range(0, depth, tall):
+                for part in range(0, wide, step):
+                    chunks.append((member, row, tall, part, step, at, depth, col + part))
+            col += wide
+        outs.append(jax.ShapeDtypeStruct((GRID * depth, col), jnp.bfloat16))
+    count = len(chunks)
+    any_spec = pl.BlockSpec(memory_space=pl.ANY)
+    in_vmem = pl.BlockSpec(memory_space=pltpu.VMEM)
+    wide = w_ada.shape[1]
+    dma = pltpu.SemaphoreType.DMA
+    return pl.pallas_call(
+        functools.partial(gather_kernel, chunks, len(shards), len(outs)),
+        out_shape=outs
+        + [
+            jax.ShapeDtypeStruct((1, wide), jnp.float32),
+            jax.ShapeDtypeStruct((GRID,) + small.shape, jnp.float32),
+            jax.ShapeDtypeStruct((GRID, cond.shape[2]), jnp.float32),
+        ],
+        in_specs=[any_spec] * len(shards) + [in_vmem] * 3,
+        out_specs=[any_spec] * len(outs) + [in_vmem] * 3,
+        scratch_shapes=[
+            pltpu.VMEM((GRID, 1, cond.shape[2]), jnp.float32),
+            pltpu.VMEM((GRID, 1, wide), jnp.float32),
+            pltpu.VMEM((GRID, 1, wide), jnp.float32),
+            dma((count, 3)),
+            dma((count, 3)),
+            dma((count, 3)),
+            dma((count, 3)),
+            dma((count, 4)),
+            dma((count, 4)),
+            dma((count,)),
+        ]
+        + [dma((GRID - 1,))] * 6,
+        compiler_params=pltpu.CompilerParams(
+            collective_id=0, has_side_effects=True, vmem_limit_bytes=VMEM_LIMIT
+        ),
+    )(*shards, cond, small, w_ada)
+
+
+def scatter_kernel(chunks, n_in, n_out, *refs):
+    grads, refs = refs[:n_in], refs[n_in:]
+    vec_ref, refs = refs[0], refs[1:]
+    outs, refs = refs[:n_out], refs[n_out:]
+    vecs_ref, refs = refs[0], refs[1:]
+    sets, refs = (refs[:4], refs[4:8], refs[8:12]), refs[12:]
+    y_s, y_r, own_sem, up_s, up_r, dn_s, dn_r, v_s, v_r = refs
+    me = lax.axis_index("dp")
+    z, y = me // 2, lax.rem(me, 2)
+    count = len(chunks)
+    peers = [lax.rem(me + step, GRID) for step in range(1, GRID)]
+    sources = [lax.rem(me + GRID - step, GRID) for step in range(1, GRID)]
+    greet("dp", peers)
+    for step in range(1, GRID):
+        there = peers[step - 1]
+        remote(vec_ref, vecs_ref.at[me], v_s.at[step - 1], v_r.at[step - 1], dp=there).start()
+    vecs_ref[pl.ds(me, 1)] = vec_ref[...][None]
+
+    def buffers(c):
+        which, slot = chunks[c][:2]
+        return [ref.at[slot] for ref in sets[which]]
+
+    def mine(c, row_y):
+        _, _, at, row, rows, col, cols = chunks[c][:7]
+        return grads[at].at[:, row_y, pl.ds(row, rows), pl.ds(col, cols)]
+
+    def across(c):
+        return remote(mine(c, 1 - y), buffers(c)[1], y_s.at[c], y_r.at[c], dp=me + 1 - 2 * y)
+
+    def load(c):
+        return pltpu.make_async_copy(mine(c, y), buffers(c)[0], own_sem.at[c])
+
+    def up(c, line):
+        held, _, above, _ = buffers(c)
+        return remote(held.at[line], above.at[line - 1], up_s.at[c, line - 1], up_r.at[c, line - 1], dp=me + 2)
+
+    def down(c, line):
+        held, _, _, below = buffers(c)
+        return remote(held.at[line], below.at[line], dn_s.at[c, line], dn_r.at[c, line], dp=me - 2)
+
+    def fold(c):
+        held, crossed, _, _ = buffers(c)
+        across(c).wait_recv()
+        load(c).wait()
+        for line in range(LINE):
+            add_rows(held.at[line], held.at[line], crossed.at[line])
+
+    def send_up(c, here):
+        held, _, above, _ = buffers(c)
+        for line in range(LINE - 1, here, -1):
+            if here > 0:
+                up(c, line).wait_recv()
+                add_rows(held.at[line], held.at[line], above.at[line - 1])
+            up(c, line).start()
+
+    def send_down(c, here):
+        held, _, _, below = buffers(c)
+        for line in range(here):
+            if here < LINE - 1:
+                down(c, line).wait_recv()
+                add_rows(held.at[line], held.at[line], below.at[line])
+            down(c, line).start()
+
+    def finish(c, here):
+        held, _, above, below = buffers(c)
+        _, _, _, row, rows, _, cols, out, out_col = chunks[c]
+        terms = [held.at[here]]
+        if here > 0:
+            up(c, here).wait_recv()
+            terms.append(above.at[here - 1])
+        if here < LINE - 1:
+            down(c, here).wait_recv()
+            terms.append(below.at[here])
+        add_rows(outs[out].at[pl.ds(row, rows), pl.ds(out_col, cols)], *terms)
+
+    def pump(t):
+        for c in ([0, 1] if t == 0 else [t + 1]):
+            if c < count:
+                across(c).start()
+                load(c).start()
+        if 0 <= t - 1 < count:
+            fold(t - 1)
+        for hop in range(LINE):
+            c = t - 1 - hop
+            if 0 <= c < count:
+                if hop < LINE - 1:
+                    pl.when(z == hop)(lambda: send_up(c, hop))
+                    pl.when(z == LINE - 1 - hop)(lambda: send_down(c, LINE - 1 - hop))
+                else:
+                    for here in range(LINE):
+                        pl.when(z == here)(lambda: finish(c, here))
+
+    for t in range(count + LINE):
+        pump(t)
+    for c in range(count):
+        across(c).wait_send()
+        for here in range(LINE):
+
+            @pl.when(z == here)
+            def _():
+                for line in range(here + 1, LINE):
+                    up(c, line).wait_send()
+                for line in range(here):
+                    down(c, line).wait_send()
+
+    for step in range(1, GRID):
+        here, there = sources[step - 1], peers[step - 1]
+        remote(vec_ref, vecs_ref.at[here], v_s.at[step - 1], v_r.at[step - 1], dp=me).wait_recv()
+        remote(vec_ref, vecs_ref.at[me], v_s.at[step - 1], v_r.at[step - 1], dp=there).wait_send()
+
+
+def scatter_all(grads, vec):
+    chunks, outs, slots = [], [], [0, 0, 0]
+    shapes = [(192, 384), (192, 512), (256, 384)]
+    for at, grad in enumerate(grads):
+        depth, wide = grad.shape[0] // GRID, grad.shape[1]
+        outs.append(jax.ShapeDtypeStruct((depth, wide), jnp.float32))
+        which = 2 if depth % 192 else (0 if wide % 384 == 0 else 1)
+        tall, step = shapes[which]
+        for row in range(0, depth, tall):
+            for col in range(0, wide, step):
+                chunks.append((which, slots[which], at, row, tall, col, step, at, col))
+                slots[which] += 1
+    count = len(chunks)
+    any_spec = pl.BlockSpec(memory_space=pl.ANY)
+    in_vmem = pl.BlockSpec(memory_space=pltpu.VMEM)
+    dma = pltpu.SemaphoreType.DMA
+    scratch = []
+    for which in range(3):
+        for lines in (4, 4, 3, 3):
+            scratch.append(pltpu.VMEM((slots[which], lines) + shapes[which], jnp.bfloat16))
+    views = [g.reshape(LINE, 2, g.shape[0] // GRID, g.shape[1]) for g in grads]
+    return pl.pallas_call(
+        functools.partial(scatter_kernel, chunks, len(grads), len(outs)),
+        out_shape=outs + [jax.ShapeDtypeStruct((GRID,) + vec.shape, jnp.float32)],
+        in_specs=[any_spec] * len(grads) + [in_vmem],
+        out_specs=[in_vmem] * (len(outs) + 1),
+        scratch_shapes=scratch
+        + [dma((count,))] * 3
+        + [dma((count, 3))] * 4
+        + [dma((GRID - 1,))] * 2,
+        compiler_params=pltpu.CompilerParams(
+            collective_id=1, has_side_effects=True, vmem_limit_bytes=VMEM_LIMIT
+        ),
+    )(*views, vec)
+
+
+TP_PARTS = 8
+
+
+def sum_kernel(p_ref, out_ref, crossed, held, other, c_s, c_r, x_s, x_r, o_s, o_r):
+    me = lax.axis_index("tp")
+    core = lax.rem(me, 2)
+    beside, across = me + 1 - 2 * core, lax.rem(me + 2, 4)
+    greet("tp", [beside, across])
+    half = p_ref.shape[0] // 2
+    rows = half // TP_PARTS
+
+    def spot(k, which):
+        return pl.ds(pl.multiple_of(which * half + k * rows, 16), rows)
+
+    def part(k):
+        return pl.ds(k * rows, rows)
+
+    def first(k):
+        return remote(p_ref.at[spot(k, 1 - core)], crossed.at[part(k)], c_s.at[k], c_r.at[k], tp=beside)
+
+    def second(k):
+        return remote(held.at[part(k)], other.at[part(k)], x_s.at[k], x_r.at[k], tp=across)
+
+    def third(k, which):
+        return remote(out_ref.at[spot(k, which)], out_ref.at[spot(k, which)], o_s.at[k], o_r.at[k], tp=beside)
+
+    for k in range(TP_PARTS):
+        first(k).start()
+    for k in range(TP_PARTS):
+        first(k).wait_recv()
+        add_rows(held.at[part(k)], p_ref.at[spot(k, core)], crossed.at[part(k)])
+        second(k).start()
+    for k in range(TP_PARTS):
+        second(k).wait_recv()
+        add_rows(out_ref.at[spot(k, core)], held.at[part(k)], other.at[part(k)])
+        third(k, core).start()
+    for k in range(TP_PARTS):
+        third(k, 1 - core).wait_recv()
+        first(k).wait_send()
+        second(k).wait_send()
+        third(k, core).wait_send()
+
+
+def sum_tp(partial):
+    rows, wide = partial.shape
+    dma = pltpu.SemaphoreType.DMA
+    in_vmem = pl.BlockSpec(memory_space=pltpu.VMEM)
+    return pl.pallas_call(
+        sum_kernel,
+        out_shape=jax.ShapeDtypeStruct((rows, wide), jnp.bfloat16),
+        in_specs=[in_vmem],
+        out_specs=in_vmem,
+        scratch_shapes=[pltpu.VMEM((rows // 2, wide), jnp.bfloat16)] * 3 + [dma((TP_PARTS,))] * 6,
+        compiler_params=pltpu.CompilerParams(
+            collective_id=2, has_side_effects=True, vmem_limit_bytes=VMEM_LIMIT
+        ),
+    )(partial)
+
+
+def dot_nt(left, right):
+    return lax.dot_general(
+        left, right, (((1,), (1,)), ((), ())), preferred_element_type=jnp.float32
+    )
+
+
+def dot_tn(left, right):
+    return lax.dot_general(
+        left, right, (((0,), (0,)), ((), ())), preferred_element_type=jnp.float32
+    )
+
+
+def gather_plain(shards, groups, cond, small, w_ada):
+    full = [lax.all_gather(shard, "dp", axis=0, tiled=True) for shard in shards]
+    packed = [jnp.concatenate([full[i] for i in group], axis=1) for group in groups]
+    act = jax.nn.silu(lax.all_to_all(cond[:, 0], "dp", 0, 0, tiled=True)).astype(jnp.bfloat16)
+    parts = jnp.dot(act, w_ada, preferred_element_type=jnp.float32)
+    mod = lax.psum_scatter(parts, "dp", scatter_dimension=0, tiled=True)
+    smalls = lax.all_gather(small, "dp", axis=0)
+    return (*packed, mod, smalls, act.astype(jnp.float32))
+
+
+def scatter_plain(grads, vec):
+    sums = [
+        lax.psum_scatter(grad, "dp", scatter_dimension=0, tiled=True).astype(jnp.float32)
+        for grad in grads
+    ]
+    return (*sums, lax.all_gather(vec, "dp", axis=0))
 
 
 def on_device(
@@ -173,34 +591,28 @@
 ):
     row_count = tokens.shape[0]
     text_count = text.shape[0]
-    fetched = fetch(
-        w_query,
-        w_key,
-        w_value,
-        w_out,
-        w_text_key,
-        w_text_value,
-        w_gate,
-        w_up,
-        w_down,
-        ada_bias,
-        norm_one,
-        norm_two,
-    )
-    (
-        full_query,
-        full_key,
-        full_value,
-        full_out,
-        full_text_key,
-        full_text_value,
-        full_gate,
-        full_up,
-        full_down,
-        bias_full,
-        gain_one,
-        gain_two,
-    ) = fetched
+    clips = lax.axis_size("dp")
+    small = jnp.concatenate([ada_bias, norm_one, norm_two]).astype(jnp.float32)[None, :]
+    shards = (w_query, w_key, w_value, w_out.T, w_text_key, w_text_value, w_gate, w_up, w_down.T)
+    cond_rows = cond.astype(jnp.float32).reshape(clips, 1, -1)
+    if clips == GRID:
+        full_attn, full_text, full_ffn, mod_sum, smalls, act_rows = gather_all(
+            shards, ((0, 1, 2, 3), (4, 5), (6, 7, 8)), cond_rows, small, w_ada
+        )
+    else:
+        full_attn, full_text, full_ffn, mod_sum, smalls, act_rows = gather_plain(
+            shards, ((0, 1, 2, 3), (4, 5), (6, 7, 8)), cond_rows, small, w_ada
+        )
+    cols, units = w_query.shape[1], w_gate.shape[1]
+    full_query, full_key = full_attn[:, :cols], full_attn[:, cols : 2 * cols]
+    full_value, out_turned = full_attn[:, 2 * cols : 3 * cols], full_attn[:, 3 * cols :]
+    full_text_key, full_text_value = full_text[:, :cols], full_text[:, cols:]
+    full_gate, full_up = full_ffn[:, :units], full_ffn[:, units : 2 * units]
+    down_turned = full_ffn[:, 2 * units :]
+    bias_rows, gain_rows = ada_bias.shape[0], norm_one.shape[0]
+    bias_full = smalls[:, 0, :bias_rows].reshape(-1)
+    gain_one = smalls[:, 0, bias_rows : bias_rows + gain_rows].reshape(-1)
+    gain_two = smalls[:, 0, bias_rows + gain_rows :].reshape(-1)
     local_cols = full_query.shape[1]
     heads_here = local_cols // HEAD
     segment = (
@@ -208,10 +620,7 @@
         == jnp.arange(heads_here, dtype=jnp.int32)[None, :]
     ).astype(jnp.float32)
     token_values = tokens.astype(jnp.float32)
-    activated = jax.nn.silu(cond.astype(jnp.float32)).astype(jnp.bfloat16)
-    ada_full = lax.all_gather(w_ada, "dp", axis=0, tiled=True)
-    modulation = jnp.dot(activated, ada_full, preferred_element_type=jnp.float32)
-    modulation = modulation[0] + bias_full.astype(jnp.float32)
+    modulation = mod_sum[0] + bias_full
     scale_attn, gate_attn, scale_ffn, gate_ffn = jnp.split(modulation, 4)
     row_index = jnp.arange(row_count, dtype=jnp.int32)
     length = frames[0] * FRAME_TOK
@@ -219,7 +628,7 @@
     live_rows = row_valid.astype(jnp.float32)[:, None]
     key_valid = row_valid[None, None, :]
     inv_one, hat_one = rms_parts(token_values)
-    mult_one = gain_one.astype(jnp.float32) * (1.0 + scale_attn)
+    mult_one = gain_one * (1.0 + scale_attn)
     h_one = (hat_one * mult_one).astype(jnp.bfloat16)
     query_pre = jnp.dot(h_one, full_query, preferred_element_type=jnp.float32)
     key_pre = jnp.dot(h_one, full_key, preferred_element_type=jnp.float32)
@@ -273,52 +682,43 @@
     gate_tanh = jnp.tanh(cross_gate.astype(jnp.float32))
     gate_wide = jnp.repeat(gate_tanh, HEAD)
     mixed = (self_outs + gate_wide[None, :] * text_outs).astype(jnp.bfloat16)
-    attn_sum = lax.psum(
-        jnp.dot(mixed, full_out, preferred_element_type=jnp.float32).astype(jnp.bfloat16), "tp"
-    ).astype(jnp.float32)
+    attn_sum = sum_tp(dot_nt(mixed, out_turned).astype(jnp.bfloat16)).astype(jnp.float32)
     tanh_attn = jnp.tanh(gate_attn)
     hidden_state = token_values + live_rows * tanh_attn * attn_sum
     inv_two, hat_two = rms_parts(hidden_state)
-    mult_two = gain_two.astype(jnp.float32) * (1.0 + scale_ffn)
+    mult_two = gain_two * (1.0 + scale_ffn)
     h_two = (hat_two * mult_two).astype(jnp.bfloat16)
     gate_pre = jnp.dot(h_two, full_gate, preferred_element_type=jnp.float32)
     up_pre = jnp.dot(h_two, full_up, preferred_element_type=jnp.float32)
     logistic = jax.nn.sigmoid(gate_pre)
     swish = gate_pre * logistic
     hidden_units = (swish * up_pre).astype(jnp.bfloat16)
-    ffn_sum = lax.psum(
-        jnp.dot(hidden_units, full_down, preferred_element_type=jnp.float32).astype(jnp.bfloat16),
-        "tp",
-    ).astype(jnp.float32)
+    ffn_sum = sum_tp(dot_nt(hidden_units, down_turned).astype(jnp.bfloat16)).astype(jnp.float32)
     tanh_ffn = jnp.tanh(gate_ffn)
     result = hidden_state + live_rows * tanh_ffn * ffn_sum
     grad_result = cotangent.astype(jnp.float32)
     grad_ffn = (live_rows * tanh_ffn * grad_result).astype(jnp.bfloat16)
     grad_gate_ffn = jnp.sum(live_rows * ffn_sum * grad_result, axis=0) * (1.0 - tanh_ffn * tanh_ffn)
-    grad_hidden = jnp.dot(grad_ffn, full_down.T, preferred_element_type=jnp.float32)
+    grad_hidden = jnp.dot(grad_ffn, down_turned, preferred_element_type=jnp.float32)
     grad_gate_pre = (grad_hidden * up_pre * logistic * (1.0 + gate_pre * (1.0 - logistic))).astype(
         jnp.bfloat16
     )
     grad_up_pre = (grad_hidden * swish).astype(jnp.bfloat16)
-    g_down = jnp.dot(hidden_units.T, grad_ffn, preferred_element_type=jnp.float32)
-    g_gate = jnp.dot(h_two.T, grad_gate_pre, preferred_element_type=jnp.float32)
-    g_up = jnp.dot(h_two.T, grad_up_pre, preferred_element_type=jnp.float32)
-    grad_n_two = lax.psum(
-        (
-            jnp.dot(grad_gate_pre, full_gate.T, preferred_element_type=jnp.float32)
-            + jnp.dot(grad_up_pre, full_up.T, preferred_element_type=jnp.float32)
-        ).astype(jnp.bfloat16),
-        "tp",
+    g_down = dot_tn(grad_ffn, hidden_units).astype(jnp.bfloat16)
+    g_gate = dot_tn(h_two, grad_gate_pre).astype(jnp.bfloat16)
+    g_up = dot_tn(h_two, grad_up_pre).astype(jnp.bfloat16)
+    grad_n_two = sum_tp(
+        (dot_nt(grad_gate_pre, full_gate) + dot_nt(grad_up_pre, full_up)).astype(jnp.bfloat16)
     ).astype(jnp.float32)
     g_norm_two = jnp.sum(grad_n_two * hat_two * (1.0 + scale_ffn), axis=0)
-    grad_scale_ffn = jnp.sum(grad_n_two * hat_two * gain_two.astype(jnp.float32), axis=0)
+    grad_scale_ffn = jnp.sum(grad_n_two * hat_two * gain_two, axis=0)
     grad_state = grad_result + rms_back(inv_two, hat_two, grad_n_two * mult_two)
     grad_attn = (live_rows * tanh_attn * grad_state).astype(jnp.bfloat16)
     grad_gate_attn = jnp.sum(live_rows * attn_sum * grad_state, axis=0) * (
         1.0 - tanh_attn * tanh_attn
     )
-    grad_mixed = jnp.dot(grad_attn, full_out.T, preferred_element_type=jnp.float32)
-    g_out = jnp.dot(mixed.T, grad_attn, preferred_element_type=jnp.float32)
+    grad_mixed = jnp.dot(grad_attn, out_turned, preferred_element_type=jnp.float32)
+    g_out = dot_tn(grad_attn, mixed).astype(jnp.bfloat16)
     column_cross = jnp.sum(grad_mixed * text_outs, axis=0)
     g_cross_gate = exact_dot(column_cross[None, :], segment)[0] * (1.0 - gate_tanh * gate_tanh)
     grad_self = to_heads(grad_mixed.astype(jnp.bfloat16))
@@ -373,62 +773,75 @@
         jnp.bfloat16
     )
     grad_text_vals = from_heads(grad_text_values).astype(jnp.bfloat16)
-    g_query = jnp.dot(h_one.T, grad_query_pre, preferred_element_type=jnp.float32)
-    g_key = jnp.dot(h_one.T, grad_key_pre, preferred_element_type=jnp.float32)
-    g_value = jnp.dot(h_one.T, grad_value_pre, preferred_element_type=jnp.float32)
-    g_text_key = jnp.dot(text.T, grad_text_pre, preferred_element_type=jnp.float32)
-    g_text_value = jnp.dot(text.T, grad_text_vals, preferred_element_type=jnp.float32)
-    grad_n_one = lax.psum(
+    g_query = dot_tn(h_one, grad_query_pre).astype(jnp.bfloat16)
+    g_key = dot_tn(h_one, grad_key_pre).astype(jnp.bfloat16)
+    g_value = dot_tn(h_one, grad_value_pre).astype(jnp.bfloat16)
+    g_text_key = dot_tn(text, grad_text_pre).astype(jnp.bfloat16)
+    g_text_value = dot_tn(text, grad_text_vals).astype(jnp.bfloat16)
+    grad_n_one = sum_tp(
         (
-            jnp.dot(grad_query_pre, full_query.T, preferred_element_type=jnp.float32)
-            + jnp.dot(grad_key_pre, full_key.T, preferred_element_type=jnp.float32)
-            + jnp.dot(grad_value_pre, full_value.T, preferred_element_type=jnp.float32)
-        ).astype(jnp.bfloat16),
-        "tp",
+            dot_nt(grad_query_pre, full_query)
+            + dot_nt(grad_key_pre, full_key)
+            + dot_nt(grad_value_pre, full_value)
+        ).astype(jnp.bfloat16)
     ).astype(jnp.float32)
     g_norm_one = jnp.sum(grad_n_one * hat_one * (1.0 + scale_attn), axis=0)
-    grad_scale_attn = jnp.sum(grad_n_one * hat_one * gain_one.astype(jnp.float32), axis=0)
+    grad_scale_attn = jnp.sum(grad_n_one * hat_one * gain_one, axis=0)
     grad_input = grad_state + rms_back(inv_one, hat_one, grad_n_one * mult_one)
-    grad_mod = jnp.concatenate([grad_scale_attn, grad_gate_attn, grad_scale_ffn, grad_gate_ffn])[
-        None, :
-    ]
-    ada_local = activated.astype(jnp.float32).reshape(-1, 1) * grad_mod
-    g_ada = lax.psum_scatter(ada_local, "dp", scatter_dimension=0, tiled=True)
-    summed = (
-        lax.psum_scatter(g_query, "dp", scatter_dimension=0, tiled=True),
-        lax.psum_scatter(g_key, "dp", scatter_dimension=0, tiled=True),
-        lax.psum_scatter(g_value, "dp", scatter_dimension=0, tiled=True),
-        lax.psum_scatter(g_out, "dp", scatter_dimension=1, tiled=True),
-        lax.psum_scatter(g_text_key, "dp", scatter_dimension=0, tiled=True),
-        lax.psum_scatter(g_text_value, "dp", scatter_dimension=0, tiled=True),
-        lax.psum_scatter(g_gate, "dp", scatter_dimension=0, tiled=True),
-        lax.psum_scatter(g_up, "dp", scatter_dimension=0, tiled=True),
-        lax.psum_scatter(g_down, "dp", scatter_dimension=1, tiled=True),
-        lax.psum_scatter(grad_mod[0], "dp", scatter_dimension=0, tiled=True),
-        lax.psum_scatter(g_norm_one, "dp", scatter_dimension=0, tiled=True),
-        lax.psum_scatter(g_norm_two, "dp", scatter_dimension=0, tiled=True),
-    )
-    small_sums = lax.psum((g_query_gain, g_key_gain, g_text_gain, g_cross_gate), "dp")
+    gate_pad = jnp.zeros((-heads_here % 128,), jnp.float32)
+    vec = jnp.concatenate(
+        [
+            grad_scale_attn,
+            grad_gate_attn,
+            grad_scale_ffn,
+            grad_gate_ffn,
+            g_norm_one,
+            g_norm_two,
+            g_query_gain,
+            g_key_gain,
+            g_text_gain,
+            g_cross_gate,
+            gate_pad,
+        ]
+    )[None, :]
+    grads = (g_down, g_gate, g_up, g_out, g_text_key, g_text_value, g_query, g_key, g_value)
+    summed = (scatter_all if clips == GRID else scatter_plain)(grads, vec)
+    s_down, s_gate, s_up, s_out, s_text_key, s_text_value, s_query, s_key, s_value, vecs = summed
+    vecs = vecs[:, 0, :]
+    mod_wide, wide = 4 * tokens.shape[1], tokens.shape[1]
+    g_ada = lax.dot_general(
+        act_rows,
+        vecs[:, :mod_wide],
+        (((0,), (0,)), ((), ())),
+        precision=lax.Precision.HIGHEST,
+        preferred_element_type=jnp.float32,
+    )
+    sums = jnp.sum(vecs, axis=0)
+    me = lax.axis_index("dp")
+    g_bias = lax.dynamic_slice(sums, (me * bias_rows,), (bias_rows,))
+    g_norm_one = lax.dynamic_slice(sums, (mod_wide + me * gain_rows,), (gain_rows,))
+    g_norm_two = lax.dynamic_slice(sums, (mod_wide + wide + me * gain_rows,), (gain_rows,))
+    rest = sums[mod_wide + 2 * wide :]
     return (
         result.astype(jnp.bfloat16),
         grad_input.astype(jnp.bfloat16),
-        summed[0],
-        summed[1],
-        summed[2],
-        summed[3],
-        summed[4],
-        summed[5],
-        summed[6],
-        summed[7],
-        summed[8],
+        s_query,
+        s_key,
+        s_value,
+        s_out.T,
+        s_text_key,
+        s_text_value,
+        s_gate,
+        s_up,
+        s_down.T,
         g_ada,
-        summed[9],
-        summed[10],
-        summed[11],
-        small_sums[0],
-        small_sums[1],
-        small_sums[2],
-        small_sums[3],
+        g_bias,
+        g_norm_one,
+        g_norm_two,
+        rest[:local_cols],
+        rest[local_cols : 2 * local_cols],
+        rest[2 * local_cols : 3 * local_cols],
+        rest[3 * local_cols : 3 * local_cols + heads_here],
     )
 
 

time: 2390 us -> 996 us (0.42)
  waiting for transfers between devices: 1890 us -> 0 us
  Pallas kernels: 0 us -> 656 us
  blocking collectives: 95.6 us -> 0 us
  matrix products: 267 us -> 219 us
    reduce_scatter x10 -> x0, waiting for transfers between devices: 1220 us -> none  [the longest x1 407 us: on_device(): g_ada = lax.psum_scatter(ada_local, 'dp', scatter_dimension=0, tiled=True)]
    pallas_call x0 -> x6, Pallas kernels: none -> 656 us  [the longest x1 249 us: scatter_all(): pl.pallas_call(functools.partial(scatter_kernel, chunks, len(grads), len(...]
    all_gather x10 -> x0, waiting for transfers between devices: 473 us -> none  [the longest x1 172 us: on_device(): ada_full = lax.all_gather(w_ada, 'dp', axis=0, tiled=True)]
    psum x3 -> x0, waiting for transfers between devices: 183 us -> none  [the longest x1 118 us: on_device(): lax.psum(jnp.dot(hidden_units, full_down, preferred_element_type=jnp.floa...]
    unnamed x2 -> x0, blocking collectives: 63.2 us -> none
    all_gather x1 -> x0, blocking collectives: 32.5 us -> none  [fetch(): lax.all_gather(ada_bias, 'dp', axis=0, tiled=True)]
  transfers between devices with their start and end apart: 23 -> 0, of which waited for: 20 -> 0; matrix products, arithmetic and copies ran while one was open for 9% -> 0% of each run, Pallas kernels for 0% -> 0%
where the time goes in v1:
time: 996 us; the launch traced here: 992 us
  Pallas kernels  656 us (66%)
  matrix products  219 us (22%)
  other arithmetic  78.7 us (8%)
  local copies, waits for them, and re-layouts  34.5 us (3%)
    pallas_call x1, Pallas kernels, scatter_all(): pl.pallas_call(functools.partial(scatter_kernel, chunks, len(grads), len(...  249 us
    pallas_call x1, Pallas kernels, gather_all(): pl.pallas_call(functools.partial(gather_kernel, chunks, len(shards), len(...  234 us
    pallas_call x4, Pallas kernels, sum_tp(): pl.pallas_call(sum_kernel, out_shape=jax.ShapeDtypeStruct((rows, wide), j...  173 us
    dot_general x17, matrix products, exact_dot(): jnp.dot(left, right, precision=lax.Precision.HIGHEST, preferred_element_t...  50.3 us
    dot_general x9, matrix products, dot_tn(): lax.dot_general(left, right, (((0,), (0,)), ((), ())), preferred_element_...  38.9 us
    dot_general x7, matrix products, dot_nt(): lax.dot_general(left, right, (((1,), (1,)), ((), ())), preferred_element_...  29.9 us
    dot_general x4, matrix products, attend_back(): jnp.einsum('hqd,hkd->hqk', grad_outputs, values, preferred_element_type=j...  29.4 us

profile of v1, /device:TPU:0, one launch (start us, length us, event | category | flops | bytes accessed | tf_op | source)
XLA Modules:
  0.0 991.9 jit_solution(14489508595659074675)
XLA Ops:
  11.6 234.1 %shard_map.357 = (bf16[1536,1536]{1,0:T(8,128)(2,1)}, bf16[4096,768]{1,0:T(8,128)(2,1)}, bf16[1536,3072]{1,0:T(8,128)(2,1)}, f32[1,6144]{1,0:T(1,128)}, f32[8,1,1152]{2,1,0:T(1,128)}, /*index=5*/f32[8,128]{1,0:T(8,128)}) custom-call(bf16[192,384]{1,0:T(8,128)(2,1)} %refs_0_.1, bf16[192,384]{1,0:T(8,128)(2,1)} %refs_1_.1, bf16[192,384]{1,0:T(8,128)(2,1)} %refs_2_.1, ...), custom_call_target="tpu_custom_call" | custom-call | tf_op jit(solution)/shard_map/pallas_call | solution.py:303
  265.1 8.7 add_convert_fusion.3
  279.1 9.0 add_convert_fusion.4
  297.7 6.5 fusion
  322.5 43.4 %shard_map.358 = bf16[1024,1536]{1,0:T(8,128)(2,1)} custom-call(bf16[1024,1536]{1,0:T(8,128)(2,1)} %convolution_convert_fusion.2.p_ref), custom_call_target="tpu_custom_call" | custom-call | tf_op jit(solution)/shard_map/pallas_call | solution.py:526
  372.6 5.5 fusion.49
  381.5 7.1 multiply_convert_fusion.3
  388.7 6.6 convolution_convert_fusion.3
  395.3 5.4 convolution_convert_fusion.4
  410.7 43.2 %shard_map.359 = bf16[1024,1536]{1,0:T(8,128)(2,1)} custom-call(bf16[1024,1536]{1,0:T(8,128)(2,1)} %convolution_convert_fusion.6.p_ref), custom_call_target="tpu_custom_call" | custom-call | tf_op jit(solution)/shard_map/pallas_call | solution.py:526
  453.9 6.1 fusion.51
  460.0 6.9 add_convert_fusion.1.p_ref
  466.9 43.2 %shard_map.360 = bf16[1024,1536]{1,0:T(8,128)(2,1)} custom-call(bf16[1024,1536]{1,0:T(8,128)(2,1)} %add_convert_fusion.1.p_ref), custom_call_target="tpu_custom_call" | custom-call | tf_op jit(solution)/shard_map/pallas_call | solution.py:526
  510.2 12.6 %multiply_reduce_fusion.2 = (f32[1536]{0:T(1024)S(1)}, f32[1536]{0:T(1024)S(1)}, f32[1024]{0:T(1024)S(1)}, f32[1536]{0:T(1024)S(1)}, bf16[1024,1536]{1,0:T(8,128)(2,1)}) fusion(bf16[1024,1536]{1,0:T(8,128)(2,1)} %shard_map.360, f32[1536]{0:T(1024)S(1)} %copy-done.81, f32[1024]{0:T(1024)S(1)} %add_rsqrt_fusion, bf16[1024,1536]{1,0:T(8,128)(2,1)} %shard_map.358, ...), kind=kLoop, calls=%fused_computation.54 | loop fusion | flops 37743104 | bytes 18935808 | tf_op jit(solution)/shard_map/reduce_sum | solution.py:713
  531.9 6.4 convolution_convert_fusion.10
  579.5 7.6 fusion.163
  587.1 18.1 %multiply_reduce_fusion.1 = (f32[6,512]{1,0:T(8,128)S(1)}, f32[6,512]{1,0:T(8,128)S(1)}, f32[6,512,1024]{2,1,0:T(8,128)}) fusion(f32[6,512]{1,0:T(8,128)S(1)} %copy-done.66, f32[6,512,1024]{2,1,0:T(8,128)} %copy-done.6, pred[1024]{0:T(1024)(128)(4,1)S(1)} %get-tuple-element.117, f32[6,512,1024]{2,1,0:T(8,128)} %fusion.163, f32[6,512]{1,0:T(8,128)S(1)} %log_add_fusion.2, ...), kind=kOutput, calls=%fused_computation.4 | convolution fusion | flops 434104320 | bytes 51569664 | tf_op jit(solution)/shard_map/hqd,hkd->hqk/dot_general | solution.py:106
  605.2 17.5 %multiply_convert_fusion.1 = (bf16[6,512,1024]{2,1,0:T(8,128)(2,1)S(1)}, bf16[6,512,1024]{2,1,0:T(8,128)(2,1)S(1)}) fusion(f32[6,512,1024]{2,1,0:T(8,128)} %get-tuple-element.112, f32[6,512]{1,0:T(8,128)S(1)} %get-tuple-element.60, f32[6,512]{1,0:T(8,128)S(1)} %copy-done.66, f32[6,512,1024]{2,1,0:T(8,128)} %copy-done.6, ...), kind=kLoop, calls=%fused_computation.3 | loop fusion | flops 37748736 | bytes 62964736 | tf_op jit(solution)/shard_map/convert_element_type | solution.py:112
  630.0 5.8 bitcast_multiply_fusion.2
  635.9 8.0 multiply_reduce_fusion.12
  643.9 8.3 multiply_reduce_fusion.11
  672.5 43.2 %shard_map.361 = bf16[1024,1536]{1,0:T(8,128)(2,1)} custom-call(bf16[1024,1536]{1,0:T(8,128)(2,1)} %add_convert_fusion.p_ref), custom_call_target="tpu_custom_call" | custom-call | tf_op jit(solution)/shard_map/pallas_call | solution.py:526
  721.4 249.1 %shard_map.362 = (f32[192,1024]{1,0:T(8,128)}, f32[192,1024]{1,0:T(8,128)}, f32[192,1024]{1,0:T(8,128)}, f32[192,384]{1,0:T(8,128)}, f32[512,384]{1,0:T(8,128)},...) custom-call(bf16[4,2,192,1024]{3,2,1,0:T(8,128)(2,1)} %bitcast.190, ...), custom_call_target="tpu_custom_call" | custom-call | tf_op jit(solution)/shard_map/pallas_call | solution.py:464
  970.5 6.8 fusion.13
  (357 shorter events, 179.7 us)
Async XLA Ops:
  0.7 248.2 %copy-start = (bf16[256,4096]{1,0:T(8,128)(2,1)S(1)}, bf16[256,4096]{1,0:T(8,128)(2,1)}, u32[]{:S(2)}) copy-start(bf16[256,4096]{1,0:T(8,128)(2,1)} %param.23) | copy-start | bytes 6291460
  1.5 277.6 %copy-start.95 = (pred[384]{0:T(512)(128)(4,1)}, pred[384]{0:T(512)(128)(4,1)S(1)}, u32[]{:S(2)}) copy-start(pred[384]{0:T(512)(128)(4,1)S(1)} %broadcast_compare_fusion) | copy-start | bytes 1156
  3.5 273.4 %copy-start.56 = (s32[384]{0:T(512)}, s32[384]{0:T(512)S(1)}, u32[]{:S(2)}) copy-start(s32[384]{0:T(512)S(1)} %add_select_fusion.4) | copy-start | bytes 4612
  4.2 274.9 %copy-start.79 = (f32[384]{0:T(512)}, f32[384]{0:T(512)S(1)}, u32[]{:S(2)}) copy-start(f32[384]{0:T(512)S(1)} %convert_element_type.282) | copy-start | bytes 4612
  4.2 274.9 %copy-start.89 = (s32[384]{0:T(512)}, s32[384]{0:T(512)S(1)}, u32[]{:S(2)}) copy-start(s32[384]{0:T(512)S(1)} %add_add_fusion) | copy-start | bytes 4612
  4.9 259.0 %copy-start.84 = (f32[384]{0:T(512)}, f32[384]{0:T(512)S(1)}, u32[]{:S(2)}) copy-start(f32[384]{0:T(512)S(1)} %convert_element_type.287) | copy-start | bytes 4612
  5.6 248.7 %copy-start.86 = (f32[384]{0:T(512)}, f32[384]{0:T(512)S(1)}, u32[]{:S(2)}) copy-start(f32[384]{0:T(512)S(1)} %convert_element_type.294) | copy-start | bytes 4612
  11.5 262.3 %copy-start.77 = (f32[1024]{0:T(1024)}, f32[1024]{0:T(1024)S(1)}, u32[]{:S(2)}) copy-start(f32[1024]{0:T(1024)S(1)} %add_rsqrt_fusion.1) | copy-start | bytes 12292
  11.6 267.5 %copy-start.82 = (f32[384]{0:T(512)}, f32[384]{0:T(512)S(1)}, u32[]{:S(2)}) copy-start(f32[384]{0:T(512)S(1)} %get-tuple-element.121) | copy-start | bytes 4612
  11.6 267.5 %copy-start.91 = (f32[384]{0:T(512)}, f32[384]{0:T(512)S(1)}, u32[]{:S(2)}) copy-start(f32[384]{0:T(512)S(1)} %get-tuple-element.122) | copy-start | bytes 4612
  11.6 267.5 %copy-start.73 = (f32[1024]{0:T(1024)}, f32[1024]{0:T(1024)S(1)}, u32[]{:S(2)}) copy-start(f32[1024]{0:T(1024)S(1)} %get-tuple-element.119) | copy-start | bytes 12292
  11.6 267.5 %copy-start.75 = (f32[1024]{0:T(1024)}, f32[1024]{0:T(1024)S(1)}, u32[]{:S(2)}) copy-start(f32[1024]{0:T(1024)S(1)} %get-tuple-element.120) | copy-start | bytes 12292
  248.9 24.9 %copy-start.69 = (f32[1536]{0:T(1024)}, f32[1536]{0:T(1024)S(1)}, u32[]{:S(2)}) copy-start(f32[1536]{0:T(1024)S(1)} %get-tuple-element.89) | copy-start | bytes 18436
  252.6 40.9 %copy-start.54 = (bf16[384,256]{1,0:T(8,128)(2,1)}, bf16[384,256]{1,0:T(8,128)(2,1)S(1)}, u32[]{:S(2)}) copy-start(bf16[384,256]{1,0:T(8,128)(2,1)S(1)} %fusion.124) | copy-start | bytes 589828
  255.5 35.7 %copy-start.34 = (bf16[256,384]{0,1:T(8,128)(2,1)}, bf16[256,384]{0,1:T(8,128)(2,1)S(1)}, u32[]{:S(2)}) copy-start(bf16[256,384]{0,1:T(8,128)(2,1)S(1)} %get-tuple-element.68) | copy-start | bytes 589828
  273.8 21.8 %copy-start.26 = (bf16[1024,384]{0,1:T(8,128)(2,1)}, bf16[1024,384]{0,1:T(8,128)(2,1)S(1)}, u32[]{:S(2)}) copy-start(bf16[1024,384]{0,1:T(8,128)(2,1)S(1)} %add_convert_fusion.3) | copy-start | bytes 2359300
  297.7 14.3 %copy-start.6 = (f32[6,512,1024]{2,1,0:T(8,128)}, f32[6,512,1024]{2,1,0:T(8,128)S(1)}, u32[]{:S(2)}) copy-start(f32[6,512,1024]{2,1,0:T(8,128)S(1)} %get-tuple-element.100) | copy-start | bytes 37748740
  466.9 43.2 %copy-start.68 = (f32[1536]{0:T(1024)S(1)}, f32[1536]{0:T(1024)}, u32[]{:S(2)}) copy-start(f32[1536]{0:T(1024)} %copy-done.67) | copy-start | bytes 18436
  466.9 43.2 %copy-start.81 = (f32[1536]{0:T(1024)S(1)}, f32[1536]{0:T(1024)}, u32[]{:S(2)}) copy-start(f32[1536]{0:T(1024)} %get-tuple-element.87) | copy-start | bytes 18436
  510.1 12.6 %copy-start.3 = (bf16[1024,1536]{1,0:T(8,128)(2,1)S(1)}, bf16[1024,1536]{1,0:T(8,128)(2,1)}, u32[]{:S(2)}) copy-start(bf16[1024,1536]{1,0:T(8,128)(2,1)} %param.22) | copy-start | bytes 9437188
  526.8 18.8 %slice-start.3 = ((s8[12582912]{0:T(1024)(128)(4,1)}), s8[4194304]{0:T(1024)(128)(4,1)S(1)}, s32[]{:S(2)}) async-start(s8[12582912]{0:T(1024)(128)(4,1)} %bitcast.166), calls=%async_computation.3 | async-start | bytes 8388608
  531.9 13.7 %slice-start.4 = ((s8[12582912]{0:T(1024)(128)(4,1)}), s8[4194304]{0:T(1024)(128)(4,1)S(1)}, s32[]{:S(2)}) async-start(s8[12582912]{0:T(1024)(128)(4,1)} %bitcast.166), calls=%async_computation.4 | async-start | bytes 8388608
  605.2 17.5 %copy-start.27 = (bf16[1024,384]{0,1:T(8,128)(2,1)S(1)}, bf16[1024,384]{0,1:T(8,128)(2,1)}, u32[]{:S(2)}) copy-start(bf16[1024,384]{0,1:T(8,128)(2,1)} %copy-done.26) | copy-start | bytes 2359300
  672.5 43.2 %copy-start.72 = (f32[1536]{0:T(1024)S(1)}, f32[1536]{0:T(1024)}, u32[]{:S(2)}) copy-start(f32[1536]{0:T(1024)} %copy-done.71) | copy-start | bytes 18436
  (91 other events, 443.4 us)

commit v2 on v0

v2 whole, which is shorter than its diff:
```python
import functools

import jax
import jax.numpy as jnp
import numpy as np
from jax import lax
from jax.experimental import pallas as pl
from jax.experimental.pallas import tpu as pltpu
from jax.sharding import PartitionSpec as P

HEAD = 64
FRAME_TOK = 64
EPS = 1e-06
ROPE_BASE = 10000.0
SCALE = HEAD**-0.5
MESH = pl.DeviceIdType.MESH
VMEM_LIMIT = 60 * 2**20
GRID = 8
LINE = 4
PAIR = 2 * HEAD
TP_PARTS = 8
AHEAD = 2
DMA = pltpu.SemaphoreType.DMA
F32 = jnp.float32
BF16 = jnp.bfloat16


def dot_nn(left, right):
    return jnp.dot(left, right, preferred_element_type=F32)


def dot_nt(left, right):
    return lax.dot_general(left, right, (((1,), (1,)), ((), ())), preferred_element_type=F32)


def dot_tn(left, right):
    return lax.dot_general(left, right, (((0,), (0,)), ((), ())), preferred_element_type=F32)


def remote(src, dst, send, recv, **where):
    return pltpu.make_async_remote_copy(
        src_ref=src, dst_ref=dst, send_sem=send, recv_sem=recv, device_id=where, device_id_type=MESH
    )


def greet(dp_peers, tp_peers):
    barrier = pltpu.get_barrier_semaphore()
    for peer in dp_peers:
        pl.semaphore_signal(barrier, inc=1, device_id={"dp": peer}, device_id_type=MESH)
    for peer in tp_peers:
        pl.semaphore_signal(barrier, inc=1, device_id={"tp": peer}, device_id_type=MESH)
    pl.semaphore_wait(barrier, len(dp_peers) + len(tp_peers))


def dp_peers():
    me = lax.axis_index("dp")
    return [lax.rem(me + step, GRID) for step in range(1, GRID)]


def tp_peers():
    me = lax.axis_index("tp")
    return [me + 1 - 2 * lax.rem(me, 2), lax.rem(me + 2, 4)]


def aligned(value, by):
    return value if isinstance(value, int) else pl.multiple_of(value, by)


def loop(count, step):
    def body(i, carry):
        step(i)
        return carry

    lax.fori_loop(0, count, body, 0)


def add_rows(out_ref, first, *others):
    rows = out_ref.shape[0]

    def step(i):
        here = pl.ds(pl.multiple_of(i * 32, 32), 32)
        total = first[here, :].astype(F32)
        for other in others:
            total = total + other[here, :].astype(F32)
        out_ref[here, :] = total.astype(out_ref.dtype)

    loop(rows // 32, step)


class Blocks:
    def __init__(self, depth, wide, rows, cols):
        self.depth, self.wide, self.rows, self.cols = depth, wide, rows, cols
        self.across = wide // cols
        self.count = (depth // rows) * self.across

    def at(self, c):
        if isinstance(c, int):
            return c // self.across * self.rows, c % self.across * self.cols
        row = aligned(lax.div(c, self.across) * self.rows, 16)
        col = aligned(lax.rem(c, self.across) * self.cols, 128)
        return row, col


class Gather:
    def __init__(self, blocks, shard, full, sems):
        self.b, self.shard, self.full = blocks, shard, full
        self.up_s, self.up_r, self.dn_s, self.dn_r, self.y_s, self.y_r, self.own_s = sems
        self.me = lax.axis_index("dp")
        self.z, self.y = self.me // 2, lax.rem(self.me, 2)
        self.ticks = blocks.count + LINE - 2

    @staticmethod
    def scratch(count):
        return [DMA((count, 3))] * 4 + [DMA((count, 4))] * 2 + [DMA((count,))]

    def own(self, c):
        row, col = self.b.at(c)
        return self.shard.at[pl.ds(row, self.b.rows), pl.ds(col, self.b.cols)]

    def place(self, c, origin):
        row, col = self.b.at(c)
        start = pl.multiple_of(origin * self.b.depth + row, 16)
        return self.full.at[pl.ds(start, self.b.rows), pl.ds(col, self.b.cols)]

    def up(self, c, hop):
        origin = self.me - 2 * hop
        src = self.own(c) if hop == 0 else self.place(c, origin)
        return remote(src, self.place(c, origin), self.up_s.at[c, hop], self.up_r.at[c, hop], dp=self.me + 2)

    def down(self, c, hop):
        origin = self.me + 2 * hop
        src = self.own(c) if hop == 0 else self.place(c, origin)
        return remote(src, self.place(c, origin), self.dn_s.at[c, hop], self.dn_r.at[c, hop], dp=self.me - 2)

    def across(self, c, line, mine=False):
        origin = 2 * line + self.y
        src = self.own(c) if mine else self.place(c, origin)
        other = self.me + 1 - 2 * self.y
        return remote(src, self.place(c, origin), self.y_s.at[c, line], self.y_r.at[c, line], dp=other)

    def came(self, c, origin, sems):
        return remote(self.place(c, origin), self.place(c, origin), sems, sems, dp=self.me)

    def local(self, c):
        return pltpu.make_async_copy(self.own(c), self.place(c, self.me), self.own_s.at[c])

    def begin(self, c):
        pl.when(self.z < LINE - 1)(lambda: self.up(c, 0).start())
        pl.when(self.z > 0)(lambda: self.down(c, 0).start())
        self.across(c, self.z, True).start()
        self.local(c).start()

    def start(self):
        for c in range(min(AHEAD, self.b.count)):
            self.begin(c)

    def pump(self, t):
        me, z, count = self.me, self.z, self.b.count
        pl.when(t + AHEAD < count)(lambda: self.begin(t + AHEAD))
        for hop in range(LINE - 1):
            c = t - hop
            valid = (c >= 0) & (c < count)

            @pl.when(valid & (z - 1 - hop >= 0))
            def _():
                self.came(c, me - 2 * (hop + 1), self.up_r.at[c, hop]).wait_recv()
                if hop < LINE - 2:
                    pl.when(z < LINE - 1)(lambda: self.up(c, hop + 1).start())
                self.across(c, z - 1 - hop).start()

            @pl.when(valid & (z + 1 + hop <= LINE - 1))
            def _():
                self.came(c, me + 2 * (hop + 1), self.dn_r.at[c, hop]).wait_recv()
                if hop < LINE - 2:
                    pl.when(z > 0)(lambda: self.down(c, hop + 1).start())
                self.across(c, z + 1 + hop).start()

    def drain(self):
        z = self.z

        def step(c):
            for line in range(LINE):
                self.came(c, 2 * line + 1 - self.y, self.y_r.at[c, line]).wait_recv()
                self.across(c, line).wait_send()
            self.local(c).wait()
            for hop in range(LINE - 1):
                pl.when((z < LINE - 1) & (z - hop >= 0))(lambda: self.up(c, hop).wait_send())
                pl.when((z > 0) & (z + hop <= LINE - 1))(lambda: self.down(c, hop).wait_send())

        loop(self.b.count, step)


class Scatter:
    def __init__(self, blocks, grad, out, bufs, sems):
        self.b, self.grad, self.out = blocks, grad, out
        self.held, self.crossed, self.above, self.below = bufs
        self.y_s, self.y_r, self.own_s, self.up_s, self.up_r, self.dn_s, self.dn_r = sems
        self.me = lax.axis_index("dp")
        self.z, self.y = self.me // 2, lax.rem(self.me, 2)
        self.ticks = blocks.count + LINE - 1

    @staticmethod
    def scratch(blocks):
        shape = (blocks.rows, blocks.cols)
        count = blocks.count
        bufs = [pltpu.VMEM((count, lines) + shape, BF16) for lines in (4, 4, 3, 3)]
        return bufs + [DMA((count,))] * 3 + [DMA((count, 3))] * 4

    def part(self, c, row_y):
        row, col = self.b.at(c)
        return self.grad.at[:, row_y, pl.ds(row, self.b.rows), pl.ds(col, self.b.cols)]

    def across(self, c):
        other = self.me + 1 - 2 * self.y
        return remote(self.part(c, 1 - self.y), self.crossed.at[c], self.y_s.at[c], self.y_r.at[c], dp=other)

    def load(self, c):
        return pltpu.make_async_copy(self.part(c, self.y), self.held.at[c], self.own_s.at[c])

    def up(self, c, line):
        return remote(
            self.held.at[c, line],
            self.above.at[c, line - 1],
            self.up_s.at[c, line - 1],
            self.up_r.at[c, line - 1],
            dp=self.me + 2,
        )

    def down(self, c, line):
        return remote(
            self.held.at[c, line],
            self.below.at[c, line],
            self.dn_s.at[c, line],
            self.dn_r.at[c, line],
            dp=self.me - 2,
        )

    def begin(self, c):
        self.across(c).start()
        self.load(c).start()

    def start(self):
        for c in range(min(AHEAD, self.b.count)):
            self.begin(c)

    def fold(self, c):
        self.across(c).wait_recv()
        self.load(c).wait()
        for line in range(LINE):
            add_rows(self.held.at[c, line], self.held.at[c, line], self.crossed.at[c, line])

    def send_up(self, c, here):
        for line in range(LINE - 1, here, -1):
            if here > 0:
                self.up(c, line).wait_recv()
                add_rows(self.held.at[c, line], self.held.at[c, line], self.above.at[c, line - 1])
            self.up(c, line).start()

    def send_down(self, c, here):
        for line in range(here):
            if here < LINE - 1:
                self.down(c, line).wait_recv()
                add_rows(self.held.at[c, line], self.held.at[c, line], self.below.at[c, line])
            self.down(c, line).start()

    def finish(self, c, here):
        row, col = self.b.at(c)
        terms = [self.held.at[c, here]]
        if here > 0:
            self.up(c, here).wait_recv()
            terms.append(self.above.at[c, here - 1])
        if here < LINE - 1:
            self.down(c, here).wait_recv()
            terms.append(self.below.at[c, here])
        add_rows(self.out.at[pl.ds(row, self.b.rows), pl.ds(col, self.b.cols)], *terms)

    def pump(self, t):
        count, z = self.b.count, self.z
        pl.when(t + AHEAD < count)(lambda: self.begin(t + AHEAD))
        pl.when(t < count)(lambda: self.fold(t))
        for hop in range(LINE):
            c = t - hop
            valid = (c >= 0) & (c < count)
            if hop < LINE - 1:
                pl.when(valid & (z == hop))(lambda: self.send_up(c, hop))
                pl.when(valid & (z == LINE - 1 - hop))(lambda: self.send_down(c, LINE - 1 - hop))
            else:
                for here in range(LINE):
                    pl.when(valid & (z == here))(lambda: self.finish(c, here))

    def drain(self):
        def step(c):
            self.across(c).wait_send()
            for here in range(LINE):

                @pl.when(self.z == here)
                def _():
                    for line in range(here + 1, LINE):
                        self.up(c, line).wait_send()
                    for line in range(here):
                        self.down(c, line).wait_send()

        loop(self.b.count, step)


class Idle:
    ticks = 0

    def start(self):
        pass

    def pump(self, t):
        pass

    def drain(self):
        pass


class TpSum:
    def __init__(self, partial, out, bufs, sems):
        self.p, self.out = partial, out
        self.crossed, self.other = bufs
        self.c_s, self.c_r, self.x_s, self.x_r, self.o_s, self.o_r = sems
        self.core = lax.rem(lax.axis_index("tp"), 2)
        self.beside, self.far = tp_peers()
        self.half = partial.shape[0] // 2
        self.rows = self.half // TP_PARTS

    @staticmethod
    def scratch(rows, wide):
        return [pltpu.VMEM((rows // 2, wide), BF16)] * 2 + [DMA((TP_PARTS,))] * 6

    def spot(self, k, which):
        return pl.ds(pl.multiple_of(which * self.half + k * self.rows, 16), self.rows)

    def part(self, k):
        return pl.ds(aligned(k * self.rows, 16), self.rows)

    def first(self, k):
        return remote(
            self.p.at[self.spot(k, 1 - self.core)],
            self.crossed.at[self.part(k)],
            self.c_s.at[k],
            self.c_r.at[k],
            tp=self.beside,
        )

    def second(self, k):
        here = self.out.at[self.spot(k, self.core)]
        return remote(here, self.other.at[self.part(k)], self.x_s.at[k], self.x_r.at[k], tp=self.far)

    def third(self, k, which):
        here = self.out.at[self.spot(k, which)]
        return remote(here, here, self.o_s.at[k], self.o_r.at[k], tp=self.beside)

    def stage_one(self, k):
        self.first(k).start()

    def stage_two(self, k):
        self.first(k).wait_recv()
        mine = self.spot(k, self.core)
        add_rows(self.out.at[mine], self.p.at[mine], self.crossed.at[self.part(k)])
        self.second(k).start()

    def stage_three(self, k):
        self.second(k).wait()
        mine = self.out.at[self.spot(k, self.core)]
        add_rows(mine, mine, self.other.at[self.part(k)])
        self.third(k, self.core).start()

    def stage_four(self, k):
        self.third(k, 1 - self.core).wait_recv()

    def drain(self):
        def step(k):
            self.first(k).wait_send()
            self.third(k, self.core).wait_send()

        loop(TP_PARTS, step)


def params(number):
    return pltpu.CompilerParams(
        collective_id=number, has_side_effects=True, vmem_limit_bytes=VMEM_LIMIT
    )


ANY = pl.BlockSpec(memory_space=pl.ANY)
IN_VMEM = pl.BlockSpec(memory_space=pltpu.VMEM)
IN_SMEM = pl.BlockSpec(memory_space=pltpu.SMEM)


def shaped(shape, dtype):
    return jax.ShapeDtypeStruct(shape, dtype)


def segment_sum(value, seg):
    high = value.astype(BF16)
    low = (value - high.astype(F32)).astype(BF16)
    return dot_nn(high, seg) + dot_nn(low, seg)


def head_inverse(value, seg):
    return lax.rsqrt(segment_sum(value * value, seg) * (1.0 / HEAD) + EPS)


def thrice(table):
    return jnp.concatenate([table] * 3, axis=1)


def rope(value, cosines, sine_a, sine_b):
    wide = value.shape[1]
    ahead = pltpu.roll(value, wide - HEAD // 4, 1)
    behind = pltpu.roll(value, HEAD // 4, 1)
    return value * cosines + ahead * sine_a + behind * sine_b


def rope_back(grad, cosines, sine_a, sine_b):
    wide = grad.shape[1]
    ahead = pltpu.roll(grad * sine_b, wide - HEAD // 4, 1)
    behind = pltpu.roll(grad * sine_a, HEAD // 4, 1)
    return grad * cosines + ahead + behind


def rope_tables(row_count):
    lane = np.arange(PAIR)
    within = lane % HEAD
    quarter = HEAD // 4
    which = within // quarter
    freqs = (ROPE_BASE ** (-(within % quarter).astype(np.float32) / np.float32(quarter))).astype(np.float32)
    row = np.arange(row_count)
    frame, place = (row // FRAME_TOK).astype(np.float32), (row % FRAME_TOK).astype(np.float32)
    position = np.where(which[None, :] < 2, frame[:, None], place[:, None])
    angles = (position * freqs[None, :]).astype(np.float32)
    cosines, sines = np.cos(angles), np.sin(angles)
    even = (which % 2 == 0)[None, :]
    return (
        jnp.asarray(cosines.astype(np.float32)),
        jnp.asarray(np.where(even, -sines, 0.0).astype(np.float32)),
        jnp.asarray(np.where(even, 0.0, sines).astype(np.float32)),
    )


def segment_ones(wide):
    head = np.arange(wide) // HEAD
    return jnp.asarray((head[:, None] == head[None, :]).astype(np.float32)).astype(BF16)


def live_rows(frames_ref, start, rows, wide):
    row = start + lax.broadcasted_iota(jnp.int32, (rows, wide), 0)
    return (row < frames_ref[0] * FRAME_TOK).astype(F32)


def half_mask(rows, head, dtype):
    lane = lax.broadcasted_iota(jnp.int32, (rows, PAIR), 1)
    return ((lane < HEAD) if head == 0 else (lane >= HEAD)).astype(dtype)


def pair_lanes(pair, wide=PAIR):
    return pl.ds(pl.multiple_of(pair * wide, PAIR), wide)


def block_rows(block, rows):
    return pl.ds(pl.multiple_of(block * rows, rows), rows)


def paced(count, step, pumps, base, engine):
    if pumps == 0 or engine.ticks == 0:
        loop(count, step)
        return base
    if pumps <= count:
        every = count // pumps

        def body(i):
            step(i)
            pl.when(lax.rem(i, every) == every - 1)(lambda: engine.pump(base + lax.div(i, every)))

    else:
        each = pumps // count

        def body(i):
            step(i)
            for j in range(each):
                engine.pump(base + i * each + j)

    loop(count, body)
    return base + pumps


def finish_pumps(base, engine):
    if base < engine.ticks:
        loop(engine.ticks - base, lambda i: engine.pump(base + i))


def first_kernel(blocks, shard, cond_ref, small_ref, ada_ref, full, mod_ref, smalls_ref, act_ref, *refs):
    conds, part, parts, c_s, c_r, m_s, m_r, p_s, p_r = refs[:9]
    engine = Gather(blocks, shard, full, refs[9:])
    me = lax.axis_index("dp")
    peers = dp_peers()
    sources = [lax.rem(me + GRID - step, GRID) for step in range(1, GRID)]
    greet(peers, [])
    engine.start()
    for i, there in enumerate(peers):
        remote(cond_ref.at[there], conds.at[me], c_s.at[i], c_r.at[i], dp=there).start()
        remote(small_ref, smalls_ref.at[me], m_s.at[i], m_r.at[i], dp=there).start()
    conds[pl.ds(me, 1)] = cond_ref[pl.ds(me, 1)]
    smalls_ref[pl.ds(me, 1)] = small_ref[...][None]
    engine.pump(0)
    for i, here in enumerate(sources):
        remote(conds.at[here], conds.at[here], c_s.at[i], c_r.at[i], dp=me).wait_recv()
    cond = jnp.concatenate([conds[i] for i in range(GRID)], axis=0)
    act = (cond * (1.0 / (1.0 + jnp.exp(-cond)))).astype(BF16)
    act_ref[...] = act.astype(F32)
    width = ada_ref.shape[1] // 4
    for i in range(4):
        cols = pl.ds(i * width, width)
        product = dot_nn(act, ada_ref[:, cols])
        for j in range(GRID):
            part[j, :, cols] = product[j : j + 1, :]
    for i, there in enumerate(peers):
        remote(part.at[there], parts.at[me], p_s.at[i], p_r.at[i], dp=there).start()
    parts[pl.ds(me, 1)] = part[pl.ds(me, 1)]
    engine.pump(1)
    engine.pump(2)
    for i, here in enumerate(sources):
        remote(parts.at[here], parts.at[here], p_s.at[i], p_r.at[i], dp=me).wait_recv()
    mod_ref[...] = sum(parts[i] for i in range(GRID))
    finish_pumps(3, engine)
    engine.drain()
    for i, there in enumerate(peers):
        here = sources[i]
        remote(small_ref, smalls_ref.at[here], m_s.at[i], m_r.at[i], dp=me).wait_recv()
        remote(cond_ref.at[there], conds.at[me], c_s.at[i], c_r.at[i], dp=there).wait_send()
        remote(small_ref, smalls_ref.at[me], m_s.at[i], m_r.at[i], dp=there).wait_send()
        remote(part.at[there], parts.at[me], p_s.at[i], p_r.at[i], dp=there).wait_send()


def gather_first(shard, cond, small, w_ada):
    depth, wide = shard.shape
    blocks = Blocks(depth, wide, 96, 384)
    mods = w_ada.shape[1]
    return pl.pallas_call(
        functools.partial(first_kernel, blocks),
        out_shape=[
            shaped((GRID * depth, wide), BF16),
            shaped((1, mods), F32),
            shaped((GRID,) + small.shape, F32),
            shaped((GRID, cond.shape[2]), F32),
        ],
        in_specs=[ANY] + [IN_VMEM] * 3,
        out_specs=[ANY] + [IN_VMEM] * 3,
        scratch_shapes=[
            pltpu.VMEM((GRID, 1, cond.shape[2]), F32),
            pltpu.VMEM((GRID, 1, mods), F32),
            pltpu.VMEM((GRID, 1, mods), F32),
        ]
        + [DMA((GRID - 1,))] * 6
        + Gather.scratch(blocks.count),
        compiler_params=params(0),
    )(shard, cond, small, w_ada)


def self_kernel(blocks, *refs):
    frames, tok, weights, mult, qgain, kgain, cos_ref, sa_ref, sb_ref, seg_ref, shard = refs[:11]
    h_one, q_pre, k_pre, q_rot, k_rot, q_text, v_out, self_o, inv_l, full = refs[11:21]
    vaug, refs = refs[21], refs[22:]
    engine = Idle()
    if blocks is not None:
        engine = Gather(blocks, shard, full, refs)
        greet(dp_peers(), [])
        engine.start()
    cols = q_pre.shape[1]
    rows = tok.shape[0]
    step_rows = 256

    def project(i):
        here = block_rows(i, step_rows)
        x = tok[here, :].astype(F32)
        inverse = lax.rsqrt(jnp.mean(x * x, axis=-1, keepdims=True) + EPS)
        h = (x * inverse * mult[...]).astype(BF16)
        h_one[here, :] = h
        cosines, sine_a, sine_b = thrice(cos_ref[here, :]), thrice(sa_ref[here, :]), thrice(sb_ref[here, :])
        q = dot_nn(h, weights[:, :cols])
        q_pre[here, :] = q
        qn = q * head_inverse(q, seg_ref[...]) * qgain[...]
        q_text[here, :] = (qn * SCALE).astype(BF16)
        q_rot[here, :] = (rope(qn, cosines, sine_a, sine_b) * SCALE).astype(BF16)
        k = dot_nn(h, weights[:, cols : 2 * cols])
        k_pre[here, :] = k
        kn = k * head_inverse(k, seg_ref[...]) * kgain[...]
        k_rot[here, :] = rope(kn, cosines, sine_a, sine_b).astype(BF16)
        v = dot_nn(h, weights[:, 2 * cols : 3 * cols]).astype(BF16)
        v_out[here, :] = v
        live = live_rows(frames, i * step_rows, step_rows, PAIR).astype(BF16)
        for pair in range(cols // PAIR):
            vaug[here, 2 * pair * PAIR : (2 * pair + 1) * PAIR] = v[:, pair * PAIR : (pair + 1) * PAIR] * live
            vaug[here, (2 * pair + 1) * PAIR : (2 * pair + 2) * PAIR] = live

    def attend(i):
        pair, block = lax.div(i, rows // step_rows), lax.rem(i, rows // step_rows)
        here, lanes = block_rows(block, step_rows), pair_lanes(pair)
        q = q_rot[here, lanes]
        keys = k_rot[:, lanes]
        values = vaug[:, pair_lanes(pair, 2 * PAIR)]
        outs = jnp.zeros((step_rows, PAIR), F32)
        sums = jnp.zeros((step_rows, PAIR), F32)
        for head in range(2):
            mask = half_mask(step_rows, head, BF16)
            p = jnp.exp(dot_nt(q * mask, keys)).astype(BF16)
            both = dot_nn(p, values)
            wide_mask = half_mask(step_rows, head, F32)
            outs = outs + both[:, :PAIR] * wide_mask
            sums = sums + both[:, PAIR:] * wide_mask
        inverse = 1.0 / sums
        inv_l[here, lanes] = inverse
        self_o[here, lanes] = outs * inverse

    base = paced(rows // step_rows, project, 4, 0, engine)
    base = paced(cols // PAIR * (rows // step_rows), attend, 6, base, engine)
    finish_pumps(base, engine)
    engine.drain()


def self_forward(clips, frames, tokens, full_attn, mult, qgain, kgain, tables, seg, text_shard):
    rows, wide = tokens.shape
    cols = qgain.shape[1]
    depth, text_wide = text_shard.shape
    blocks = Blocks(depth, text_wide, 64, text_wide) if clips == GRID else None
    f, b = shaped((rows, cols), F32), shaped((rows, cols), BF16)
    return pl.pallas_call(
        functools.partial(self_kernel, blocks),
        out_shape=[shaped((rows, wide), BF16), f, f, b, b, b, b, f, f, shaped((GRID * depth, text_wide), BF16)],
        in_specs=[IN_SMEM] + [IN_VMEM] * 9 + [ANY],
        out_specs=[IN_VMEM] * 9 + [ANY],
        scratch_shapes=[pltpu.VMEM((rows, 2 * cols), BF16)]
        + (Gather.scratch(blocks.count) if blocks is not None else []),
        compiler_params=params(1) if blocks is not None else pltpu.CompilerParams(vmem_limit_bytes=VMEM_LIMIT),
    )(frames, tokens, full_attn, mult, qgain, kgain, *tables, seg, text_shard)


def text_kernel(blocks, *refs):
    frames, text, w_text, kygain, seg_ref, q_text, self_o, gate, weights, tok, tanh_attn, mult, shard = refs[:13]
    ky_pre, kyr, vy_out, text_o, inv_lt, mixed, attn_sum, h_two, full = refs[13:22]
    vaug, partial = refs[22:24]
    sums = TpSum(partial, attn_sum, refs[24:26], refs[26:32])
    engine = Idle()
    if blocks is not None:
        engine = Gather(blocks, shard, full, refs[32:])
        greet(dp_peers(), tp_peers())
        engine.start()
    else:
        greet([], tp_peers())
    cols, rows = self_o.shape[1], tok.shape[0]
    step_rows = 256
    rows_t = text.shape[0]

    ky = dot_nn(text[...], w_text[:, :cols])
    ky_pre[...] = ky
    kyr[...] = (ky * head_inverse(ky, seg_ref[...]) * kygain[...]).astype(BF16)
    engine.pump(0)
    vy = dot_nn(text[...], w_text[:, cols:]).astype(BF16)
    vy_out[...] = vy
    for pair in range(cols // PAIR):
        vaug[:, 2 * pair * PAIR : (2 * pair + 1) * PAIR] = vy[:, pair * PAIR : (pair + 1) * PAIR]
        vaug[:, (2 * pair + 1) * PAIR : (2 * pair + 2) * PAIR] = jnp.ones((rows_t, PAIR), BF16)
    engine.pump(1)

    def attend(i):
        pair, block = lax.div(i, rows // step_rows), lax.rem(i, rows // step_rows)
        here, lanes = block_rows(block, step_rows), pair_lanes(pair)
        q = q_text[here, lanes]
        keys = kyr[:, lanes]
        values = vaug[:, pair_lanes(pair, 2 * PAIR)]
        outs = jnp.zeros((step_rows, PAIR), F32)
        total = jnp.zeros((step_rows, PAIR), F32)
        for head in range(2):
            p = jnp.exp(dot_nt(q * half_mask(step_rows, head, BF16), keys)).astype(BF16)
            both = dot_nn(p, values)
            wide_mask = half_mask(step_rows, head, F32)
            outs = outs + both[:, :PAIR] * wide_mask
            total = total + both[:, PAIR:] * wide_mask
        inverse = 1.0 / total
        inv_lt[here, lanes] = inverse
        out = outs * inverse
        text_o[here, lanes] = out
        mixed[here, lanes] = (self_o[here, lanes] + gate[:, lanes] * out).astype(BF16)

    base = paced(cols // PAIR * (rows // step_rows), attend, 4, 2, engine)

    def project(which):
        def step(i):
            start = which * sums.half + i * step_rows
            here = pl.ds(pl.multiple_of(start, 16), step_rows)
            partial[here, :] = dot_nt(mixed[here, :], weights[...]).astype(BF16)

        return step

    parts_each = TP_PARTS // (sums.half // step_rows)

    def project_send(i):
        project(1 - sums.core)(i)
        loop(parts_each, lambda k: sums.stage_one(i * parts_each + k))

    base = paced(sums.half // step_rows, project_send, 2, base, engine)
    loop(sums.half // step_rows, project(sums.core))
    loop(TP_PARTS, sums.stage_two)

    def update(k, which):
        here = sums.spot(k, which)
        live = live_rows(frames, which * sums.half + k * sums.rows, sums.rows, tok.shape[1])
        state = tok[here, :].astype(F32) + live * tanh_attn[...] * attn_sum[here, :].astype(F32)
        inverse = lax.rsqrt(jnp.mean(state * state, axis=-1, keepdims=True) + EPS)
        h_two[here, :] = (state * inverse * mult[...]).astype(BF16)

    def three(k):
        sums.stage_three(k)
        update(k, sums.core)

    base = paced(TP_PARTS, three, 8, base, engine)

    def four(k):
        sums.stage_four(k)
        update(k, 1 - sums.core)

    base = paced(TP_PARTS, four, 2, base, engine)
    finish_pumps(base, engine)
    sums.drain()
    engine.drain()


def text_forward(
    clips, frames, text, full_text, kygain, seg, q_text, self_o, gate, w_out, tokens, tanh_attn, mult, ffn_shard
):
    rows, wide = tokens.shape
    rows_t = text.shape[0]
    cols = kygain.shape[1]
    depth, ffn_wide = ffn_shard.shape
    blocks = Blocks(depth, ffn_wide, 96, 384) if clips == GRID else None
    f, b = shaped((rows, cols), F32), shaped((rows, cols), BF16)
    return pl.pallas_call(
        functools.partial(text_kernel, blocks),
        out_shape=[
            shaped((rows_t, cols), F32),
            shaped((rows_t, cols), BF16),
            shaped((rows_t, cols), BF16),
            f,
            f,
            b,
            shaped((rows, wide), BF16),
            shaped((rows, wide), BF16),
            shaped((GRID * depth, ffn_wide), BF16),
        ],
        in_specs=[IN_SMEM] + [IN_VMEM] * 11 + [ANY],
        out_specs=[IN_VMEM] * 8 + [ANY],
        scratch_shapes=[pltpu.VMEM((rows_t, 2 * cols), BF16), pltpu.VMEM((rows, wide), BF16)]
        + TpSum.scratch(rows, wide)
        + (Gather.scratch(blocks.count) if blocks is not None else []),
        compiler_params=params(2),
    )(frames, text, full_text, kygain, seg, q_text, self_o, gate, w_out, tokens, tanh_attn, mult, ffn_shard)


def state_kernel(blocks, *refs):
    frames, partial, tok, attn_sum, cot, tanh_attn, mult, grad = refs[:8]
    grad_attn, grad_state, colsums, out = refs[8:12]
    grad_n = refs[12]
    sums = TpSum(partial, grad_n, refs[13:15], refs[15:21])
    engine = Idle()
    if blocks is not None:
        engine = Scatter(blocks, grad, out, refs[21:25], refs[25:])
        greet(dp_peers(), tp_peers())
        engine.start()
    else:
        greet([], tp_peers())
    loop(TP_PARTS, sums.stage_one)
    colsums[...] = jnp.zeros_like(colsums)

    def update(k, which):
        here = sums.spot(k, which)
        live = live_rows(frames, which * sums.half + k * sums.rows, sums.rows, tok.shape[1])
        added = attn_sum[here, :].astype(F32)
        state = tok[here, :].astype(F32) + live * tanh_attn[...] * added
        inverse = lax.rsqrt(jnp.mean(state * state, axis=-1, keepdims=True) + EPS)
        hat = state * inverse
        g = grad_n[here, :].astype(F32)
        scaled = g * mult[...]
        g_hat = g * hat
        back = inverse * (scaled - hat * jnp.mean(scaled * hat, axis=-1, keepdims=True))
        total = cot[here, :].astype(F32) + back
        grad_state[here, :] = total
        live_total = live * total
        grad_attn[here, :] = (tanh_attn[...] * live_total).astype(BF16)
        colsums[0:1, :] += jnp.sum(g_hat, axis=0, keepdims=True)
        colsums[1:2, :] += jnp.sum(live_total * added, axis=0, keepdims=True)

    base = paced(TP_PARTS, sums.stage_two, 2, 0, engine)

    def three(k):
        sums.stage_three(k)
        update(k, sums.core)

    base = paced(TP_PARTS, three, 8, base, engine)

    def four(k):
        sums.stage_four(k)
        update(k, 1 - sums.core)

    base = paced(TP_PARTS, four, 1, base, engine)
    finish_pumps(base, engine)
    sums.drain()
    engine.drain()


def lined(grad):
    return grad.reshape(LINE, 2, grad.shape[0] // GRID, grad.shape[1])


def state_backward(clips, frames, partial, tokens, attn_sum, cotangent, tanh_attn, mult, g_down):
    rows, wide = tokens.shape
    depth, down_wide = g_down.shape[0] // clips, g_down.shape[1]
    blocks = Blocks(depth, down_wide, 96, 256) if clips == GRID else None
    view = lined(g_down) if blocks is not None else g_down
    return pl.pallas_call(
        functools.partial(state_kernel, blocks),
        out_shape=[
            shaped((rows, wide), BF16),
            shaped((rows, wide), F32),
            shaped((8, wide), F32),
            shaped((depth, down_wide), F32),
        ],
        in_specs=[IN_SMEM] + [IN_VMEM] * 6 + [ANY],
        out_specs=[IN_VMEM] * 4,
        scratch_shapes=[pltpu.VMEM((rows, wide), BF16)]
        + TpSum.scratch(rows, wide)
        + (Scatter.scratch(blocks) if blocks is not None else []),
        compiler_params=params(3),
    )(frames, partial, tokens, attn_sum, cotangent, tanh_attn, mult, view)


def attn_back_kernel(blocks, *refs):
    (frames, grad_attn, weights, gate, cos_ref, sa_ref, sb_ref, seg_ref, qgain, kgain, kygain) = refs[:11]
    (q_pre, k_pre, q_rot, k_rot, q_text, v_ref, self_o, inv_l) = refs[11:19]
    (ky_pre, kyr, vy, text_o, inv_lt, partial, grad) = refs[19:26]
    grad_qkv, grad_text, gains, ffn_sum, out = refs[26:31]
    do_self, do_text, d_self, d_text, dq_rot, dq_text, dk, dv, dky, dvy, klive = refs[31:42]
    sums = TpSum(partial, ffn_sum, refs[42:44], refs[44:50])
    engine = Idle()
    if blocks is not None:
        engine = Scatter(blocks, grad, out, refs[50:54], refs[54:])
        greet(dp_peers(), tp_peers())
        engine.start()
    else:
        greet([], tp_peers())
    loop(TP_PARTS, sums.stage_one)
    rows, cols = q_rot.shape
    rows_t = kyr.shape[0]
    step_rows = 256
    blocks_here = rows // step_rows
    pairs = cols // PAIR
    gains[...] = jnp.zeros_like(gains)
    dk[...] = jnp.zeros_like(dk)
    dv[...] = jnp.zeros_like(dv)
    dky[...] = jnp.zeros_like(dky)
    dvy[...] = jnp.zeros_like(dvy)

    def halves(value, first_head):
        lane = lax.broadcasted_iota(jnp.int32, (step_rows, PAIR), 1)
        out = jnp.zeros((step_rows, PAIR), F32)
        for head in range(2):
            total = jnp.sum(value * half_mask(step_rows, head, F32), axis=-1, keepdims=True)
            high = total.astype(BF16).astype(F32)
            spot = 2 * (first_head + head)
            out = out + jnp.where(lane == spot, high, jnp.where(lane == spot + 1, total - high, 0.0))
        return out

    def start_rows(i):
        here = block_rows(i, step_rows)
        g = dot_nn(grad_attn[here, :], weights[...])
        other = text_o[here, :]
        gains[3:4, :] += jnp.sum(g * other, axis=0, keepdims=True)
        first = (g * inv_l[here, :]).astype(BF16)
        do_self[here, :] = first
        second = (g * gate[...] * inv_lt[here, :]).astype(BF16)
        do_text[here, :] = second
        dot_self = first.astype(F32) * self_o[here, :]
        dot_text = second.astype(F32) * other
        each = [slice(pair * PAIR, (pair + 1) * PAIR) for pair in range(pairs)]
        d_self[here, :] = sum(halves(dot_self[:, lanes], 2 * pair) for pair, lanes in enumerate(each)).astype(BF16)
        d_text[here, :] = sum(halves(dot_text[:, lanes], 2 * pair) for pair, lanes in enumerate(each)).astype(BF16)
        klive[here, :] = k_rot[here, :] * live_rows(frames, i * step_rows, step_rows, cols).astype(BF16)

    def back(q_ref, k_ref, k_live, v_in, do_ref, d_ref, dq_ref, dk_ref, dv_ref):
        def step(i):
            pair, block = lax.div(i, blocks_here), lax.rem(i, blocks_here)
            here, lanes = block_rows(block, step_rows), pair_lanes(pair)
            keys = k_ref[:, lanes]
            values = v_in[:, lanes]
            lane = lax.broadcasted_iota(jnp.int32, values.shape, 1)
            dq = jnp.zeros((step_rows, PAIR), F32)
            for head in range(2):
                mask = half_mask(step_rows, head, BF16)
                q = q_ref[here, lanes] * mask
                do = do_ref[here, lanes] * mask
                scores = dot_nt(keys, q)
                p = jnp.exp(scores)
                dv_ref[:, lanes] += dot_nn(p.astype(BF16), do)
                spot = 2 * (2 * pair + head)
                minus = jnp.where((lane == spot) | (lane == spot + 1), -1.0, 0.0).astype(BF16)
                left = jnp.concatenate([values, minus], axis=1)
                right = jnp.concatenate([do, d_ref[here, :]], axis=1)
                ds = (p * dot_nt(left, right)).astype(BF16)
                dk_ref[:, lanes] += dot_nn(ds, q)
                key_mask = half_mask(keys.shape[0], head, BF16)
                dq = dq + dot_tn(ds, k_live[:, lanes] * key_mask)
            dq_ref[here, lanes] = dq * SCALE

        return step

    base = paced(blocks_here, start_rows, 2, 0, engine)
    self_back = back(q_rot, k_rot, klive, v_ref, do_self, d_self, dq_rot, dk, dv)

    def self_step(i):
        self_back(i)
        pl.when(i < TP_PARTS)(lambda: sums.stage_two(i))

    base = paced(pairs * blocks_here, self_step, 6, base, engine)
    text_back = back(q_text, kyr, kyr, vy, do_text, d_text, dq_text, dky, dvy)

    def text_step(i):
        text_back(i)
        pl.when(i < TP_PARTS)(lambda: sums.stage_three(i))

    base = paced(pairs * blocks_here, text_step, 2, base, engine)

    def norm_back(grad_normed, pre, gain, row):
        inverse = head_inverse(pre, seg_ref[...])
        hat = pre * inverse
        gains[row : row + 1, :] += jnp.sum(grad_normed * hat, axis=0, keepdims=True)
        scaled = grad_normed * gain
        average = segment_sum(scaled * hat, seg_ref[...]) * (1.0 / HEAD)
        return (inverse * (scaled - hat * average)).astype(BF16)

    def end_rows(i):
        here = block_rows(i, step_rows)
        cosines, sine_a, sine_b = thrice(cos_ref[here, :]), thrice(sa_ref[here, :]), thrice(sb_ref[here, :])
        live = live_rows(frames, i * step_rows, step_rows, cols)
        dqn = rope_back(dq_rot[here, :], cosines, sine_a, sine_b) + dq_text[here, :]
        grad_qkv[here, :cols] = norm_back(dqn, q_pre[here, :], qgain[...], 0)
        dkn = rope_back(dk[here, :] * live, cosines, sine_a, sine_b)
        grad_qkv[here, cols : 2 * cols] = norm_back(dkn, k_pre[here, :], kgain[...], 1)
        grad_qkv[here, 2 * cols : 3 * cols] = (dv[here, :] * live).astype(BF16)

    base = paced(blocks_here, end_rows, 1, base, engine)
    grad_text[:, :cols] = norm_back(dky[...], ky_pre[...], kygain[...], 2)
    grad_text[:, cols:] = dvy[...].astype(BF16)
    finish_pumps(base, engine)
    loop(TP_PARTS, sums.stage_four)
    sums.drain()
    engine.drain()


def attn_backward(clips, frames, grad_attn, w_out, gate, tables, seg, gain_rows, saved, partial, g_in):
    rows, wide = grad_attn.shape
    cols = gate.shape[1]
    rows_t = saved[8].shape[0]
    depth, in_wide = g_in.shape[0] // clips, g_in.shape[1]
    blocks = Blocks(depth, in_wide, 192, 256) if clips == GRID else None
    view = lined(g_in) if blocks is not None else g_in
    f, b = pltpu.VMEM((rows, cols), F32), pltpu.VMEM((rows, cols), BF16)
    ft = pltpu.VMEM((rows_t, cols), F32)
    slim = pltpu.VMEM((rows, PAIR), BF16)
    return pl.pallas_call(
        functools.partial(attn_back_kernel, blocks),
        out_shape=[
            shaped((rows, 3 * cols), BF16),
            shaped((rows_t, 2 * cols), BF16),
            shaped((8, cols), F32),
            shaped((rows, wide), BF16),
            shaped((depth, in_wide), F32),
        ],
        in_specs=[IN_SMEM] + [IN_VMEM] * 24 + [ANY],
        out_specs=[IN_VMEM] * 5,
        scratch_shapes=[b, b, slim, slim, f, f, f, f, ft, ft, b]
        + TpSum.scratch(rows, wide)
        + (Scatter.scratch(blocks) if blocks is not None else []),
        compiler_params=params(4),
    )(frames, grad_attn, w_out, gate, *tables, seg, *gain_rows, *saved, partial, view)


def last_kernel(blocks_t, blocks_a, *refs):
    partial, tok, grad_state, mult, gain, lift, vec_in, grad_t, grad_a = refs[:9]
    grad_tokens, vecs, out_t, out_a = refs[9:13]
    grad_n, colsum, vec = refs[13:16]
    sums = TpSum(partial, grad_n, refs[16:18], refs[18:24])
    me = lax.axis_index("dp")
    text_engine, attn_engine = Idle(), Idle()
    peers = []
    if blocks_t is not None:
        v_s, v_r = refs[24:26]
        peers = dp_peers()
        text_engine = Scatter(blocks_t, grad_t, out_t, refs[26:30], refs[30:37])
        attn_engine = Scatter(blocks_a, grad_a, out_a, refs[37:41], refs[41:48])
        greet(peers, tp_peers())
        text_engine.start()
    else:
        greet([], tp_peers())
    loop(TP_PARTS, sums.stage_one)
    colsum[...] = jnp.zeros_like(colsum)

    def update(k, which):
        here = sums.spot(k, which)
        x = tok[here, :].astype(F32)
        inverse = lax.rsqrt(jnp.mean(x * x, axis=-1, keepdims=True) + EPS)
        hat = x * inverse
        g = grad_n[here, :].astype(F32)
        scaled = g * mult[...]
        back = inverse * (scaled - hat * jnp.mean(scaled * hat, axis=-1, keepdims=True))
        grad_tokens[here, :] = (grad_state[here, :] + back).astype(BF16)
        colsum[...] += jnp.sum(g * hat, axis=0, keepdims=True)

    base = paced(TP_PARTS, sums.stage_two, 2, 0, text_engine)

    def three(k):
        sums.stage_three(k)
        update(k, sums.core)

    base = paced(TP_PARTS, three, 8, base, text_engine)
    finish_pumps(base, text_engine)
    attn_engine.start()

    def four(k):
        sums.stage_four(k)
        update(k, 1 - sums.core)

    base = paced(TP_PARTS, four, 4, 0, attn_engine)
    vec[...] = vec_in[...]
    wide = tok.shape[1]
    vec[:, :wide] = colsum[...] * gain[...]
    vec[:, 4 * wide : 5 * wide] = colsum[...] * lift[...]
    for i, there in enumerate(peers):
        remote(vec, vecs.at[me], v_s.at[i], v_r.at[i], dp=there).start()
    finish_pumps(base, attn_engine)
    vecs[pl.ds(me if peers else 0, 1)] = vec[...][None]
    for i, there in enumerate(peers):
        here = lax.rem(me + GRID - 1 - i, GRID)
        remote(vec, vecs.at[here], v_s.at[i], v_r.at[i], dp=me).wait_recv()
        remote(vec, vecs.at[me], v_s.at[i], v_r.at[i], dp=there).wait_send()
    sums.drain()
    text_engine.drain()
    attn_engine.drain()


def last_backward(clips, partial, tokens, grad_state, mult, gain, lift, vec, g_text, g_attn):
    rows, wide = tokens.shape
    grid = clips == GRID
    depth_t, wide_t = g_text.shape[0] // clips, g_text.shape[1]
    depth_a, wide_a = g_attn.shape[0] // clips, g_attn.shape[1]
    blocks_t = Blocks(depth_t, wide_t, 64, wide_t) if grid else None
    blocks_a = Blocks(depth_a, wide_a, 96, 384) if grid else None
    views = [lined(g_text), lined(g_attn)] if grid else [g_text, g_attn]
    return pl.pallas_call(
        functools.partial(last_kernel, blocks_t, blocks_a),
        out_shape=[
            shaped((rows, wide), BF16),
            shaped(((GRID if grid else 1),) + vec.shape, F32),
            shaped((depth_t, wide_t), F32),
            shaped((depth_a, wide_a), F32),
        ],
        in_specs=[IN_VMEM] * 7 + [ANY] * 2,
        out_specs=[IN_VMEM] * 4,
        scratch_shapes=[
            pltpu.VMEM((rows, wide), BF16),
            pltpu.VMEM((1, wide), F32),
            pltpu.VMEM(vec.shape, F32),
        ]
        + TpSum.scratch(rows, wide)
        + ([DMA((GRID - 1,))] * 2 + Scatter.scratch(blocks_t) + Scatter.scratch(blocks_a) if grid else []),
        compiler_params=params(5),
    )(partial, tokens, grad_state, mult, gain, lift, vec, *views)


def gather_plain(shard):
    return lax.all_gather(shard, "dp", axis=0, tiled=True)


def scatter_plain(grad):
    return lax.psum_scatter(grad, "dp", scatter_dimension=0, tiled=True).astype(F32)


def first_plain(shard, cond, small, w_ada):
    act = jax.nn.silu(lax.all_to_all(cond[:, 0], "dp", 0, 0, tiled=True)).astype(BF16)
    parts = dot_nn(act, w_ada)
    mod = lax.psum_scatter(parts, "dp", scatter_dimension=0, tiled=True)
    return gather_plain(shard), mod, lax.all_gather(small, "dp", axis=0), act.astype(F32)


def on_device(
    tokens,
    text,
    cond,
    frames,
    w_query,
    w_key,
    w_value,
    w_out,
    w_text_key,
    w_text_value,
    w_gate,
    w_up,
    w_down,
    w_ada,
    ada_bias,
    norm_one,
    norm_two,
    query_gain,
    key_gain,
    text_key_gain,
    cross_gate,
    cotangent,
):
    rows, wide = tokens.shape
    clips = lax.axis_size("dp")
    grid = clips == GRID
    cols, units = w_query.shape[1], w_gate.shape[1]
    heads_here = cols // HEAD
    bias_rows, gain_rows = ada_bias.shape[0], norm_one.shape[0]
    small = jnp.concatenate([ada_bias, norm_one, norm_two]).astype(F32)[None, :]
    cond_rows = cond.astype(F32).reshape(clips, 1, -1)
    attn_shard = jnp.concatenate([w_query, w_key, w_value, w_out.T], axis=1)
    text_shard = jnp.concatenate([w_text_key, w_text_value], axis=1)
    ffn_shard = jnp.concatenate([w_gate, w_up, w_down.T], axis=1)
    first = gather_first if grid else first_plain
    full_attn, mod_sum, smalls, act_rows = first(attn_shard, cond_rows, small, w_ada)
    modulation = mod_sum[0] + smalls[:, 0, :bias_rows].reshape(-1)
    gain_one = smalls[:, 0, bias_rows : bias_rows + gain_rows].reshape(-1)
    gain_two = smalls[:, 0, bias_rows + gain_rows :].reshape(-1)
    scale_attn, gate_attn, scale_ffn, gate_ffn = jnp.split(modulation, 4)
    lift_one, lift_two = 1.0 + scale_attn, 1.0 + scale_ffn
    mult_one, mult_two = (gain_one * lift_one)[None, :], (gain_two * lift_two)[None, :]
    tanh_attn, tanh_ffn = jnp.tanh(gate_attn), jnp.tanh(gate_ffn)
    qgain = query_gain.astype(F32)[None, :]
    kgain = key_gain.astype(F32)[None, :]
    kygain = text_key_gain.astype(F32)[None, :]
    gate_tanh = jnp.tanh(cross_gate.astype(F32))
    gate_wide = jnp.repeat(gate_tanh, HEAD)[None, :]
    tables, seg = rope_tables(rows), segment_ones(cols)
    out_turned = full_attn[:, 3 * cols :]

    h_one, q_pre, k_pre, q_rot, k_rot, q_text, values, self_o, inv_l, full_text = self_forward(
        clips, frames, tokens, full_attn, mult_one, qgain, kgain, tables, seg, text_shard
    )
    if not grid:
        full_text = gather_plain(text_shard)
    ky_pre, kyr, vy, text_o, inv_lt, mixed, attn_sum, h_two, full_ffn = text_forward(
        clips,
        frames,
        text,
        full_text,
        kygain,
        seg,
        q_text,
        self_o,
        gate_wide,
        out_turned,
        tokens,
        tanh_attn[None, :],
        mult_two,
        ffn_shard,
    )
    if not grid:
        full_ffn = gather_plain(ffn_shard)
    live = (jnp.arange(rows, dtype=jnp.int32) < frames[0] * FRAME_TOK).astype(F32)[:, None]

    gate_pre = dot_nn(h_two, full_ffn[:, :units])
    up_pre = dot_nn(h_two, full_ffn[:, units : 2 * units])
    down_turned = full_ffn[:, 2 * units :]
    logistic = jax.nn.sigmoid(gate_pre)
    swish = gate_pre * logistic
    hidden_units = (swish * up_pre).astype(BF16)
    grad_result = cotangent.astype(F32)
    grad_ffn = (live * tanh_ffn * grad_result).astype(BF16)
    grad_hidden = dot_nn(grad_ffn, down_turned)
    g_down = dot_tn(grad_ffn, hidden_units).astype(BF16)
    grad_gate_pre = (grad_hidden * up_pre * logistic * (1.0 + gate_pre * (1.0 - logistic))).astype(BF16)
    grad_up_pre = (grad_hidden * swish).astype(BF16)
    grad_in = jnp.concatenate([grad_gate_pre, grad_up_pre], axis=1)
    partial_two = dot_nt(grad_in, full_ffn[:, : 2 * units]).astype(BF16)
    grad_attn, grad_state, sums_two, s_down = state_backward(
        clips, frames, partial_two, tokens, attn_sum, cotangent, tanh_attn[None, :], mult_two, g_down
    )
    g_in = dot_tn(h_two, grad_in).astype(BF16)
    partial_ffn = dot_nt(hidden_units, down_turned).astype(BF16)
    saved = (q_pre, k_pre, q_rot, k_rot, q_text, values, self_o, inv_l, ky_pre, kyr, vy, text_o, inv_lt)
    grad_qkv, grad_text, gains, ffn_sum, s_in = attn_backward(
        clips, frames, grad_attn, out_turned, gate_wide, tables, seg, (qgain, kgain, kygain), saved, partial_ffn, g_in
    )
    ffn_sum = ffn_sum.astype(F32)
    hidden_state = tokens.astype(F32) + live * tanh_attn * attn_sum.astype(F32)
    result = (hidden_state + live * tanh_ffn * ffn_sum).astype(BF16)
    grad_gate_ffn = jnp.sum(live * ffn_sum * grad_result, axis=0) * (1.0 - tanh_ffn * tanh_ffn)
    g_text = dot_tn(text, grad_text).astype(BF16)
    g_attn = jnp.concatenate(
        [dot_tn(h_one, grad_qkv).astype(BF16), dot_tn(grad_attn, mixed).astype(BF16)], axis=1
    )
    partial_one = dot_nt(grad_qkv, full_attn[:, : 3 * cols]).astype(BF16)
    g_cross_gate = jnp.sum(gains[3].reshape(heads_here, HEAD), axis=1) * (1.0 - gate_tanh * gate_tanh)
    blank = jnp.zeros((wide,), F32)
    vec = jnp.concatenate(
        [
            blank,
            sums_two[1] * (1.0 - tanh_attn * tanh_attn),
            sums_two[0] * gain_two,
            grad_gate_ffn,
            blank,
            sums_two[0] * lift_two,
            gains[0],
            gains[1],
            gains[2],
            g_cross_gate,
            jnp.zeros((-heads_here % 128,), F32),
        ]
    )[None, :]
    grad_tokens, vecs, s_text, s_attn = last_backward(
        clips, partial_one, tokens, grad_state, mult_one, gain_one[None, :], lift_one[None, :], vec, g_text, g_attn
    )
    if not grid:
        s_down, s_in, s_text, s_attn = (scatter_plain(g) for g in (g_down, g_in, g_text, g_attn))
        vecs = lax.all_gather(vecs[0], "dp", axis=0)
    vecs = vecs[:, 0, :]
    mod_wide = 4 * wide
    g_ada = lax.dot_general(
        act_rows,
        vecs[:, :mod_wide],
        (((0,), (0,)), ((), ())),
        precision=lax.Precision.HIGHEST,
        preferred_element_type=F32,
    )
    sums = jnp.sum(vecs, axis=0)
    me = lax.axis_index("dp")
    g_bias = lax.dynamic_slice(sums, (me * bias_rows,), (bias_rows,))
    g_norm_one = lax.dynamic_slice(sums, (mod_wide + me * gain_rows,), (gain_rows,))
    g_norm_two = lax.dynamic_slice(sums, (mod_wide + wide + me * gain_rows,), (gain_rows,))
    rest = sums[mod_wide + 2 * wide :]
    return (
        result,
        grad_tokens,
        s_attn[:, :cols],
        s_attn[:, cols : 2 * cols],
        s_attn[:, 2 * cols : 3 * cols],
        s_attn[:, 3 * cols :].T,
        s_text[:, :cols],
        s_text[:, cols:],
        s_in[:, :units],
        s_in[:, units:],
        s_down.T,
        g_ada,
        g_bias,
        g_norm_one,
        g_norm_two,
        rest[:cols],
        rest[cols : 2 * cols],
        rest[2 * cols : 3 * cols],
        rest[3 * cols : 3 * cols + heads_here],
    )


def solution(mesh):
    placed = (
        P("dp", None),
        P("dp", None),
        P("dp", None),
        P("dp"),
        P("dp", "tp"),
        P("dp", "tp"),
        P("dp", "tp"),
        P("tp", "dp"),
        P("dp", "tp"),
        P("dp", "tp"),
        P("dp", "tp"),
        P("dp", "tp"),
        P("tp", "dp"),
        P("dp", None),
        P("dp"),
        P("dp"),
        P("dp"),
        P("tp"),
        P("tp"),
        P("tp"),
        P("tp"),
        P("dp", None),
    )
    return jax.shard_map(
        on_device,
        mesh=mesh,
        in_specs=placed,
        out_specs=(
            P("dp", None),
            P("dp", None),
            P("dp", "tp"),
            P("dp", "tp"),
            P("dp", "tp"),
            P("tp", "dp"),
            P("dp", "tp"),
            P("dp", "tp"),
            P("dp", "tp"),
            P("dp", "tp"),
            P("tp", "dp"),
            P("dp", None),
            P("dp"),
            P("dp"),
            P("dp"),
            P("tp"),
            P("tp"),
            P("tp"),
            P("tp"),
        ),
        check_vma=False,
    )
```

time: 2390 us -> 725 us (0.30)
  waiting for transfers between devices: 1890 us -> 0 us
  Pallas kernels: 0 us -> 578 us
  matrix products: 267 us -> 76.7 us
  blocking collectives: 95.6 us -> 0 us
  other arithmetic: 87 us -> 18.8 us
    reduce_scatter x10 -> x0, waiting for transfers between devices: 1220 us -> none  [the longest x1 407 us: on_device(): g_ada = lax.psum_scatter(ada_local, 'dp', scatter_dimension=0, tiled=True)]
    pallas_call x0 -> x6, Pallas kernels: none -> 578 us  [the longest x1 156 us: last_backward(): pl.pallas_call(functools.partial(last_kernel, blocks_t, blocks_a), out_sh...]
    all_gather x10 -> x0, waiting for transfers between devices: 473 us -> none  [the longest x1 172 us: on_device(): ada_full = lax.all_gather(w_ada, 'dp', axis=0, tiled=True)]
    dot_general x67 -> x12, matrix products: 267 us -> 76.7 us  [the longest x5 27.4 us: dot_tn(): lax.dot_general(left, right, (((0,), (0,)), ((), ())), preferred_element_...]
    psum x3 -> x0, waiting for transfers between devices: 183 us -> none  [the longest x1 118 us: on_device(): lax.psum(jnp.dot(hidden_units, full_down, preferred_element_type=jnp.floa...]
    unnamed x2 -> x0, blocking collectives: 63.2 us -> none
    all_gather x1 -> x0, blocking collectives: 32.5 us -> none  [fetch(): lax.all_gather(ada_bias, 'dp', axis=0, tiled=True)]
    convert_element_type x15 -> x2, other arithmetic: 31.5 us -> 0.6 us  [the longest x1 0.6 us: on_device(): small = jnp.concatenate([ada_bias, norm_one, norm_two]).astype(F32)[None, :]]
  transfers between devices with their start and end apart: 23 -> 0, of which waited for: 20 -> 0; matrix products, arithmetic and copies ran while one was open for 9% -> 0% of each run, Pallas kernels for 0% -> 0%
where the time goes in v2:
time: 725 us; the launch traced here: 717 us
  Pallas kernels  578 us (80%)
  matrix products  76.7 us (11%)
  local copies, waits for them, and re-layouts  42.7 us (6%)
  other arithmetic  18.8 us (3%)
    pallas_call x1, Pallas kernels, last_backward(): pl.pallas_call(functools.partial(last_kernel, blocks_t, blocks_a), out_sh...  156 us
    pallas_call x1, Pallas kernels, text_forward(): pl.pallas_call(functools.partial(text_kernel, blocks), out_shape=[shaped(...  118 us
    pallas_call x1, Pallas kernels, attn_backward(): pl.pallas_call(functools.partial(attn_back_kernel, blocks), out_shape=[sh...  101 us
    pallas_call x1, Pallas kernels, self_forward(): pl.pallas_call(functools.partial(self_kernel, blocks), out_shape=[shaped(...  79.5 us
    pallas_call x1, Pallas kernels, gather_first(): pl.pallas_call(functools.partial(first_kernel, blocks), out_shape=[shaped...  64.4 us
    pallas_call x1, Pallas kernels, state_backward(): pl.pallas_call(functools.partial(state_kernel, blocks), out_shape=[shaped...  58 us
    dot_general x5, matrix products, dot_tn(): lax.dot_general(left, right, (((0,), (0,)), ((), ())), preferred_element_...  27.4 us
    dot_general x3, matrix products, dot_nn(): return jnp.dot(left, right, preferred_element_type=F32)  22.8 us

profile of v2, /device:TPU:0, one launch (start us, length us, event | category | flops | bytes accessed | tf_op | source)
XLA Modules:
  0.0 717.5 jit_solution(10472668896793925149)
XLA Ops:
  14.4 2.3 pad_maximum_fusion.4.refs_12_
  16.8 64.4 %shard_map.393 = (bf16[1536,1536]{1,0:T(8,128)(2,1)}, f32[1,6144]{1,0:T(1,128)}, f32[8,1,1152]{2,1,0:T(1,128)}, f32[8,128]{1,0:T(8,128)}) custom-call(bf16[192,1536]{1,0:T(8,128)(2,1)} %pad_maximum_fusion.6.shard, f32[8,1,128]{2,1,0:T(1,128)} %bitcast_convert_fusion.cond_ref, f32[1,1152]{1,0:T(1,128)} %convert_element_type.83.small_ref, ...), custom_call_target="tpu_custom_call" | custom-call | tf_op jit(solution)/shard_map/pallas_call | solution.py:542
  86.2 2.4 slice.92.refs_8_.refs_2_
  88.6 79.5 %shard_map.394 = (bf16[1024,1536]{1,0:T(8,128)(2,1)}, f32[1024,384]{1,0:T(8,128)}, f32[1024,384]{1,0:T(8,128)}, bf16[1024,384]{1,0:T(8,128)(2,1)}, bf16[1024,384...) custom-call(s32[1]{0:T(128)S(6)} %copy.52.refs_0_, ...), custom_call_target="tpu_custom_call" | custom-call | tf_op jit(solution)/shard_map/pallas_call | solution.py:630
  168.1 118.0 %shard_map.395 = (f32[256,384]{1,0:T(8,128)}, bf16[256,384]{1,0:T(8,128)(2,1)}, bf16[256,384]{1,0:T(8,128)(2,1)}, f32[1024,384]{1,0:T(8,128)}, f32[1024,384]{1,0...) custom-call(s32[1]{0:T(128)S(6)} %copy.52.refs_0_, ...), custom_call_target="tpu_custom_call" | custom-call | tf_op jit(solution)/shard_map/pallas_call | solution.py:740
  286.1 8.5 %fusion.12 = f32[1024,1024]{0,1:T(8,128)} fusion(bf16[1024,1536]{1,0:T(8,128)(2,1)} %get-tuple-element.63, bf16[1536,3072]{1,0:T(8,128)(2,1)} %get-tuple-element.62), kind=kOutput, calls=%fused_computation.26 | convolution fusion | flops 3221225472 | bytes 10485760 | tf_op jit(solution)/shard_map/dot_general | solution.py:29
  294.6 5.4 fusion.17
  300.0 8.9 %multiply_convert_fusion = (bf16[1024,1024]{0,1:T(8,128)(2,1)S(1)}, bf16[1024,1024]{0,1:T(8,128)(2,1)}, bf16[1024,1024]{0,1:T(8,128)(2,1)}) fusion(f32[1024,1024]{0,1:T(8,128)} %fusion.12, f32[1024,1024]{0,1:T(8,128)} %fusion.17, bf16[1024,1536]{1,0:T(8,128)(2,1)S(1)} %copy-done.16, bf16[1536,3072]{1,0:T(8,128)(2,1)S(1)} %copy-done.14), kind=kOutput, calls=%fused_computation.16 | convolution fusion | flops 3236954112 | bytes 20971520 | tf_op jit(solution)/shard_map/dot_general | solution.py:29
  309.0 5.1 convolution_convert_fusion.3.refs_24_
  314.1 8.3 %fusion.8.refs_1_ = bf16[1024,1536]{1,0:T(8,128)(2,1)} fusion(bf16[1536,3072]{1,0:T(8,128)(2,1)S(1)} %copy-done.14, bf16[1024,1024]{0,1:T(8,128)(2,1)S(1)} %copy-done.20, bf16[1024,1024]{0,1:T(8,128)(2,1)S(1)} %copy-done.19), kind=kOutput, calls=%fused_computation.21 | convolution fusion | flops 6452412416 | bytes 13631488 | tf_op jit(solution)/shard_map/dot_general | solution.py:33
  322.3 9.9 %convolution_convert_fusion.1 = bf16[1536,2048]{1,0:T(8,128)(2,1)} fusion(bf16[1024,1536]{1,0:T(8,128)(2,1)S(1)} %copy-done.16, bf16[1024,1024]{0,1:T(8,128)(2,1)S(1)} %copy-done.20, bf16[1024,1024]{0,1:T(8,128)(2,1)S(1)} %copy-done.19), kind=kOutput, calls=%fused_computation.5 | convolution fusion | flops 6453985280 | bytes 13631488 | tf_op jit(solution)/shard_map/dot_general | solution.py:37
  332.3 5.6 convolution_convert_fusion.4
  337.9 58.0 %shard_map.396 = (bf16[1024,1536]{1,0:T(8,128)(2,1)}, f32[1024,1536]{1,0:T(8,128)}, f32[8,1536]{1,0:T(8,128)}, f32[192,1024]{1,0:T(8,128)}) custom-call(s32[1]{0:T(128)S(6)} %copy.52.refs_0_, bf16[1024,1536]{1,0:T(8,128)(2,1)} %fusion.8.refs_1_, bf16[1024,1536]{1,0:T(8,128)(2,1)} %refs_1_.5, bf16[1024,1536]{1,0:T(8,128)(2,1)} %get-tuple-element.61.refs_3_, ...), custom_call_target="tpu_custom_call" | custom-call | tf_op jit(solution)/shard_map/pallas_call | solution.py:822
  395.9 101.5 %shard_map.397 = (bf16[1024,1152]{1,0:T(8,128)(2,1)}, bf16[256,768]{1,0:T(8,128)(2,1)}, f32[8,384]{1,0:T(8,128)}, bf16[1024,1536]{1,0:T(8,128)(2,1)}, f32[192,2048]{1,0:T(8,128)}) custom-call(s32[1]{0:T(128)S(6)} %copy.52.refs_0_, bf16[1024,1536]{1,0:T(8,128)(2,1)} %get-tuple-element.64.refs_1_, bf16[1536,384]{1,0:T(8,128)(2,1)} %slice.92.refs_8_.refs_2_, ...), custom_call_target="tpu_custom_call" | custom-call | tf_op jit(solution)/shard_map/pallas_call | solution.py:971
  497.4 8.8 %convolution_convert_fusion.5.refs_0_ = bf16[1024,1536]{1,0:T(8,128)(2,1)} fusion(bf16[1024,1152]{1,0:T(8,128)(2,1)} %get-tuple-element.77, bf16[1536,1536]{1,0:T(8,128)(2,1)} %get-tuple-element.57.refs_2_), kind=kOutput, calls=%fused_computation.24 | convolution fusion | flops 3625451520 | bytes 9043968 | tf_op jit(solution)/shard_map/dot_general | solution.py:33
  506.3 5.1 fusion
  513.9 6.0 convolution_convert_fusion
  521.3 2.5 pad_maximum_fusion
  523.9 6.8 copy.46
  532.8 4.4 fusion.6
  537.3 8.7 %copy.45 = bf16[4096,768]{1,0:T(8,128)(2,1)} copy(bf16[4096,768]{0,1:T(8,128)(2,1)} %fusion.6) | data formatting | bytes 12582912 | tf_op jit(solution)/shard_map/convert_element_type | solution.py:1200
  545.9 156.2 %shard_map.398 = (bf16[1024,1536]{1,0:T(8,128)(2,1)}, f32[8,1,10496]{2,1,0:T(1,128)}, f32[512,768]{1,0:T(8,128)}, f32[192,1536]{1,0:T(8,128)}) custom-call(bf16[1024,1536]{1,0:T(8,128)(2,1)} %convolution_convert_fusion.5.refs_0_, bf16[1024,1536]{1,0:T(8,128)(2,1)} %refs_1_.5, f32[1024,1536]{1,0:T(8,128)} %get-tuple-element.78.refs_2_, ...), custom_call_target="tpu_custom_call" | custom-call | tf_op jit(solution)/shard_map/pallas_call | solution.py:1060
  706.9 2.3 slice_bitcast_fusion
  710.4 4.3 fusion.21
  (89 shorter events, 32.8 us)
Async XLA Ops:
  286.1 8.5 %copy-start.1 = (bf16[1024,1536]{1,0:T(8,128)(2,1)S(1)}, bf16[1024,1536]{1,0:T(8,128)(2,1)}, u32[]{:S(2)}) copy-start(bf16[1024,1536]{1,0:T(8,128)(2,1)} %refs_4_.2) | copy-start | bytes 9437188
  286.1 8.5 %copy-start.14 = (bf16[1536,3072]{1,0:T(8,128)(2,1)S(1)}, bf16[1536,3072]{1,0:T(8,128)(2,1)}, u32[]{:S(2)}) copy-start(bf16[1536,3072]{1,0:T(8,128)(2,1)} %get-tuple-element.62) | copy-start | bytes 28311556
  294.6 5.4 copy-start.16
  309.0 5.1 copy-start.19
  309.0 5.1 copy-start.20
  497.4 8.8 %copy-start = (bf16[1024,1536]{1,0:T(8,128)(2,1)S(1)}, bf16[1024,1536]{1,0:T(8,128)(2,1)}, u32[]{:S(2)}) copy-start(bf16[1024,1536]{1,0:T(8,128)(2,1)} %refs_1_.5) | copy-start | bytes 9437188
  497.4 8.8 %copy-start.2 = (bf16[1024,1536]{1,0:T(8,128)(2,1)S(1)}, bf16[1024,1536]{1,0:T(8,128)(2,1)}, u32[]{:S(2)}) copy-start(bf16[1024,1536]{1,0:T(8,128)(2,1)} %refs_4_.2) | copy-start | bytes 9437188
  497.4 8.8 %copy-start.3 = (bf16[1024,1536]{1,0:T(8,128)(2,1)S(1)}, bf16[1024,1536]{1,0:T(8,128)(2,1)}, u32[]{:S(2)}) copy-start(bf16[1024,1536]{1,0:T(8,128)(2,1)} %get-tuple-element.61.refs_3_) | copy-start | bytes 9437188
  497.4 8.8 %copy-start.7 = (bf16[1024,1536]{1,0:T(8,128)(2,1)S(1)}, bf16[1024,1536]{1,0:T(8,128)(2,1)}, u32[]{:S(2)}) copy-start(bf16[1024,1536]{1,0:T(8,128)(2,1)} %get-tuple-element.76) | copy-start | bytes 9437188
  506.2 5.1 copy-start.13
  506.2 5.3 copy-start.18
  506.3 7.6 %copy-start.15 = (bf16[1024,1536]{1,0:T(8,128)(2,1)S(1)}, bf16[1024,1536]{1,0:T(8,128)(2,1)}, u32[]{:S(2)}) copy-start(bf16[1024,1536]{1,0:T(8,128)(2,1)} %get-tuple-element.82) | copy-start | bytes 9437188
  513.9 6.0 copy-start.5
  513.9 6.0 copy-start.17
  523.9 6.8 copy-start.8
  530.6 2.2 copy-start.4
  530.6 2.2 copy-start.11
  702.1 7.0 copy-start.9
  703.5 6.9 copy-start.12
  709.2 5.6 copy-start.6
  714.7 1.7 copy-start.10

commit v3 on v2

--- a/solution.py
+++ b/solution.py
@@ -107,7 +107,7 @@
         self.up_s, self.up_r, self.dn_s, self.dn_r, self.y_s, self.y_r, self.own_s = sems
         self.me = lax.axis_index("dp")
         self.z, self.y = self.me // 2, lax.rem(self.me, 2)
-        self.ticks = blocks.count + LINE - 2
+        self.ticks, self.done = blocks.count + LINE - 2, 0
 
     @staticmethod
     def scratch(count):
@@ -197,7 +197,7 @@
         self.y_s, self.y_r, self.own_s, self.up_s, self.up_r, self.dn_s, self.dn_r = sems
         self.me = lax.axis_index("dp")
         self.z, self.y = self.me // 2, lax.rem(self.me, 2)
-        self.ticks = blocks.count + LINE - 1
+        self.ticks, self.done = blocks.count + LINE - 1, 0
 
     @staticmethod
     def scratch(blocks):
@@ -304,7 +304,7 @@
 
 
 class Idle:
-    ticks = 0
+    ticks = done = 0
 
     def start(self):
         pass
@@ -317,7 +317,7 @@
 
 
 class TpSum:
-    def __init__(self, partial, out, bufs, sems):
+    def __init__(self, partial, out, bufs, sems, own_sems=None):
         self.p, self.out = partial, out
         self.crossed, self.other = bufs
         self.c_s, self.c_r, self.x_s, self.x_r, self.o_s, self.o_r = sems
@@ -325,6 +325,7 @@
         self.beside, self.far = tp_peers()
         self.half = partial.shape[0] // 2
         self.rows = self.half // TP_PARTS
+        self.own_s = own_sems
 
     @staticmethod
     def scratch(rows, wide):
@@ -353,13 +354,23 @@
         here = self.out.at[self.spot(k, which)]
         return remote(here, here, self.o_s.at[k], self.o_r.at[k], tp=self.beside)
 
+    def load(self, k):
+        mine = self.spot(k, self.core)
+        return pltpu.make_async_copy(self.p.at[mine], self.out.at[mine], self.own_s.at[k])
+
     def stage_one(self, k):
         self.first(k).start()
+        if self.own_s is not None:
+            self.load(k).start()
 
     def stage_two(self, k):
         self.first(k).wait_recv()
         mine = self.spot(k, self.core)
-        add_rows(self.out.at[mine], self.p.at[mine], self.crossed.at[self.part(k)])
+        held = self.p.at[mine]
+        if self.own_s is not None:
+            self.load(k).wait()
+            held = self.out.at[mine]
+        add_rows(self.out.at[mine], held, self.crossed.at[self.part(k)])
         self.second(k).start()
 
     def stage_three(self, k):
@@ -464,48 +475,67 @@
     return pl.ds(pl.multiple_of(block * rows, rows), rows)
 
 
-def paced(count, step, pumps, base, engine):
-    if pumps == 0 or engine.ticks == 0:
-        loop(count, step)
-        return base
-    if pumps <= count:
-        every = count // pumps
-
-        def body(i):
-            step(i)
-            pl.when(lax.rem(i, every) == every - 1)(lambda: engine.pump(base + lax.div(i, every)))
-
-    else:
-        each = pumps // count
-
-        def body(i):
-            step(i)
-            for j in range(each):
-                engine.pump(base + i * each + j)
+def paced(count, step, *plans):
+    jobs = []
+    for engine, pumps in plans:
+        pumps = min(pumps, engine.ticks - engine.done)
+        if pumps > 0:
+            jobs.append((engine, pumps, engine.done))
+            engine.done += pumps
+
+    def body(i):
+        step(i)
+        for engine, pumps, base in jobs:
+            if pumps <= count:
+                every = count // pumps
+                turn = lax.div(i, every)
+                now = (lax.rem(i, every) == every - 1) & (turn < pumps)
+                pl.when(now)(functools.partial(engine.pump, base + turn))
+            else:
+                each = -(-pumps // count)
+                for j in range(each):
+                    pl.when(i * each + j < pumps)(functools.partial(engine.pump, base + i * each + j))
 
     loop(count, body)
-    return base + pumps
-
-
-def finish_pumps(base, engine):
+
+
+def finish_pumps(engine):
+    base = engine.done
     if base < engine.ticks:
         loop(engine.ticks - base, lambda i: engine.pump(base + i))
-
-
-def first_kernel(blocks, shard, cond_ref, small_ref, ada_ref, full, mod_ref, smalls_ref, act_ref, *refs):
-    conds, part, parts, c_s, c_r, m_s, m_r, p_s, p_r = refs[:9]
-    engine = Gather(blocks, shard, full, refs[9:])
-    me = lax.axis_index("dp")
-    peers = dp_peers()
+    engine.done = engine.ticks
+
+
+def first_kernel(blocks, *refs):
+    shard, cond_ref, small_ref, ada_ref, text_ref, w_tk, w_tv = refs[:7]
+    full, mod_ref, smalls_ref, act_ref, text_all, products = refs[7:13]
+    conds, part, parts, c_s, c_r, m_s, m_r, p_s, p_r, t_s, t_r, q_s, q_r, own_s = refs[13:27]
+    engine = Gather(blocks, shard, full, refs[27:])
+    me, tp = lax.axis_index("dp"), lax.axis_index("tp")
+    peers, (beside, far) = dp_peers(), tp_peers()
     sources = [lax.rem(me + GRID - step, GRID) for step in range(1, GRID)]
-    greet(peers, [])
+    depth = text_all.shape[2]
+    share = text_all.shape[1] // 4
+    greet(peers, [beside, far])
     engine.start()
+
+    def quarter(which):
+        rows = pl.ds(pl.multiple_of(which * share, 16), share)
+        return text_all.at[:, rows, :]
+
+    def slab(there, origin):
+        rows = pl.ds(pl.multiple_of(tp * share, 16), share)
+        return text_ref.at[rows, pl.ds(pl.multiple_of(there * depth, 128), depth)], text_all.at[origin, rows, :]
+
     for i, there in enumerate(peers):
         remote(cond_ref.at[there], conds.at[me], c_s.at[i], c_r.at[i], dp=there).start()
         remote(small_ref, smalls_ref.at[me], m_s.at[i], m_r.at[i], dp=there).start()
+    for i, there in enumerate(peers):
+        remote(*slab(there, me), t_s.at[i], t_r.at[i], dp=there).start()
+    own = pltpu.make_async_copy(*slab(me, me), own_s)
+    own.start()
     conds[pl.ds(me, 1)] = cond_ref[pl.ds(me, 1)]
     smalls_ref[pl.ds(me, 1)] = small_ref[...][None]
-    engine.pump(0)
     for i, here in enumerate(sources):
         remote(conds.at[here], conds.at[here], c_s.at[i], c_r.at[i], dp=me).wait_recv()
     cond = jnp.concatenate([conds[i] for i in range(GRID)], axis=0)
@@ -520,25 +550,55 @@
     for i, there in enumerate(peers):
         remote(part.at[there], parts.at[me], p_s.at[i], p_r.at[i], dp=there).start()
     parts[pl.ds(me, 1)] = part[pl.ds(me, 1)]
-    engine.pump(1)
-    engine.pump(2)
+    paced(1, lambda i: None, (engine, 1))
+    own.wait()
+    for i, here in enumerate(sources):
+        remote(*slab(here, here), t_s.at[i], t_r.at[i], dp=me).wait_recv()
+    mine = quarter(tp)
+    to_beside = remote(mine, mine, q_s.at[0], q_r.at[0], tp=beside)
+    to_far = remote(mine, mine, q_s.at[1], q_r.at[1], tp=far)
+    to_beside.start()
+    to_far.start()
+    paced(2, lambda i: None, (engine, 2))
+    from_far = quarter(lax.rem(tp + 2, 4))
+    remote(from_far, from_far, q_s.at[1], q_r.at[1], tp=far).wait_recv()
+    passed = remote(from_far, from_far, q_s.at[2], q_r.at[2], tp=beside)
+    passed.start()
     for i, here in enumerate(sources):
         remote(parts.at[here], parts.at[here], p_s.at[i], p_r.at[i], dp=me).wait_recv()
     mod_ref[...] = sum(parts[i] for i in range(GRID))
-    finish_pumps(3, engine)
+    paced(1, lambda i: None, (engine, 1))
+    from_beside = quarter(tp + 1 - 2 * lax.rem(tp, 2))
+    remote(from_beside, from_beside, q_s.at[0], q_r.at[0], tp=beside).wait_recv()
+    remote(from_beside, from_beside, q_s.at[2], q_r.at[2], tp=beside).wait_recv()
+    wide = w_tk.shape[1]
+
+    def multiply(i):
+        rows = text_all[i]
+        line, y = lax.div(i, 2), lax.rem(i, 2)
+        products[line, y, :, :wide] = dot_nn(rows, w_tk[...]).astype(BF16)
+        products[line, y, :, wide:] = dot_nn(rows, w_tv[...]).astype(BF16)
+
+    paced(GRID, multiply, (engine, 4))
+    finish_pumps(engine)
     engine.drain()
+    to_beside.wait_send()
+    to_far.wait_send()
+    passed.wait_send()
     for i, there in enumerate(peers):
         here = sources[i]
         remote(small_ref, smalls_ref.at[here], m_s.at[i], m_r.at[i], dp=me).wait_recv()
         remote(cond_ref.at[there], conds.at[me], c_s.at[i], c_r.at[i], dp=there).wait_send()
         remote(small_ref, smalls_ref.at[me], m_s.at[i], m_r.at[i], dp=there).wait_send()
+        remote(*slab(there, me), t_s.at[i], t_r.at[i], dp=there).wait_send()
         remote(part.at[there], parts.at[me], p_s.at[i], p_r.at[i], dp=there).wait_send()
 
 
-def gather_first(shard, cond, small, w_ada):
+def gather_first(shard, cond, small, w_ada, text, w_tk, w_tv):
     depth, wide = shard.shape
     blocks = Blocks(depth, wide, 96, 384)
     mods = w_ada.shape[1]
+    rows_t, slab, cols = text.shape[0], w_tk.shape[0], w_tk.shape[1]
     return pl.pallas_call(
         functools.partial(first_kernel, blocks),
         out_shape=[
@@ -546,32 +606,46 @@
             shaped((1, mods), F32),
             shaped((GRID,) + small.shape, F32),
             shaped((GRID, cond.shape[2]), F32),
+            shaped((GRID, rows_t, slab), BF16),
+            shaped((LINE, 2, rows_t, 2 * cols), BF16),
         ],
-        in_specs=[ANY] + [IN_VMEM] * 3,
-        out_specs=[ANY] + [IN_VMEM] * 3,
+        in_specs=[ANY] + [IN_VMEM] * 3 + [ANY] + [IN_VMEM] * 2,
+        out_specs=[ANY] + [IN_VMEM] * 5,
         scratch_shapes=[
             pltpu.VMEM((GRID, 1, cond.shape[2]), F32),
             pltpu.VMEM((GRID, 1, mods), F32),
             pltpu.VMEM((GRID, 1, mods), F32),
         ]
-        + [DMA((GRID - 1,))] * 6
+        + [DMA((GRID - 1,))] * 8
+        + [DMA((3,))] * 2
+        + [DMA]
         + Gather.scratch(blocks.count),
         compiler_params=params(0),
-    )(shard, cond, small, w_ada)
-
-
-def self_kernel(blocks, *refs):
-    frames, tok, weights, mult, qgain, kgain, cos_ref, sa_ref, sb_ref, seg_ref, shard = refs[:11]
-    h_one, q_pre, k_pre, q_rot, k_rot, q_text, v_out, self_o, inv_l, full = refs[11:21]
-    vaug, refs = refs[21], refs[22:]
-    engine = Idle()
+    )(shard, cond, small, w_ada, text, w_tk, w_tv)
+
+
+def forward_kernel(blocks_t, blocks, *refs):
+    frames, tok, weights, mult, qgain, kgain, kygain, cos_ref, sa_ref, sb_ref, seg_ref = refs[:11]
+    gate, tanh_attn, mult_two, products, shard = refs[11:16]
+    h_one, q_pre, k_pre, q_rot, k_rot, q_text, v_out, self_o, inv_l = refs[16:25]
+    ky_pre, kyr, vy_out, text_o, inv_lt, mixed, attn_sum, h_two, full = refs[25:34]
+    vaug, vyaug, partial, ty = refs[34:38]
+    sums = TpSum(partial, attn_sum, refs[38:40], refs[40:46])
+    text_engine, engine = Idle(), Idle()
     if blocks is not None:
-        engine = Gather(blocks, shard, full, refs)
-        greet(dp_peers(), [])
+        text_engine = Scatter(blocks_t, products, ty, refs[46:50], refs[50:57])
+        engine = Gather(blocks, shard, full, refs[57:64])
+        greet(dp_peers(), tp_peers())
+        text_engine.start()
         engine.start()
+    else:
+        greet([], tp_peers())
+        ty = products
     cols = q_pre.shape[1]
     rows = tok.shape[0]
     step_rows = 256
+    blocks_here = rows // step_rows
+    pairs = cols // PAIR
 
     def project(i):
         here = block_rows(i, step_rows)
@@ -592,191 +666,197 @@
         v = dot_nn(h, weights[:, 2 * cols : 3 * cols]).astype(BF16)
         v_out[here, :] = v
         live = live_rows(frames, i * step_rows, step_rows, PAIR).astype(BF16)
-        for pair in range(cols // PAIR):
+        for pair in range(pairs):
             vaug[here, 2 * pair * PAIR : (2 * pair + 1) * PAIR] = v[:, pair * PAIR : (pair + 1) * PAIR] * live
             vaug[here, (2 * pair + 1) * PAIR : (2 * pair + 2) * PAIR] = live
 
+    def attention(q_ref, k_ref, v_ref, inv_ref):
+        def step(i):
+            pair, block = lax.div(i, blocks_here), lax.rem(i, blocks_here)
+            here, lanes = block_rows(block, step_rows), pair_lanes(pair)
+            q = q_ref[here, lanes]
+            keys = k_ref[:, lanes]
+            values = v_ref[:, pair_lanes(pair, 2 * PAIR)]
+            outs = jnp.zeros((step_rows, PAIR), F32)
+            total = jnp.zeros((step_rows, PAIR), F32)
+            for head in range(2):
+                p = jnp.exp(dot_nt(q * half_mask(step_rows, head, BF16), keys)).astype(BF16)
+                both = dot_nn(p, values)
+                wide_mask = half_mask(step_rows, head, F32)
+                outs = outs + both[:, :PAIR] * wide_mask
+                total = total + both[:, PAIR:] * wide_mask
+            inverse = 1.0 / total
+            inv_ref[here, lanes] = inverse
+            return here, lanes, outs * inverse
+
+        return step
+
+    self_attention = attention(q_rot, k_rot, vaug, inv_l)
+    text_attention = attention(q_text, kyr, vyaug, inv_lt)
+
     def attend(i):
-        pair, block = lax.div(i, rows // step_rows), lax.rem(i, rows // step_rows)
-        here, lanes = block_rows(block, step_rows), pair_lanes(pair)
-        q = q_rot[here, lanes]
-        keys = k_rot[:, lanes]
-        values = vaug[:, pair_lanes(pair, 2 * PAIR)]
-        outs = jnp.zeros((step_rows, PAIR), F32)
-        sums = jnp.zeros((step_rows, PAIR), F32)
-        for head in range(2):
-            mask = half_mask(step_rows, head, BF16)
-            p = jnp.exp(dot_nt(q * mask, keys)).astype(BF16)
-            both = dot_nn(p, values)
-            wide_mask = half_mask(step_rows, head, F32)
-            outs = outs + both[:, :PAIR] * wide_mask
-            sums = sums + both[:, PAIR:] * wide_mask
-        inverse = 1.0 / sums
-        inv_l[here, lanes] = inverse
-        self_o[here, lanes] = outs * inverse
-
-    base = paced(rows // step_rows, project, 4, 0, engine)
-    base = paced(cols // PAIR * (rows // step_rows), attend, 6, base, engine)
-    finish_pumps(base, engine)
-    engine.drain()
-
-
-def self_forward(clips, frames, tokens, full_attn, mult, qgain, kgain, tables, seg, text_shard):
-    rows, wide = tokens.shape
-    cols = qgain.shape[1]
-    depth, text_wide = text_shard.shape
-    blocks = Blocks(depth, text_wide, 64, text_wide) if clips == GRID else None
-    f, b = shaped((rows, cols), F32), shaped((rows, cols), BF16)
-    return pl.pallas_call(
-        functools.partial(self_kernel, blocks),
-        out_shape=[shaped((rows, wide), BF16), f, f, b, b, b, b, f, f, shaped((GRID * depth, text_wide), BF16)],
-        in_specs=[IN_SMEM] + [IN_VMEM] * 9 + [ANY],
-        out_specs=[IN_VMEM] * 9 + [ANY],
-        scratch_shapes=[pltpu.VMEM((rows, 2 * cols), BF16)]
-        + (Gather.scratch(blocks.count) if blocks is not None else []),
-        compiler_params=params(1) if blocks is not None else pltpu.CompilerParams(vmem_limit_bytes=VMEM_LIMIT),
-    )(frames, tokens, full_attn, mult, qgain, kgain, *tables, seg, text_shard)
-
-
-def text_kernel(blocks, *refs):
-    frames, text, w_text, kygain, seg_ref, q_text, self_o, gate, weights, tok, tanh_attn, mult, shard = refs[:13]
-    ky_pre, kyr, vy_out, text_o, inv_lt, mixed, attn_sum, h_two, full = refs[13:22]
-    vaug, partial = refs[22:24]
-    sums = TpSum(partial, attn_sum, refs[24:26], refs[26:32])
-    engine = Idle()
-    if blocks is not None:
-        engine = Gather(blocks, shard, full, refs[32:])
-        greet(dp_peers(), tp_peers())
-        engine.start()
-    else:
-        greet([], tp_peers())
-    cols, rows = self_o.shape[1], tok.shape[0]
-    step_rows = 256
-    rows_t = text.shape[0]
-
-    ky = dot_nn(text[...], w_text[:, :cols])
+        here, lanes, out = self_attention(i)
+        mixed_self[here, lanes] = out
+        self_o[here, lanes] = out.astype(BF16)
+
+    def attend_text(i):
+        here, lanes, out = text_attention(i)
+        text_o[here, lanes] = out.astype(BF16)
+        mixed[here, lanes] = (mixed_self[here, lanes] + gate[:, lanes] * out).astype(BF16)
+
+    mixed_self = refs[-1]
+    paced(blocks_here, project, (text_engine, 6))
+    paced(pairs * blocks_here, attend, (text_engine, 12), (engine, 2))
+    finish_pumps(text_engine)
+
+    ky = ty[:, :cols]
     ky_pre[...] = ky
     kyr[...] = (ky * head_inverse(ky, seg_ref[...]) * kygain[...]).astype(BF16)
-    engine.pump(0)
-    vy = dot_nn(text[...], w_text[:, cols:]).astype(BF16)
+    vy = ty[:, cols:].astype(BF16)
     vy_out[...] = vy
-    for pair in range(cols // PAIR):
-        vaug[:, 2 * pair * PAIR : (2 * pair + 1) * PAIR] = vy[:, pair * PAIR : (pair + 1) * PAIR]
-        vaug[:, (2 * pair + 1) * PAIR : (2 * pair + 2) * PAIR] = jnp.ones((rows_t, PAIR), BF16)
-    engine.pump(1)
-
-    def attend(i):
-        pair, block = lax.div(i, rows // step_rows), lax.rem(i, rows // step_rows)
-        here, lanes = block_rows(block, step_rows), pair_lanes(pair)
-        q = q_text[here, lanes]
-        keys = kyr[:, lanes]
-        values = vaug[:, pair_lanes(pair, 2 * PAIR)]
-        outs = jnp.zeros((step_rows, PAIR), F32)
-        total = jnp.zeros((step_rows, PAIR), F32)
-        for head in range(2):
-            p = jnp.exp(dot_nt(q * half_mask(step_rows, head, BF16), keys)).astype(BF16)
-            both = dot_nn(p, values)
-            wide_mask = half_mask(step_rows, head, F32)
-            outs = outs + both[:, :PAIR] * wide_mask
-            total = total + both[:, PAIR:] * wide_mask
-        inverse = 1.0 / total
-        inv_lt[here, lanes] = inverse
-        out = outs * inverse
-        text_o[here, lanes] = out
-        mixed[here, lanes] = (self_o[here, lanes] + gate[:, lanes] * out).astype(BF16)
-
-    base = paced(cols // PAIR * (rows // step_rows), attend, 4, 2, engine)
-
-    def project(which):
+    for pair in range(pairs):
+        vyaug[:, 2 * pair * PAIR : (2 * pair + 1) * PAIR] = vy[:, pair * PAIR : (pair + 1) * PAIR]
+        vyaug[:, (2 * pair + 1) * PAIR : (2 * pair + 2) * PAIR] = jnp.ones((vy.shape[0], PAIR), BF16)
+    paced(pairs * blocks_here, attend_text, (engine, 2))
+
+    def output(which):
         def step(i):
-            start = which * sums.half + i * step_rows
-            here = pl.ds(pl.multiple_of(start, 16), step_rows)
-            partial[here, :] = dot_nt(mixed[here, :], weights[...]).astype(BF16)
+            here = pl.ds(pl.multiple_of(which * sums.half + i * step_rows, 16), step_rows)
+            partial[here, :] = dot_nt(mixed[here, :], weights[:, 3 * cols :]).astype(BF16)
 
         return step
 
     parts_each = TP_PARTS // (sums.half // step_rows)
 
-    def project_send(i):
-        project(1 - sums.core)(i)
+    def output_send(i):
+        output(1 - sums.core)(i)
         loop(parts_each, lambda k: sums.stage_one(i * parts_each + k))
 
-    base = paced(sums.half // step_rows, project_send, 2, base, engine)
-    loop(sums.half // step_rows, project(sums.core))
-    loop(TP_PARTS, sums.stage_two)
+    paced(sums.half // step_rows, output_send)
+    paced(sums.half // step_rows, output(sums.core), (engine, 2))
+    paced(TP_PARTS, sums.stage_two, (engine, 2))
 
     def update(k, which):
         here = sums.spot(k, which)
         live = live_rows(frames, which * sums.half + k * sums.rows, sums.rows, tok.shape[1])
         state = tok[here, :].astype(F32) + live * tanh_attn[...] * attn_sum[here, :].astype(F32)
         inverse = lax.rsqrt(jnp.mean(state * state, axis=-1, keepdims=True) + EPS)
-        h_two[here, :] = (state * inverse * mult[...]).astype(BF16)
+        h_two[here, :] = (state * inverse * mult_two[...]).astype(BF16)
 
     def three(k):
         sums.stage_three(k)
         update(k, sums.core)
 
-    base = paced(TP_PARTS, three, 8, base, engine)
+    paced(TP_PARTS, three, (engine, 8))
 
     def four(k):
         sums.stage_four(k)
         update(k, 1 - sums.core)
 
-    base = paced(TP_PARTS, four, 2, base, engine)
-    finish_pumps(base, engine)
+    paced(TP_PARTS, four, (engine, 2))
+    finish_pumps(engine)
     sums.drain()
+    text_engine.drain()
     engine.drain()
 
 
-def text_forward(
-    clips, frames, text, full_text, kygain, seg, q_text, self_o, gate, w_out, tokens, tanh_attn, mult, ffn_shard
-):
+def forward(clips, frames, tokens, full_attn, mult, gain_rows, tables, seg, gate, tanh_attn, mult_two, products, ffn_shard):
     rows, wide = tokens.shape
-    rows_t = text.shape[0]
-    cols = kygain.shape[1]
+    cols = gate.shape[1]
+    rows_t = products.shape[-2]
     depth, ffn_wide = ffn_shard.shape
-    blocks = Blocks(depth, ffn_wide, 96, 384) if clips == GRID else None
+    grid = clips == GRID
+    blocks_t = Blocks(rows_t, 2 * cols, 32, 2 * cols) if grid else None
+    blocks = Blocks(depth, ffn_wide, 96, 384) if grid else None
     f, b = shaped((rows, cols), F32), shaped((rows, cols), BF16)
+    bt = shaped((rows_t, cols), BF16)
     return pl.pallas_call(
-        functools.partial(text_kernel, blocks),
+        functools.partial(forward_kernel, blocks_t, blocks),
         out_shape=[
+            shaped((rows, wide), BF16),
+            f,
+            f,
+            b,
+            b,
+            b,
+            b,
+            b,
+            f,
             shaped((rows_t, cols), F32),
-            shaped((rows_t, cols), BF16),
-            shaped((rows_t, cols), BF16),
-            f,
+            bt,
+            bt,
+            b,
             f,
             b,
             shaped((rows, wide), BF16),
             shaped((rows, wide), BF16),
             shaped((GRID * depth, ffn_wide), BF16),
         ],
-        in_specs=[IN_SMEM] + [IN_VMEM] * 11 + [ANY],
-        out_specs=[IN_VMEM] * 8 + [ANY],
-        scratch_shapes=[pltpu.VMEM((rows_t, 2 * cols), BF16), pltpu.VMEM((rows, wide), BF16)]
+        in_specs=[IN_SMEM] + [IN_VMEM] * 13 + [ANY if grid else IN_VMEM, ANY],
+        out_specs=[IN_VMEM] * 17 + [ANY],
+        scratch_shapes=[
+            pltpu.VMEM((rows, 2 * cols), BF16),
+            pltpu.VMEM((rows_t, 2 * cols), BF16),
+            pltpu.VMEM((rows, wide), BF16),
+            pltpu.VMEM((rows_t, 2 * cols), F32),
+        ]
         + TpSum.scratch(rows, wide)
-        + (Gather.scratch(blocks.count) if blocks is not None else []),
-        compiler_params=params(2),
-    )(frames, text, full_text, kygain, seg, q_text, self_o, gate, w_out, tokens, tanh_attn, mult, ffn_shard)
+        + (Scatter.scratch(blocks_t) + Gather.scratch(blocks.count) if grid else [])
+        + [pltpu.VMEM((rows, cols), F32)],
+        compiler_params=params(1),
+    )(frames, tokens, full_attn, mult, *gain_rows, *tables, seg, gate, tanh_attn, mult_two, products, ffn_shard)
 
 
 def state_kernel(blocks, *refs):
-    frames, partial, tok, attn_sum, cot, tanh_attn, mult, grad = refs[:8]
-    grad_attn, grad_state, colsums, out = refs[8:12]
-    grad_n = refs[12]
-    sums = TpSum(partial, grad_n, refs[13:15], refs[15:21])
+    frames, partial, tok, attn_sum, cot, tanh_attn, mult, h_two, grad_ffn, hid, grad_in, down = refs[:12]
+    grad_attn, grad_state, colsums, out, g_in, p_ffn = refs[12:18]
+    grad_n, g_down, staged, stage_s, p_staged, p_s = refs[18:24]
+    sums = TpSum(partial, grad_n, refs[24:26], refs[26:32])
     engine = Idle()
     if blocks is not None:
-        engine = Scatter(blocks, grad, out, refs[21:25], refs[25:])
+        engine = Scatter(blocks, g_down, out, refs[32:36], refs[36:])
         greet(dp_peers(), tp_peers())
-        engine.start()
     else:
         greet([], tp_peers())
     loop(TP_PARTS, sums.stage_one)
     colsums[...] = jnp.zeros_like(colsums)
+    wide = tok.shape[1]
+    units = hid.shape[1]
+    step_rows = 256
+    tall = wide // LINE
+
+    def down_block(m):
+        lanes = pl.ds(pl.multiple_of(m * tall, 128), tall)
+        product = dot_tn(grad_ffn[:, lanes], hid[...]).astype(BF16)
+        g_down[m, 0] = product[: tall // 2]
+        g_down[m, 1] = product[tall // 2 :]
+
+    def in_copy(m):
+        return pltpu.make_async_copy(staged.at[lax.rem(m, 2)], g_in.at[m], stage_s.at[lax.rem(m, 2)])
+
+    def in_block(m):
+        lanes = pl.ds(pl.multiple_of(m * tall, 128), tall)
+        pl.when(m >= 2)(lambda: in_copy(m - 2).wait())
+        for half in range(2):
+            cols = slice(half * units, (half + 1) * units)
+            product = dot_tn(h_two[:, lanes], grad_in[:, cols]).astype(BF16)
+            staged[lax.rem(m, 2), 0, :, cols] = product[: tall // 2]
+            staged[lax.rem(m, 2), 1, :, cols] = product[tall // 2 :]
+        in_copy(m).start()
+
+    def p_copy(i):
+        return pltpu.make_async_copy(
+            p_staged.at[lax.rem(i, 2)], p_ffn.at[block_rows(i, step_rows)], p_s.at[lax.rem(i, 2)]
+        )
+
+    def p_block(i):
+        pl.when(i >= 2)(lambda: p_copy(i - 2).wait())
+        p_staged[lax.rem(i, 2)] = dot_nt(hid[block_rows(i, step_rows), :], down[...]).astype(BF16)
+        p_copy(i).start()
 
     def update(k, which):
         here = sums.spot(k, which)
-        live = live_rows(frames, which * sums.half + k * sums.rows, sums.rows, tok.shape[1])
+        live = live_rows(frames, which * sums.half + k * sums.rows, sums.rows, wide)
         added = attn_sum[here, :].astype(F32)
         state = tok[here, :].astype(F32) + live * tanh_attn[...] * added
         inverse = lax.rsqrt(jnp.mean(state * state, axis=-1, keepdims=True) + EPS)
@@ -786,73 +866,89 @@
         g_hat = g * hat
         back = inverse * (scaled - hat * jnp.mean(scaled * hat, axis=-1, keepdims=True))
         total = cot[here, :].astype(F32) + back
-        grad_state[here, :] = total
+        grad_state[here, :] = total.astype(BF16)
         live_total = live * total
         grad_attn[here, :] = (tanh_attn[...] * live_total).astype(BF16)
         colsums[0:1, :] += jnp.sum(g_hat, axis=0, keepdims=True)
         colsums[1:2, :] += jnp.sum(live_total * added, axis=0, keepdims=True)
 
-    base = paced(TP_PARTS, sums.stage_two, 2, 0, engine)
+    loop(2, down_block)
+    loop(TP_PARTS, sums.stage_two)
+    loop(2, lambda m: down_block(m + 2))
+    if blocks is None:
+        out[...] = g_down[...]
+    engine.start()
+    paced(LINE, in_block, (engine, 2))
+    paced(p_ffn.shape[0] // step_rows, p_block, (engine, 1))
 
     def three(k):
         sums.stage_three(k)
         update(k, sums.core)
 
-    base = paced(TP_PARTS, three, 8, base, engine)
+    paced(TP_PARTS, three, (engine, 8))
 
     def four(k):
         sums.stage_four(k)
         update(k, 1 - sums.core)
 
-    base = paced(TP_PARTS, four, 1, base, engine)
-    finish_pumps(base, engine)
+    paced(TP_PARTS, four, (engine, 1))
+    finish_pumps(engine)
+    last_p = p_ffn.shape[0] // step_rows
+    for i in (1, 2):
+        in_copy(LINE - i).wait()
+        p_copy(last_p - i).wait()
     sums.drain()
     engine.drain()
 
 
-def lined(grad):
-    return grad.reshape(LINE, 2, grad.shape[0] // GRID, grad.shape[1])
-
-
-def state_backward(clips, frames, partial, tokens, attn_sum, cotangent, tanh_attn, mult, g_down):
+def state_backward(clips, frames, partial, tokens, attn_sum, cotangent, tanh_attn, mult, h_two, grad_ffn, hid, grad_in, down):
     rows, wide = tokens.shape
-    depth, down_wide = g_down.shape[0] // clips, g_down.shape[1]
-    blocks = Blocks(depth, down_wide, 96, 256) if clips == GRID else None
-    view = lined(g_down) if blocks is not None else g_down
+    units = hid.shape[1]
+    depth = wide // GRID
+    blocks = Blocks(depth, units, 96, 256) if clips == GRID else None
     return pl.pallas_call(
         functools.partial(state_kernel, blocks),
         out_shape=[
             shaped((rows, wide), BF16),
-            shaped((rows, wide), F32),
+            shaped((rows, wide), BF16),
             shaped((8, wide), F32),
-            shaped((depth, down_wide), F32),
+            shaped((depth, units), F32) if clips == GRID else shaped((LINE, 2, depth, units), BF16),
+            shaped((LINE, 2, depth, 2 * units), BF16),
+            shaped((rows, wide), BF16),
         ],
-        in_specs=[IN_SMEM] + [IN_VMEM] * 6 + [ANY],
-        out_specs=[IN_VMEM] * 4,
-        scratch_shapes=[pltpu.VMEM((rows, wide), BF16)]
+        in_specs=[IN_SMEM] + [IN_VMEM] * 11,
+        out_specs=[IN_VMEM] * 4 + [ANY] * 2,
+        scratch_shapes=[
+            pltpu.VMEM((rows, wide), BF16),
+            pltpu.VMEM((LINE, 2, depth, units), BF16),
+            pltpu.VMEM((2, 2, depth, 2 * units), BF16),
+            DMA((2,)),
+            pltpu.VMEM((2, 256, wide), BF16),
+            DMA((2,)),
+        ]
         + TpSum.scratch(rows, wide)
         + (Scatter.scratch(blocks) if blocks is not None else []),
-        compiler_params=params(3),
-    )(frames, partial, tokens, attn_sum, cotangent, tanh_attn, mult, view)
+        compiler_params=params(2),
+    )(frames, partial, tokens, attn_sum, cotangent, tanh_attn, mult, h_two, grad_ffn, hid, grad_in, down)
 
 
 def attn_back_kernel(blocks, *refs):
     (frames, grad_attn, weights, gate, cos_ref, sa_ref, sb_ref, seg_ref, qgain, kgain, kygain) = refs[:11]
     (q_pre, k_pre, q_rot, k_rot, q_text, v_ref, self_o, inv_l) = refs[11:19]
-    (ky_pre, kyr, vy, text_o, inv_lt, partial, grad) = refs[19:26]
-    grad_qkv, grad_text, gains, ffn_sum, out = refs[26:31]
-    do_self, do_text, d_self, d_text, dq_rot, dq_text, dk, dv, dky, dvy, klive = refs[31:42]
-    sums = TpSum(partial, ffn_sum, refs[42:44], refs[44:50])
+    (ky_pre, kyr, vy, text_o, inv_lt, h_one, mixed, partial, grad) = refs[19:28]
+    grad_qkv, grad_text, gains, ffn_sum, out, g_attn = refs[28:34]
+    do_self, do_text, d_self, d_text, dqn, dk, dv, dky, dvy, klive, staged, stage_s = refs[34:46]
+    sums = TpSum(partial, ffn_sum, refs[46:48], refs[48:54], refs[54])
     engine = Idle()
     if blocks is not None:
-        engine = Scatter(blocks, grad, out, refs[50:54], refs[54:])
+        engine = Scatter(blocks, grad, out, refs[55:59], refs[59:])
         greet(dp_peers(), tp_peers())
         engine.start()
     else:
         greet([], tp_peers())
     loop(TP_PARTS, sums.stage_one)
     rows, cols = q_rot.shape
-    rows_t = kyr.shape[0]
+    wide = grad_attn.shape[1]
     step_rows = 256
     blocks_here = rows // step_rows
     pairs = cols // PAIR
@@ -875,20 +971,20 @@
     def start_rows(i):
         here = block_rows(i, step_rows)
         g = dot_nn(grad_attn[here, :], weights[...])
-        other = text_o[here, :]
+        other = text_o[here, :].astype(F32)
         gains[3:4, :] += jnp.sum(g * other, axis=0, keepdims=True)
         first = (g * inv_l[here, :]).astype(BF16)
         do_self[here, :] = first
         second = (g * gate[...] * inv_lt[here, :]).astype(BF16)
         do_text[here, :] = second
-        dot_self = first.astype(F32) * self_o[here, :]
+        dot_self = first.astype(F32) * self_o[here, :].astype(F32)
         dot_text = second.astype(F32) * other
         each = [slice(pair * PAIR, (pair + 1) * PAIR) for pair in range(pairs)]
         d_self[here, :] = sum(halves(dot_self[:, lanes], 2 * pair) for pair, lanes in enumerate(each)).astype(BF16)
         d_text[here, :] = sum(halves(dot_text[:, lanes], 2 * pair) for pair, lanes in enumerate(each)).astype(BF16)
         klive[here, :] = k_rot[here, :] * live_rows(frames, i * step_rows, step_rows, cols).astype(BF16)
 
-    def back(q_ref, k_ref, k_live, v_in, do_ref, d_ref, dq_ref, dk_ref, dv_ref):
+    def back(q_ref, k_ref, k_live, v_in, do_ref, d_ref, dk_ref, dv_ref, turned):
         def step(i):
             pair, block = lax.div(i, blocks_here), lax.rem(i, blocks_here)
             here, lanes = block_rows(block, step_rows), pair_lanes(pair)
@@ -911,25 +1007,29 @@
                 dk_ref[:, lanes] += dot_nn(ds, q)
                 key_mask = half_mask(keys.shape[0], head, BF16)
                 dq = dq + dot_tn(ds, k_live[:, lanes] * key_mask)
-            dq_ref[here, lanes] = dq * SCALE
+            dq = dq * SCALE
+            if turned:
+                dqn[here, lanes] = rope_back(dq, cos_ref[here, :], sa_ref[here, :], sb_ref[here, :])
+            else:
+                dqn[here, lanes] += dq
 
         return step
 
-    base = paced(blocks_here, start_rows, 2, 0, engine)
-    self_back = back(q_rot, k_rot, klive, v_ref, do_self, d_self, dq_rot, dk, dv)
+    paced(blocks_here, start_rows, (engine, 2))
+    self_back = back(q_rot, k_rot, klive, v_ref, do_self, d_self, dk, dv, True)
 
     def self_step(i):
         self_back(i)
         pl.when(i < TP_PARTS)(lambda: sums.stage_two(i))
 
-    base = paced(pairs * blocks_here, self_step, 6, base, engine)
-    text_back = back(q_text, kyr, kyr, vy, do_text, d_text, dq_text, dky, dvy)
+    paced(pairs * blocks_here, self_step, (engine, 4))
+    text_back = back(q_text, kyr, kyr, vy, do_text, d_text, dky, dvy, False)
 
     def text_step(i):
         text_back(i)
         pl.when(i < TP_PARTS)(lambda: sums.stage_three(i))
 
-    base = paced(pairs * blocks_here, text_step, 2, base, engine)
+    paced(pairs * blocks_here, text_step, (engine, 2))
 
     def norm_back(grad_normed, pre, gain, row):
         inverse = head_inverse(pre, seg_ref[...])
@@ -943,17 +1043,35 @@
         here = block_rows(i, step_rows)
         cosines, sine_a, sine_b = thrice(cos_ref[here, :]), thrice(sa_ref[here, :]), thrice(sb_ref[here, :])
         live = live_rows(frames, i * step_rows, step_rows, cols)
-        dqn = rope_back(dq_rot[here, :], cosines, sine_a, sine_b) + dq_text[here, :]
-        grad_qkv[here, :cols] = norm_back(dqn, q_pre[here, :], qgain[...], 0)
+        grad_qkv[here, :cols] = norm_back(dqn[here, :], q_pre[here, :], qgain[...], 0)
         dkn = rope_back(dk[here, :] * live, cosines, sine_a, sine_b)
         grad_qkv[here, cols : 2 * cols] = norm_back(dkn, k_pre[here, :], kgain[...], 1)
         grad_qkv[here, 2 * cols : 3 * cols] = (dv[here, :] * live).astype(BF16)
 
-    base = paced(blocks_here, end_rows, 1, base, engine)
+    paced(blocks_here, end_rows, (engine, 1))
     grad_text[:, :cols] = norm_back(dky[...], ky_pre[...], kygain[...], 2)
     grad_text[:, cols:] = dvy[...].astype(BF16)
-    finish_pumps(base, engine)
+    tall = wide // LINE
+
+    def copy(m):
+        return pltpu.make_async_copy(staged.at[lax.rem(m, 2)], g_attn.at[m], stage_s.at[lax.rem(m, 2)])
+
+    def products(m):
+        lanes = pl.ds(pl.multiple_of(m * tall, 128), tall)
+        pl.when(m >= 2)(lambda: copy(m - 2).wait())
+        first = dot_tn(h_one[:, lanes], grad_qkv[...]).astype(BF16)
+        second = dot_tn(grad_attn[:, lanes], mixed[...]).astype(BF16)
+        for y in range(2):
+            part = slice(y * tall // 2, (y + 1) * tall // 2)
+            staged[lax.rem(m, 2), y, :, : 3 * cols] = first[part]
+            staged[lax.rem(m, 2), y, :, 3 * cols :] = second[part]
+        copy(m).start()
+
+    paced(LINE, products, (engine, 2))
+    finish_pumps(engine)
     loop(TP_PARTS, sums.stage_four)
+    copy(LINE - 2).wait()
+    copy(LINE - 1).wait()
     sums.drain()
     engine.drain()
 
@@ -962,9 +1080,8 @@
     rows, wide = grad_attn.shape
     cols = gate.shape[1]
     rows_t = saved[8].shape[0]
-    depth, in_wide = g_in.shape[0] // clips, g_in.shape[1]
+    depth, in_wide = wide // GRID, g_in.shape[-1]
     blocks = Blocks(depth, in_wide, 192, 256) if clips == GRID else None
-    view = lined(g_in) if blocks is not None else g_in
     f, b = pltpu.VMEM((rows, cols), F32), pltpu.VMEM((rows, cols), BF16)
     ft = pltpu.VMEM((rows_t, cols), F32)
     slim = pltpu.VMEM((rows, PAIR), BF16)
@@ -976,35 +1093,57 @@
             shaped((8, cols), F32),
             shaped((rows, wide), BF16),
             shaped((depth, in_wide), F32),
+            shaped((LINE, 2, depth, 4 * cols), BF16),
         ],
-        in_specs=[IN_SMEM] + [IN_VMEM] * 24 + [ANY],
-        out_specs=[IN_VMEM] * 5,
-        scratch_shapes=[b, b, slim, slim, f, f, f, f, ft, ft, b]
+        in_specs=[IN_SMEM] + [IN_VMEM] * 25 + [ANY] * 2,
+        out_specs=[IN_VMEM] * 5 + [ANY],
+        scratch_shapes=[b, b, slim, slim, f, f, f, ft, ft, b]
+        + [pltpu.VMEM((2, 2, depth, 4 * cols), BF16), DMA((2,))]
         + TpSum.scratch(rows, wide)
+        + [DMA((TP_PARTS,))]
         + (Scatter.scratch(blocks) if blocks is not None else []),
-        compiler_params=params(4),
-    )(frames, grad_attn, w_out, gate, *tables, seg, *gain_rows, *saved, partial, view)
+        compiler_params=params(3),
+    )(frames, grad_attn, w_out, gate, *tables, seg, *gain_rows, *saved, partial, g_in)
 
 
 def last_kernel(blocks_t, blocks_a, *refs):
-    partial, tok, grad_state, mult, gain, lift, vec_in, grad_t, grad_a = refs[:9]
-    grad_tokens, vecs, out_t, out_a = refs[9:13]
-    grad_n, colsum, vec = refs[13:16]
-    sums = TpSum(partial, grad_n, refs[16:18], refs[18:24])
+    grad_qkv, weights, tok, grad_state, mult, gain, lift, vec_in, text_all, grad_text, grad_a = refs[:11]
+    grad_tokens, vecs, g_tk, g_tv, out_a = refs[11:16]
+    partial, grad_n, colsum, vec = refs[16:20]
+    sums = TpSum(partial, grad_n, refs[20:22], refs[22:28])
     me = lax.axis_index("dp")
     text_engine, attn_engine = Idle(), Idle()
     peers = []
     if blocks_t is not None:
-        v_s, v_r = refs[24:26]
+        v_s, v_r, all_text = refs[28:31]
         peers = dp_peers()
-        text_engine = Scatter(blocks_t, grad_t, out_t, refs[26:30], refs[30:37])
-        attn_engine = Scatter(blocks_a, grad_a, out_a, refs[37:41], refs[41:48])
+        text_engine = Gather(blocks_t, grad_text, all_text, refs[31:38])
+        attn_engine = Scatter(blocks_a, grad_a, out_a, refs[38:42], refs[42:49])
         greet(peers, tp_peers())
+        attn_engine.start()
         text_engine.start()
     else:
         greet([], tp_peers())
-    loop(TP_PARTS, sums.stage_one)
     colsum[...] = jnp.zeros_like(colsum)
+    wide = tok.shape[1]
+    cols = grad_qkv.shape[1] // 3
+    step_rows = 256
+
+    def project(which):
+        def step(i):
+            here = pl.ds(pl.multiple_of(which * sums.half + i * step_rows, 16), step_rows)
+            partial[here, :] = dot_nt(grad_qkv[here, :], weights[:, : 3 * cols]).astype(BF16)
+
+        return step
+
+    parts_each = TP_PARTS // (sums.half // step_rows)
+
+    def project_send(i):
+        project(1 - sums.core)(i)
+        loop(parts_each, lambda k: sums.stage_one(i * parts_each + k))
+
+    paced(sums.half // step_rows, project_send)
+    paced(sums.half // step_rows, project(sums.core), (attn_engine, 1))
 
     def update(k, which):
         here = sums.spot(k, which)
@@ -1014,68 +1153,85 @@
         g = grad_n[here, :].astype(F32)
         scaled = g * mult[...]
         back = inverse * (scaled - hat * jnp.mean(scaled * hat, axis=-1, keepdims=True))
-        grad_tokens[here, :] = (grad_state[here, :] + back).astype(BF16)
+        grad_tokens[here, :] = (grad_state[here, :].astype(F32) + back).astype(BF16)
         colsum[...] += jnp.sum(g * hat, axis=0, keepdims=True)
 
-    base = paced(TP_PARTS, sums.stage_two, 2, 0, text_engine)
+    paced(TP_PARTS, sums.stage_two, (attn_engine, 2))
 
     def three(k):
         sums.stage_three(k)
         update(k, sums.core)
 
-    base = paced(TP_PARTS, three, 8, base, text_engine)
-    finish_pumps(base, text_engine)
-    attn_engine.start()
+    paced(TP_PARTS, three, (attn_engine, 4), (text_engine, 4))
 
     def four(k):
         sums.stage_four(k)
         update(k, 1 - sums.core)
 
-    base = paced(TP_PARTS, four, 4, 0, attn_engine)
+    paced(TP_PARTS, four, (attn_engine, 2), (text_engine, 2))
     vec[...] = vec_in[...]
-    wide = tok.shape[1]
     vec[:, :wide] = colsum[...] * gain[...]
     vec[:, 4 * wide : 5 * wide] = colsum[...] * lift[...]
     for i, there in enumerate(peers):
         remote(vec, vecs.at[me], v_s.at[i], v_r.at[i], dp=there).start()
-    finish_pumps(base, attn_engine)
+    finish_pumps(text_engine)
+    finish_pumps(attn_engine)
+    text_engine.drain()
+    if blocks_t is not None:
+        rows_t = grad_text.shape[0]
+        total_k = jnp.zeros(g_tk.shape, F32)
+        total_v = jnp.zeros(g_tv.shape, F32)
+        for clip in range(GRID):
+            here = slice(clip * rows_t, (clip + 1) * rows_t)
+            total_k = total_k + dot_tn(text_all[clip], all_text[here, :cols])
+            total_v = total_v + dot_tn(text_all[clip], all_text[here, cols:])
+        g_tk[...] = total_k
+        g_tv[...] = total_v
     vecs[pl.ds(me if peers else 0, 1)] = vec[...][None]
     for i, there in enumerate(peers):
         here = lax.rem(me + GRID - 1 - i, GRID)
         remote(vec, vecs.at[here], v_s.at[i], v_r.at[i], dp=me).wait_recv()
         remote(vec, vecs.at[me], v_s.at[i], v_r.at[i], dp=there).wait_send()
     sums.drain()
-    text_engine.drain()
     attn_engine.drain()
 
 
-def last_backward(clips, partial, tokens, grad_state, mult, gain, lift, vec, g_text, g_attn):
+def last_backward(clips, grad_qkv, full_attn, tokens, grad_state, mult, gain, lift, vec, text_all, grad_text, g_attn):
     rows, wide = tokens.shape
     grid = clips == GRID
-    depth_t, wide_t = g_text.shape[0] // clips, g_text.shape[1]
-    depth_a, wide_a = g_attn.shape[0] // clips, g_attn.shape[1]
-    blocks_t = Blocks(depth_t, wide_t, 64, wide_t) if grid else None
+    rows_t, cols2 = grad_text.shape
+    depth_a, wide_a = g_attn.shape[-2:]
+    slab = text_all.shape[-1]
+    blocks_t = Blocks(rows_t, cols2, 64, cols2) if grid else None
     blocks_a = Blocks(depth_a, wide_a, 96, 384) if grid else None
-    views = [lined(g_text), lined(g_attn)] if grid else [g_text, g_attn]
     return pl.pallas_call(
         functools.partial(last_kernel, blocks_t, blocks_a),
         out_shape=[
             shaped((rows, wide), BF16),
             shaped(((GRID if grid else 1),) + vec.shape, F32),
-            shaped((depth_t, wide_t), F32),
+            shaped((slab, cols2 // 2), F32),
+            shaped((slab, cols2 // 2), F32),
             shaped((depth_a, wide_a), F32),
         ],
-        in_specs=[IN_VMEM] * 7 + [ANY] * 2,
-        out_specs=[IN_VMEM] * 4,
+        in_specs=[IN_VMEM] * 10 + [ANY],
+        out_specs=[IN_VMEM] * 5,
         scratch_shapes=[
+            pltpu.VMEM((rows, wide), BF16),
             pltpu.VMEM((rows, wide), BF16),
             pltpu.VMEM((1, wide), F32),
             pltpu.VMEM(vec.shape, F32),
         ]
         + TpSum.scratch(rows, wide)
-        + ([DMA((GRID - 1,))] * 2 + Scatter.scratch(blocks_t) + Scatter.scratch(blocks_a) if grid else []),
-        compiler_params=params(5),
-    )(partial, tokens, grad_state, mult, gain, lift, vec, *views)
+        + (
+            [DMA((GRID - 1,))] * 2
+            + [pltpu.VMEM((GRID * rows_t, cols2), BF16)]
+            + Gather.scratch(blocks_t.count)
+            + Scatter.scratch(blocks_a)
+            if grid
+            else []
+        ),
+        compiler_params=params(4),
+    )(grad_qkv, full_attn, tokens, grad_state, mult, gain, lift, vec, text_all, grad_text, g_attn)
 
 
 def gather_plain(shard):
@@ -1086,11 +1242,13 @@
     return lax.psum_scatter(grad, "dp", scatter_dimension=0, tiled=True).astype(F32)
 
 
-def first_plain(shard, cond, small, w_ada):
+def first_plain(shard, cond, small, w_ada, text, w_tk, w_tv):
     act = jax.nn.silu(lax.all_to_all(cond[:, 0], "dp", 0, 0, tiled=True)).astype(BF16)
     parts = dot_nn(act, w_ada)
     mod = lax.psum_scatter(parts, "dp", scatter_dimension=0, tiled=True)
-    return gather_plain(shard), mod, lax.all_gather(small, "dp", axis=0), act.astype(F32)
+    full_text = gather_plain(jnp.concatenate([w_tk, w_tv], axis=1))
+    smalls = lax.all_gather(small, "dp", axis=0)
+    return gather_plain(shard), mod, smalls, act.astype(F32), text[:1, :128], dot_nn(text, full_text)
 
 
 def on_device(
@@ -1126,10 +1284,11 @@
     small = jnp.concatenate([ada_bias, norm_one, norm_two]).astype(F32)[None, :]
     cond_rows = cond.astype(F32).reshape(clips, 1, -1)
     attn_shard = jnp.concatenate([w_query, w_key, w_value, w_out.T], axis=1)
-    text_shard = jnp.concatenate([w_text_key, w_text_value], axis=1)
     ffn_shard = jnp.concatenate([w_gate, w_up, w_down.T], axis=1)
     first = gather_first if grid else first_plain
-    full_attn, mod_sum, smalls, act_rows = first(attn_shard, cond_rows, small, w_ada)
+    full_attn, mod_sum, smalls, act_rows, text_all, products = first(
+        attn_shard, cond_rows, small, w_ada, text, w_text_key, w_text_value
+    )
     modulation = mod_sum[0] + smalls[:, 0, :bias_rows].reshape(-1)
     gain_one = smalls[:, 0, bias_rows : bias_rows + gain_rows].reshape(-1)
     gain_two = smalls[:, 0, bias_rows + gain_rows :].reshape(-1)
@@ -1145,25 +1304,20 @@
     tables, seg = rope_tables(rows), segment_ones(cols)
     out_turned = full_attn[:, 3 * cols :]
 
-    h_one, q_pre, k_pre, q_rot, k_rot, q_text, values, self_o, inv_l, full_text = self_forward(
-        clips, frames, tokens, full_attn, mult_one, qgain, kgain, tables, seg, text_shard
-    )
-    if not grid:
-        full_text = gather_plain(text_shard)
-    ky_pre, kyr, vy, text_o, inv_lt, mixed, attn_sum, h_two, full_ffn = text_forward(
+    gain_set = (qgain, kgain, kygain)
+    (h_one, *saved, mixed, attn_sum, h_two, full_ffn) = forward(
         clips,
         frames,
-        text,
-        full_text,
-        kygain,
+        tokens,
+        full_attn,
+        mult_one,
+        gain_set,
+        tables,
         seg,
-        q_text,
-        self_o,
         gate_wide,
-        out_turned,
-        tokens,
         tanh_attn[None, :],
         mult_two,
+        products,
         ffn_shard,
     )
     if not grid:
@@ -1179,29 +1333,42 @@
     grad_result = cotangent.astype(F32)
     grad_ffn = (live * tanh_ffn * grad_result).astype(BF16)
     grad_hidden = dot_nn(grad_ffn, down_turned)
-    g_down = dot_tn(grad_ffn, hidden_units).astype(BF16)
     grad_gate_pre = (grad_hidden * up_pre * logistic * (1.0 + gate_pre * (1.0 - logistic))).astype(BF16)
     grad_up_pre = (grad_hidden * swish).astype(BF16)
     grad_in = jnp.concatenate([grad_gate_pre, grad_up_pre], axis=1)
     partial_two = dot_nt(grad_in, full_ffn[:, : 2 * units]).astype(BF16)
-    grad_attn, grad_state, sums_two, s_down = state_backward(
-        clips, frames, partial_two, tokens, attn_sum, cotangent, tanh_attn[None, :], mult_two, g_down
+    grad_attn, grad_state, sums_two, s_down, g_in, partial_ffn = state_backward(
+        clips,
+        frames,
+        partial_two,
+        tokens,
+        attn_sum,
+        cotangent,
+        tanh_attn[None, :],
+        mult_two,
+        h_two,
+        grad_ffn,
+        hidden_units,
+        grad_in,
+        down_turned,
     )
-    g_in = dot_tn(h_two, grad_in).astype(BF16)
-    partial_ffn = dot_nt(hidden_units, down_turned).astype(BF16)
-    saved = (q_pre, k_pre, q_rot, k_rot, q_text, values, self_o, inv_l, ky_pre, kyr, vy, text_o, inv_lt)
-    grad_qkv, grad_text, gains, ffn_sum, s_in = attn_backward(
-        clips, frames, grad_attn, out_turned, gate_wide, tables, seg, (qgain, kgain, kygain), saved, partial_ffn, g_in
+    grad_qkv, grad_text, gains, ffn_sum, s_in, g_attn = attn_backward(
+        clips,
+        frames,
+        grad_attn,
+        out_turned,
+        gate_wide,
+        tables,
+        seg,
+        gain_set,
+        (*saved, h_one, mixed),
+        partial_ffn,
+        g_in,
     )
     ffn_sum = ffn_sum.astype(F32)
     hidden_state = tokens.astype(F32) + live * tanh_attn * attn_sum.astype(F32)
     result = (hidden_state + live * tanh_ffn * ffn_sum).astype(BF16)
     grad_gate_ffn = jnp.sum(live * ffn_sum * grad_result, axis=0) * (1.0 - tanh_ffn * tanh_ffn)
-    g_text = dot_tn(text, grad_text).astype(BF16)
-    g_attn = jnp.concatenate(
-        [dot_tn(h_one, grad_qkv).astype(BF16), dot_tn(grad_attn, mixed).astype(BF16)], axis=1
-    )
-    partial_one = dot_nt(grad_qkv, full_attn[:, : 3 * cols]).astype(BF16)
     g_cross_gate = jnp.sum(gains[3].reshape(heads_here, HEAD), axis=1) * (1.0 - gate_tanh * gate_tanh)
     blank = jnp.zeros((wide,), F32)
     vec = jnp.concatenate(
@@ -1219,11 +1386,24 @@
             jnp.zeros((-heads_here % 128,), F32),
         ]
     )[None, :]
-    grad_tokens, vecs, s_text, s_attn = last_backward(
-        clips, partial_one, tokens, grad_state, mult_one, gain_one[None, :], lift_one[None, :], vec, g_text, g_attn
+    grad_tokens, vecs, s_text_key, s_text_value, s_attn = last_backward(
+        clips,
+        grad_qkv,
+        full_attn,
+        tokens,
+        grad_state,
+        mult_one,
+        gain_one[None, :],
+        lift_one[None, :],
+        vec,
+        text_all,
+        grad_text,
+        g_attn,
     )
     if not grid:
-        s_down, s_in, s_text, s_attn = (scatter_plain(g) for g in (g_down, g_in, g_text, g_attn))
+        s_down, s_in, s_attn = (scatter_plain(g.reshape(wide, -1)) for g in (s_down, g_in, g_attn))
+        s_text = scatter_plain(dot_tn(text, grad_text).astype(BF16))
+        s_text_key, s_text_value = s_text[:, :cols], s_text[:, cols:]
         vecs = lax.all_gather(vecs[0], "dp", axis=0)
     vecs = vecs[:, 0, :]
     mod_wide = 4 * wide
@@ -1247,8 +1427,8 @@
         s_attn[:, cols : 2 * cols],
         s_attn[:, 2 * cols : 3 * cols],
         s_attn[:, 3 * cols :].T,
-        s_text[:, :cols],
-        s_text[:, cols:],
+        s_text_key,
+        s_text_value,
         s_in[:, :units],
         s_in[:, units:],
         s_down.T,

time: 725 us -> 594 us (0.82)
  Pallas kernels: 578 us -> 510 us
  matrix products: 76.7 us -> 31.5 us
  local copies, waits for them, and re-layouts: 42.7 us -> 27.1 us
    pallas_call x1, Pallas kernels: 156 us -> 104 us  [last_backward(): pl.pallas_call(functools.partial(last_kernel, blocks_t, blocks_a), out_sh...]
    pallas_call x2 -> x1, Pallas kernels: 197 us -> 162 us  [forward(): pl.pallas_call(functools.partial(forward_kernel, blocks_t, blocks), out_s...]
    dot_general x5 -> x0, matrix products: 27.4 us -> none  [dot_tn(): lax.dot_general(left, right, (((0,), (0,)), ((), ())), preferred_element_...]
    dot_general x3 -> x1, matrix products: 22.1 us -> 8.05 us  [dot_nt(): lax.dot_general(left, right, (((1,), (1,)), ((), ())), preferred_element_...]
    pallas_call x1, Pallas kernels: 58 us -> 70.9 us  [state_backward(): pl.pallas_call(functools.partial(state_kernel, blocks), out_shape=[shaped...]
    pallas_call x1, Pallas kernels: 64.4 us -> 75 us  [gather_first(): pl.pallas_call(functools.partial(first_kernel, blocks), out_shape=[shaped...]
    convert_element_type x1 -> x0, local copies, waits for them, and re-layouts: 8.66 us -> none  [on_device(): g_text = dot_tn(text, grad_text).astype(BF16)]
where the time goes in v3:
time: 594 us; the launch traced here: 587 us
  Pallas kernels  510 us (86%)
  matrix products  31.5 us (5%)
  local copies, waits for them, and re-layouts  27.1 us (5%)
  other arithmetic  16.3 us (3%)
    pallas_call x1, Pallas kernels, forward(): pl.pallas_call(functools.partial(forward_kernel, blocks_t, blocks), out_s...  162 us
    pallas_call x1, Pallas kernels, last_backward(): pl.pallas_call(functools.partial(last_kernel, blocks_t, blocks_a), out_sh...  104 us
    pallas_call x1, Pallas kernels, attn_backward(): pl.pallas_call(functools.partial(attn_back_kernel, blocks), out_shape=[sh...  98.8 us
    pallas_call x1, Pallas kernels, gather_first(): pl.pallas_call(functools.partial(first_kernel, blocks), out_shape=[shaped...  75 us
    pallas_call x1, Pallas kernels, state_backward(): pl.pallas_call(functools.partial(state_kernel, blocks), out_shape=[shaped...  70.9 us
    dot_general x3, matrix products, dot_nn(): return jnp.dot(left, right, preferred_element_type=F32)  19.1 us

profile of v3, /device:TPU:0, one launch (start us, length us, event | category | flops | bytes accessed | tf_op | source)
XLA Modules:
  0.0 586.5 jit_solution(1951749879081457117)
XLA Ops:
  0.7 2.1 pad_maximum_fusion.2.refs_0_
  5.5 1.3 bitcast_convert_fusion.refs_1_
  6.8 75.0 %shard_map.393 = (bf16[1536,1536]{1,0:T(8,128)(2,1)}, f32[1,6144]{1,0:T(1,128)}, f32[8,1,1152]{2,1,0:T(1,128)}, f32[8,128]{1,0:T(8,128)}, bf16[8,256,512]{2,1,0:...) custom-call(bf16[192,1536]{1,0:T(8,128)(2,1)} %pad_maximum_fusion.2.refs_0_, f32[8,1,128]{2,1,0:T(1,128)} %bitcast_convert_fusion.refs_1_, ...), custom_call_target="tpu_custom_call" | custom-call | tf_op jit(solution)/shard_map/pallas_call | solution.py:602
  89.2 1.1 pad_maximum_fusion.1.refs_15_
  90.3 161.6 %shard_map.394 = (bf16[1024,1536]{1,0:T(8,128)(2,1)}, f32[1024,384]{1,0:T(8,128)}, f32[1024,384]{1,0:T(8,128)}, bf16[1024,384]{1,0:T(8,128)(2,1)}, bf16[1024,384...) custom-call(s32[1]{0:T(128)S(6)} %copy.62.refs_0_, ...), custom_call_target="tpu_custom_call" | custom-call | tf_op jit(solution)/shard_map/pallas_call | solution.py:773
  251.9 6.4 %fusion.10 = f32[1024,1024]{1,0:T(8,128)S(1)} fusion(bf16[1024,1536]{1,0:T(8,128)(2,1)} %get-tuple-element.66.refs_7_, bf16[1536,3072]{1,0:T(8,128)(2,1)} %get-tuple-element.65), kind=kOutput, calls=%fused_computation.17 | convolution fusion | flops 3221225472 | bytes 10485760 | tf_op jit(solution)/shard_map/dot_general | solution.py:29
  259.2 5.0 fusion.20
  264.2 7.8 %multiply_convert_fusion = (bf16[1024,1024]{1,0:T(8,128)(2,1)}, bf16[1024,1024]{1,0:T(8,128)(2,1)S(1)}, bf16[1024,1024]{1,0:T(8,128)(2,1)S(1)}) fusion(f32[1024,1024]{1,0:T(8,128)S(1)} %fusion.10, f32[1024,1024]{1,0:T(8,128)} %fusion.20, bf16[1024,1536]{1,0:T(8,128)(2,1)S(1)} %copy-done.3, bf16[1536,3072]{1,0:T(8,128)(2,1)S(1)} %copy-done.7), kind=kOutput, calls=%fused_computation.11 | convolution fusion | flops 3236954112 | bytes 20971520 | tf_op jit(solution)/shard_map/dot_general | solution.py:29
  271.9 2.4 pad_maximum_fusion.refs_10_
  274.3 8.0 %fusion.7.refs_1_ = bf16[1024,1536]{1,0:T(8,128)(2,1)} fusion(bf16[1536,3072]{1,0:T(8,128)(2,1)S(1)} %copy-done.7, bf16[1024,1024]{1,0:T(8,128)(2,1)S(1)} %get-tuple-element.111, bf16[1024,1024]{1,0:T(8,128)(2,1)S(1)} %get-tuple-element.110), kind=kOutput, calls=%fused_computation.16 | convolution fusion | flops 6452412416 | bytes 13631488 | tf_op jit(solution)/shard_map/dot_general | solution.py:33
  282.4 2.0 slice.84.refs_11_
  284.4 70.9 %shard_map.395 = (bf16[1024,1536]{1,0:T(8,128)(2,1)}, bf16[1024,1536]{1,0:T(8,128)(2,1)}, f32[8,1536]{1,0:T(8,128)}, f32[192,1024]{1,0:T(8,128)}, bf16[4,2,192,2...) custom-call(s32[1]{0:T(128)S(6)} %copy.62.refs_0_, bf16[1024,1536]{1,0:T(8,128)(2,1)} %fusion.7.refs_1_, ...), custom_call_target="tpu_custom_call" | custom-call | tf_op jit(solution)/shard_map/pallas_call | solution.py:909
  355.3 2.4 slice.88.refs_2_
  357.7 98.8 %shard_map.396 = (bf16[1024,1152]{1,0:T(8,128)(2,1)}, bf16[256,768]{1,0:T(8,128)(2,1)}, f32[8,384]{1,0:T(8,128)}, bf16[1024,1536]{1,0:T(8,128)(2,1)}, f32[192,20...) custom-call(s32[1]{0:T(128)S(6)} %copy.62.refs_0_, bf16[1024,1536]{1,0:T(8,128)(2,1)} %get-tuple-element.67.refs_1_, ...), custom_call_target="tpu_custom_call" | custom-call | tf_op jit(solution)/shard_map/pallas_call | solution.py:1088
  456.5 6.9 %fusion = (f32[1536]{0:T(1024)S(1)}, bf16[1024,1536]{1,0:T(8,128)(2,1)}) fusion(bf16[1024,1536]{1,0:T(8,128)(2,1)} %refs_4_.4, bf16[1024,1536]{1,0:T(8,128)(2,1)} %get-tuple-element.85, f32[1024]{0:T(1024)S(1)} %fusion.18, f32[1536]{0:T(1024)S(1)} %get-tuple-element.129, bf16[1024,1536]{1,0:T(8,128)(2,1)} %get-tuple-element.64.refs_3_, ...), kind=kLoop, calls=%fused_computation.4 | loop fusion | flops 22018560 | bytes 15751168 | tf_op jit(solution)/shard_map/reduce_sum | solution.py:1371
  463.4 0.9 slice_reduce_fusion.2
  466.6 103.6 %shard_map.397 = (bf16[1024,1536]{1,0:T(8,128)(2,1)}, f32[8,1,10496]{2,1,0:T(1,128)}, f32[512,384]{1,0:T(8,128)}, f32[512,384]{1,0:T(8,128)}, f32[192,1536]{1,0:T(8,128)}) custom-call(bf16[1024,1152]{1,0:T(8,128)(2,1)} %get-tuple-element.86.refs_0_, bf16[1536,1536]{1,0:T(8,128)(2,1)} %get-tuple-element.62.refs_2_.refs_1_, bf16[1024,1536]{1,0:T(8,128)(2,1)} %refs_2_.3, ...), custom_call_target="tpu_custom_call" | custom-call | tf_op jit(solution)/shard_map/pallas_call | solution.py:1207
  570.2 1.1 copy.57
  571.3 4.3 fusion.14
  575.6 1.0 slice_bitcast_fusion
  579.3 2.7 fusion.22
  582.0 1.7 copy.63
  583.7 0.9 copy.64
  585.5 0.9 copy.66
  (79 shorter events, 16.1 us)
Async XLA Ops:
  0.7 86.1 %copy-start.19 = (bf16[6]{0:T(256)(128)(2,1)S(1)}, bf16[6]{0:T(256)(128)(2,1)}, u32[]{:S(2)}) copy-start(bf16[6]{0:T(256)(128)(2,1)} %param.46) | copy-start | bytes 40
  0.7 86.8 %copy-start.16 = (bf16[384]{0:T(512)(128)(2,1)S(1)}, bf16[384]{0:T(512)(128)(2,1)}, u32[]{:S(2)}) copy-start(bf16[384]{0:T(512)(128)(2,1)} %param.45) | copy-start | bytes 2308
  0.7 87.4 %copy-start.17 = (bf16[384]{0:T(512)(128)(2,1)S(1)}, bf16[384]{0:T(512)(128)(2,1)}, u32[]{:S(2)}) copy-start(bf16[384]{0:T(512)(128)(2,1)} %param.43) | copy-start | bytes 2308
  0.7 87.9 %copy-start.18 = (bf16[384]{0:T(512)(128)(2,1)S(1)}, bf16[384]{0:T(512)(128)(2,1)}, u32[]{:S(2)}) copy-start(bf16[384]{0:T(512)(128)(2,1)} %param.44) | copy-start | bytes 2308
  0.7 88.5 %copy-start.11 = (bf16[1024,192]{0,1:T(8,128)(2,1)S(1)}, bf16[1024,192]{0,1:T(8,128)(2,1)}, u32[]{:S(2)}) copy-start(bf16[1024,192]{0,1:T(8,128)(2,1)} %param.38) | copy-start | bytes 1179652
  0.7 88.5 %copy-start.12 = (bf16[192,1024]{1,0:T(8,128)(2,1)S(1)}, bf16[192,1024]{1,0:T(8,128)(2,1)}, u32[]{:S(2)}) copy-start(bf16[192,1024]{1,0:T(8,128)(2,1)} %param.37) | copy-start | bytes 1179652
  0.7 88.5 %copy-start.13 = (bf16[192,1024]{1,0:T(8,128)(2,1)S(1)}, bf16[192,1024]{1,0:T(8,128)(2,1)}, u32[]{:S(2)}) copy-start(bf16[192,1024]{1,0:T(8,128)(2,1)} %param.36) | copy-start | bytes 1179652
  251.9 6.4 %copy-start.1 = (bf16[1024,1536]{1,0:T(8,128)(2,1)S(1)}, bf16[1024,1536]{1,0:T(8,128)(2,1)}, u32[]{:S(2)}) copy-start(bf16[1024,1536]{1,0:T(8,128)(2,1)} %refs_4_.4) | copy-start | bytes 9437188
  251.9 7.2 %copy-start.7 = (bf16[1536,3072]{1,0:T(8,128)(2,1)S(1)}, bf16[1536,3072]{1,0:T(8,128)(2,1)}, u32[]{:S(2)}) copy-start(bf16[1536,3072]{1,0:T(8,128)(2,1)} %get-tuple-element.65) | copy-start | bytes 28311556
  259.2 5.0 copy-start.2
  259.2 5.0 copy-start.3
  357.7 98.8 %copy-start = (bf16[1024,1536]{1,0:T(8,128)(2,1)S(1)}, bf16[1024,1536]{1,0:T(8,128)(2,1)}, u32[]{:S(2)}) copy-start(bf16[1024,1536]{1,0:T(8,128)(2,1)} %refs_2_.3) | copy-start | bytes 9437188
  456.5 7.8 %copy-start.15 = (f32[8,384]{1,0:T(8,128)S(1)}, f32[8,384]{1,0:T(8,128)}, u32[]{:S(2)}) copy-start(f32[8,384]{1,0:T(8,128)} %get-tuple-element.89) | copy-start | bytes 36868
  466.6 104.7 %copy-start.14 = (f32[8,128]{1,0:T(8,128)S(1)}, f32[8,128]{1,0:T(8,128)}, u32[]{:S(2)}) copy-start(f32[8,128]{1,0:T(8,128)} %get-tuple-element.99) | copy-start | bytes 12292
  570.2 5.5 copy-start.6
  570.2 6.5 %copy-start.5 = (f32[8,1,10496]{2,1,0:T(1,128)S(1)}, f32[8,1,10496]{2,1,0:T(1,128)}, u32[]{:S(2)}) copy-start(f32[8,1,10496]{2,1,0:T(1,128)} %get-tuple-element.100) | copy-start | bytes 1007620
  575.6 6.4 %copy-start.4 = (bf16[1024,1536]{1,0:T(8,128)(2,1)S(1)}, bf16[1024,1536]{1,0:T(8,128)(2,1)}, u32[]{:S(2)}) copy-start(bf16[1024,1536]{1,0:T(8,128)(2,1)} %get-tuple-element.154) | copy-start | bytes 9437188
  582.0 1.7 copy-start.10
  582.0 2.6 copy-start.9
  583.7 1.8 copy-start.8

commit v4 on v3

v4 whole, which is shorter than its diff:
```python
import functools
import types

import jax
import jax.numpy as jnp
import numpy as np
from jax import lax
from jax.experimental import pallas as pl
from jax.experimental.pallas import tpu as pltpu
from jax.sharding import PartitionSpec as P

HEAD = 64
FRAME_TOK = 64
EPS = 1e-06
ROPE_BASE = 10000.0
SCALE = HEAD**-0.5
MESH = pl.DeviceIdType.MESH
VMEM_LIMIT = 60 * 2**20
GRID = 8
LINE = 4
PAIR = 2 * HEAD
TP_PARTS = 8
AHEAD = 2
LAG = 3
P_1 = 1
P_2 = 0
P_3 = 4
P_4 = 4
O_1 = 2
O_2 = 2
O_3 = 1
O_4 = 1
A_A = 3
A_T = 2
A_S1 = 2
A_S0 = 2
A_S2 = 3
A_P = 2
DMA = pltpu.SemaphoreType.DMA
F32 = jnp.float32
BF16 = jnp.bfloat16


def dot_nn(left, right):
    return jnp.dot(left, right, preferred_element_type=F32)


def dot_nt(left, right):
    return lax.dot_general(left, right, (((1,), (1,)), ((), ())), preferred_element_type=F32)


def dot_tn(left, right):
    return lax.dot_general(left, right, (((0,), (0,)), ((), ())), preferred_element_type=F32)


def remote(src, dst, send, recv, **where):
    return pltpu.make_async_remote_copy(
        src_ref=src, dst_ref=dst, send_sem=send, recv_sem=recv, device_id=where, device_id_type=MESH
    )


def greet(dp_peers, tp_peers):
    barrier = pltpu.get_barrier_semaphore()
    for peer in dp_peers:
        pl.semaphore_signal(barrier, inc=1, device_id={"dp": peer}, device_id_type=MESH)
    for peer in tp_peers:
        pl.semaphore_signal(barrier, inc=1, device_id={"tp": peer}, device_id_type=MESH)
    pl.semaphore_wait(barrier, len(dp_peers) + len(tp_peers))


def dp_peers():
    me = lax.axis_index("dp")
    return [lax.rem(me + step, GRID) for step in range(1, GRID)]


def tp_peers():
    me = lax.axis_index("tp")
    return [me + 1 - 2 * lax.rem(me, 2), lax.rem(me + 2, 4)]


def aligned(value, by):
    return value if isinstance(value, int) else pl.multiple_of(value, by)


def loop(count, step):
    def body(i, carry):
        step(i)
        return carry

    lax.fori_loop(0, count, body, 0)


def add_rows(out_ref, first, *others):
    rows, wide = out_ref.shape
    tall = min(rows, 96 if wide <= 384 else 32)
    plain = len(others) == 1 and out_ref.dtype == BF16

    def step(i):
        here = pl.ds(aligned(i * tall, 16), tall)
        total = first[here, :] if plain else first[here, :].astype(F32)
        for other in others:
            total = total + (other[here, :] if plain else other[here, :].astype(F32))
        out_ref[here, :] = total.astype(out_ref.dtype)

    if rows == tall:
        step(0)
    else:
        loop(rows // tall, step)


class Blocks:
    def __init__(self, depth, wide, rows, cols, first=0):
        self.depth, self.wide, self.rows, self.cols, self.first = depth, wide, rows, cols, first
        self.down = depth // rows
        self.count = self.down * (wide // cols)

    def at(self, c):
        if isinstance(c, int):
            return c % self.down * self.rows, self.first + c // self.down * self.cols
        row = aligned(lax.rem(c, self.down) * self.rows, 16)
        col = aligned(self.first + lax.div(c, self.down) * self.cols, 128)
        return row, col

class Gather:
    def __init__(self, blocks, shard, full, sems, ahead=AHEAD):
        self.b, self.shard, self.full, self.ahead = blocks, shard, full, min(ahead, blocks.count)
        self.z_s, self.z_r, self.y_s, self.y_r, self.own_s = sems
        self.me = lax.axis_index("dp")
        self.z, self.y = self.me // 2, lax.rem(self.me, 2)
        self.lines = [lax.rem(self.z + step, LINE) for step in range(1, LINE)]
        self.ticks, self.done = blocks.count, 0

    @staticmethod
    def scratch(count):
        return [DMA((count, 3))] * 2 + [DMA((count, 4))] * 2 + [DMA((count,))]

    def own(self, c):
        row, col = self.b.at(c)
        return self.shard.at[pl.ds(row, self.b.rows), pl.ds(col, self.b.cols)]

    def place(self, c, origin):
        row, col = self.b.at(c)
        start = pl.multiple_of(origin * self.b.depth + row, 16)
        return self.full.at[pl.ds(start, self.b.rows), pl.ds(col, self.b.cols)]

    def along(self, c, i):
        there = 2 * self.lines[i] + self.y
        return remote(self.own(c), self.place(c, self.me), self.z_s.at[c, i], self.z_r.at[c, i], dp=there)

    def came_along(self, c, i):
        line = lax.rem(self.z + LINE - 1 - i, LINE)
        place = self.place(c, 2 * line + self.y)
        return line, remote(place, place, self.z_s.at[c, i], self.z_r.at[c, i], dp=self.me)

    def across(self, c, line, mine=False):
        origin = 2 * line + self.y
        src = self.own(c) if mine else self.place(c, origin)
        other = self.me + 1 - 2 * self.y
        return remote(src, self.place(c, origin), self.y_s.at[c, line], self.y_r.at[c, line], dp=other)

    def came_across(self, c, line):
        place = self.place(c, 2 * line + 1 - self.y)
        return remote(place, place, self.y_s.at[c, line], self.y_r.at[c, line], dp=self.me)

    def local(self, c):
        return pltpu.make_async_copy(self.own(c), self.place(c, self.me), self.own_s.at[c])

    def begin(self, c):
        for i in range(LINE - 1):
            self.along(c, i).start()
        self.across(c, self.z, True).start()
        self.local(c).start()

    def start(self):
        for c in range(self.ahead):
            self.begin(c)

    def pump(self, t):
        pl.when(t + self.ahead < self.b.count)(lambda: self.begin(t + self.ahead))
        for i in range(LINE - 1):
            line, came = self.came_along(t, i)
            came.wait_recv()
            self.across(t, line).start()

    def arrive(self, first=0, count=None):
        def step(i):
            c = first + i
            for line in range(LINE):
                self.came_across(c, line).wait_recv()
            self.local(c).wait()

        loop(self.b.count if count is None else count, step)

    def drain(self):
        def step(c):
            for line in range(LINE):
                self.across(c, line).wait_send()
            for i in range(LINE - 1):
                self.along(c, i).wait_send()

        loop(self.b.count, step)


class GatherChain:
    def __init__(self, blocks, shard, full, sems, ahead=AHEAD):
        self.b, self.shard, self.full, self.ahead = blocks, shard, full, min(ahead, blocks.count)
        self.up_s, self.up_r, self.dn_s, self.dn_r, self.y_s, self.y_r, self.own_s = sems
        self.me = lax.axis_index("dp")
        self.z, self.y = self.me // 2, lax.rem(self.me, 2)
        self.ticks, self.done = blocks.count + LINE - 2, 0

    @staticmethod
    def scratch(count):
        return [DMA((count, 3))] * 4 + [DMA((count, 4))] * 2 + [DMA((count,))]

    def own(self, c):
        row, col = self.b.at(c)
        return self.shard.at[pl.ds(row, self.b.rows), pl.ds(col, self.b.cols)]

    def place(self, c, origin):
        row, col = self.b.at(c)
        start = pl.multiple_of(origin * self.b.depth + row, 16)
        return self.full.at[pl.ds(start, self.b.rows), pl.ds(col, self.b.cols)]

    def up(self, c, hop):
        origin = self.me - 2 * hop
        src = self.own(c) if hop == 0 else self.place(c, origin)
        return remote(src, self.place(c, origin), self.up_s.at[c, hop], self.up_r.at[c, hop], dp=self.me + 2)

    def down(self, c, hop):
        origin = self.me + 2 * hop
        src = self.own(c) if hop == 0 else self.place(c, origin)
        return remote(src, self.place(c, origin), self.dn_s.at[c, hop], self.dn_r.at[c, hop], dp=self.me - 2)

    def across(self, c, line, mine=False):
        origin = 2 * line + self.y
        src = self.own(c) if mine else self.place(c, origin)
        other = self.me + 1 - 2 * self.y
        return remote(src, self.place(c, origin), self.y_s.at[c, line], self.y_r.at[c, line], dp=other)

    def came(self, c, origin, sems):
        return remote(self.place(c, origin), self.place(c, origin), sems, sems, dp=self.me)

    def local(self, c):
        return pltpu.make_async_copy(self.own(c), self.place(c, self.me), self.own_s.at[c])

    def begin(self, c):
        pl.when(self.z < LINE - 1)(lambda: self.up(c, 0).start())
        pl.when(self.z > 0)(lambda: self.down(c, 0).start())
        self.across(c, self.z, True).start()
        self.local(c).start()

    def start(self):
        for c in range(self.ahead):
            self.begin(c)

    def pump(self, t):
        me, z, count = self.me, self.z, self.b.count
        pl.when(t + self.ahead < count)(lambda: self.begin(t + self.ahead))
        for hop in range(LINE - 1):
            c = t - hop
            valid = (c >= 0) & (c < count)

            @pl.when(valid & (z - 1 - hop >= 0))
            def _():
                self.came(c, me - 2 * (hop + 1), self.up_r.at[c, hop]).wait_recv()
                if hop < LINE - 2:
                    pl.when(z < LINE - 1)(lambda: self.up(c, hop + 1).start())
                self.across(c, z - 1 - hop).start()

            @pl.when(valid & (z + 1 + hop <= LINE - 1))
            def _():
                self.came(c, me + 2 * (hop + 1), self.dn_r.at[c, hop]).wait_recv()
                if hop < LINE - 2:
                    pl.when(z > 0)(lambda: self.down(c, hop + 1).start())
                self.across(c, z + 1 + hop).start()

    def arrive(self, first=0, count=None):
        def step(i):
            c = first + i
            for line in range(LINE):
                self.came(c, 2 * line + 1 - self.y, self.y_r.at[c, line]).wait_recv()
            self.local(c).wait()

        loop(self.b.count if count is None else count, step)

    def drain(self):
        z = self.z

        def step(c):
            for line in range(LINE):
                self.across(c, line).wait_send()
            for hop in range(LINE - 1):
                pl.when((z < LINE - 1) & (z - hop >= 0))(lambda: self.up(c, hop).wait_send())
                pl.when((z > 0) & (z + hop <= LINE - 1))(lambda: self.down(c, hop).wait_send())

        loop(self.b.count, step)


class Scatter:
    def __init__(self, blocks, grad, out, refs, inplace=False, ahead=AHEAD):
        self.b, self.grad, self.out, self.inplace = blocks, grad, out, inplace
        self.ahead = min(ahead, blocks.count)
        self.crossed, self.landed = refs[:2]
        self.y_s, self.y_r, self.own_s, self.z_s, self.z_r = refs[2:7]
        self.held = None if inplace else refs[7]
        self.me = lax.axis_index("dp")
        self.z, self.y = self.me // 2, lax.rem(self.me, 2)
        self.lines = [lax.rem(self.z + step, LINE) for step in range(1, LINE)]
        self.ticks, self.done = blocks.count + LAG, 0

    @staticmethod
    def scratch(blocks, inplace=False):
        shape = (blocks.rows, blocks.cols)
        count = blocks.count
        bufs = [pltpu.VMEM((count, lines) + shape, BF16) for lines in (4, 3)]
        held = [] if inplace else [pltpu.VMEM((count, 4) + shape, BF16)]
        return bufs + [DMA((count,))] * 3 + [DMA((count, 3))] * 2 + held

    def part(self, c, row_y):
        row, col = self.b.at(c)
        return self.grad.at[:, row_y, pl.ds(row, self.b.rows), pl.ds(col, self.b.cols)]

    def hold(self, c, line):
        if not self.inplace:
            return self.held.at[c, line]
        row, col = self.b.at(c)
        return self.grad.at[line, self.y, pl.ds(row, self.b.rows), pl.ds(col, self.b.cols)]

    def across(self, c):
        other = self.me + 1 - 2 * self.y
        return remote(self.part(c, 1 - self.y), self.crossed.at[c], self.y_s.at[c], self.y_r.at[c], dp=other)

    def load(self, c):
        return pltpu.make_async_copy(self.part(c, self.y), self.held.at[c], self.own_s.at[c])

    def along(self, c, i):
        line = self.lines[i]
        return remote(
            self.hold(c, line), self.landed.at[c, i], self.z_s.at[c, i], self.z_r.at[c, i], dp=2 * line + self.y
        )

    def begin(self, c):
        self.across(c).start()
        if not self.inplace:
            self.load(c).start()

    def start(self):
        for c in range(self.ahead):
            self.begin(c)

    def fold(self, c):
        self.across(c).wait_recv()
        if not self.inplace:
            self.load(c).wait()
        for i in (1, 0, 2):
            line = self.lines[i]
            add_rows(self.hold(c, line), self.hold(c, line), self.crossed.at[c, line])
            self.along(c, i).start()

    def finish(self, c):
        row, col = self.b.at(c)
        for i in range(LINE - 1):
            self.along(c, i).wait_recv()
        out_col = aligned(col - self.b.first, 128)
        out = self.out.at[pl.ds(row, self.b.rows), pl.ds(out_col, self.b.cols)]
        landed = [self.landed.at[c, i] for i in range(LINE - 1)]
        add_rows(out, self.hold(c, self.z), self.crossed.at[c, self.z], *landed)

    def pump(self, t):
        pl.when(t + self.ahead < self.b.count)(lambda: self.begin(t + self.ahead))
        pl.when(t < self.b.count)(lambda: self.fold(t))
        pl.when(t >= LAG)(lambda: self.finish(t - LAG))

    def drain(self):
        def step(c):
            self.across(c).wait_send()
            for i in range(LINE - 1):
                self.along(c, i).wait_send()

        loop(self.b.count, step)


class Idle:
    ticks = done = 0

    def start(self):
        pass

    def pump(self, t):
        pass

    def arrive(self):
        pass

    def drain(self):
        pass


class TpSum:
    def __init__(self, partial, out, bufs, sems, own_sems=None):
        self.p, self.out = partial, out
        self.crossed, self.other = bufs
        self.c_s, self.c_r, self.x_s, self.x_r, self.o_s, self.o_r = sems
        self.core = lax.rem(lax.axis_index("tp"), 2)
        self.beside, self.far = tp_peers()
        self.half = partial.shape[0] // 2
        self.rows = self.half // TP_PARTS
        self.own_s = own_sems

    @staticmethod
    def scratch(rows, wide):
        return [pltpu.VMEM((rows // 2, wide), BF16)] * 2 + [DMA((TP_PARTS,))] * 6

    def spot(self, k, which):
        return pl.ds(pl.multiple_of(which * self.half + k * self.rows, 16), self.rows)

    def part(self, k):
        return pl.ds(aligned(k * self.rows, 16), self.rows)

    def first(self, k):
        return remote(
            self.p.at[self.spot(k, 1 - self.core)],
            self.crossed.at[self.part(k)],
            self.c_s.at[k],
            self.c_r.at[k],
            tp=self.beside,
        )

    def second(self, k):
        here = self.out.at[self.spot(k, self.core)]
        return remote(here, self.other.at[self.part(k)], self.x_s.at[k], self.x_r.at[k], tp=self.far)

    def third(self, k, which):
        here = self.out.at[self.spot(k, which)]
        return remote(here, here, self.o_s.at[k], self.o_r.at[k], tp=self.beside)

    def load(self, k):
        mine = self.spot(k, self.core)
        return pltpu.make_async_copy(self.p.at[mine], self.out.at[mine], self.own_s.at[k])

    def stage_one(self, k):
        self.first(k).start()
        if self.own_s is not None:
            self.load(k).start()

    def stage_two(self, k):
        self.first(k).wait_recv()
        mine = self.spot(k, self.core)
        held = self.p.at[mine]
        if self.own_s is not None:
            self.load(k).wait()
            held = self.out.at[mine]
        add_rows(self.out.at[mine], held, self.crossed.at[self.part(k)])
        self.second(k).start()

    def stage_three(self, k):
        self.second(k).wait()
        mine = self.out.at[self.spot(k, self.core)]
        add_rows(mine, mine, self.other.at[self.part(k)])
        self.third(k, self.core).start()

    def stage_four(self, k):
        self.third(k, 1 - self.core).wait_recv()

    def sent(self, k):
        self.third(k, self.core).wait_send()

    def drain(self, sent=False):
        def step(k):
            self.first(k).wait_send()
            if not sent:
                self.sent(k)

        loop(TP_PARTS, step)


def params(number):
    return pltpu.CompilerParams(
        collective_id=number, has_side_effects=True, vmem_limit_bytes=VMEM_LIMIT
    )


def plain_params():
    return pltpu.CompilerParams(vmem_limit_bytes=VMEM_LIMIT)


ANY = pl.BlockSpec(memory_space=pl.ANY)
IN_VMEM = pl.BlockSpec(memory_space=pltpu.VMEM)
IN_SMEM = pl.BlockSpec(memory_space=pltpu.SMEM)


def shaped(shape, dtype):
    return jax.ShapeDtypeStruct(shape, dtype)


def segment_sum(value, seg):
    high = value.astype(BF16)
    low = (value - high.astype(F32)).astype(BF16)
    return dot_nn(high, seg) + dot_nn(low, seg)


def head_inverse(value, seg):
    return lax.rsqrt(segment_sum(value * value, seg) * (1.0 / HEAD) + EPS)


def thrice(table):
    return jnp.concatenate([table] * 3, axis=1)


def rope(value, cosines, sine_a, sine_b):
    wide = value.shape[1]
    ahead = pltpu.roll(value, wide - HEAD // 4, 1)
    behind = pltpu.roll(value, HEAD // 4, 1)
    return value * cosines + ahead * sine_a + behind * sine_b


def rope_back(grad, cosines, sine_a, sine_b):
    wide = grad.shape[1]
    ahead = pltpu.roll(grad * sine_b, wide - HEAD // 4, 1)
    behind = pltpu.roll(grad * sine_a, HEAD // 4, 1)
    return grad * cosines + ahead + behind


def rope_tables(row_count):
    lane = np.arange(PAIR)
    within = lane % HEAD
    quarter = HEAD // 4
    which = within // quarter
    freqs = (ROPE_BASE ** (-(within % quarter).astype(np.float32) / np.float32(quarter))).astype(np.float32)
    row = np.arange(row_count)
    frame, place = (row // FRAME_TOK).astype(np.float32), (row % FRAME_TOK).astype(np.float32)
    position = np.where(which[None, :] < 2, frame[:, None], place[:, None])
    angles = (position * freqs[None, :]).astype(np.float32)
    cosines, sines = np.cos(angles), np.sin(angles)
    even = (which % 2 == 0)[None, :]
    return (
        jnp.asarray(cosines.astype(np.float32)),
        jnp.asarray(np.where(even, -sines, 0.0).astype(np.float32)),
        jnp.asarray(np.where(even, 0.0, sines).astype(np.float32)),
    )


def segment_ones(wide):
    head = np.arange(wide) // HEAD
    return jnp.asarray((head[:, None] == head[None, :]).astype(np.float32)).astype(BF16)


def live_rows(frames_ref, start, rows, wide):
    row = start + lax.broadcasted_iota(jnp.int32, (rows, wide), 0)
    return (row < frames_ref[0] * FRAME_TOK).astype(F32)


def half_mask(rows, head, dtype):
    lane = lax.broadcasted_iota(jnp.int32, (rows, PAIR), 1)
    return ((lane < HEAD) if head == 0 else (lane >= HEAD)).astype(dtype)


def pair_lanes(pair, wide=PAIR):
    return pl.ds(pl.multiple_of(pair * wide, PAIR), wide)


def block_rows(block, rows):
    return pl.ds(pl.multiple_of(block * rows, rows), rows)


def paced(count, step, *plans):
    jobs = []
    for engine, pumps in plans:
        pumps = min(pumps, engine.ticks - engine.done)
        if pumps > 0:
            jobs.append((engine, pumps, engine.done))
            engine.done += pumps

    def body(i):
        step(i)
        for engine, pumps, base in jobs:
            if pumps <= count:
                every = count // pumps
                turn = lax.div(i, every)
                now = (lax.rem(i, every) == every - 1) & (turn < pumps)
                pl.when(now)(functools.partial(engine.pump, base + turn))
            else:
                each = -(-pumps // count)
                for j in range(each):
                    pl.when(i * each + j < pumps)(functools.partial(engine.pump, base + i * each + j))

    loop(count, body)


def finish_pumps(engine):
    base = engine.done
    if base < engine.ticks:
        loop(engine.ticks - base, lambda i: engine.pump(base + i))
    engine.done = engine.ticks


class Named:
    def __init__(self):
        self.ins, self.outs, self.scratch = {}, {}, {}

    def take(self, refs):
        found, at = {}, 0
        for name in (*self.ins, *self.outs):
            found[name] = refs[at]
            at += 1
        for name, item in self.scratch.items():
            many = isinstance(item, list)
            found[name] = refs[at : at + len(item)] if many else refs[at]
            at += len(item) if many else 1
        return types.SimpleNamespace(**found)

    def call(self, kernel, compiler_params):
        flat = []
        for item in self.scratch.values():
            flat += item if isinstance(item, list) else [item]
        results = pl.pallas_call(
            kernel,
            out_shape=[shape for shape, _ in self.outs.values()],
            in_specs=[spec for _, spec in self.ins.values()],
            out_specs=[spec for _, spec in self.outs.values()],
            scratch_shapes=flat,
            compiler_params=compiler_params,
        )(*[value for value, _ in self.ins.values()])
        return types.SimpleNamespace(**dict(zip(self.outs, results)))


class Opening:
    def __init__(self, r):
        self.r = r
        self.me, self.tp = lax.axis_index("dp"), lax.axis_index("tp")
        self.peers, (self.beside, self.far) = dp_peers(), tp_peers()
        self.sources = [lax.rem(self.me + GRID - step, GRID) for step in range(1, GRID)]
        self.share = r.text_all.shape[1] // 4
        self.cond, self.small, self.parts, self.slabs, self.quarters = (r.sems_set[2 * i : 2 * i + 2] for i in range(5))
        self.own_s = r.sems_set[10]

    def send(self, sems, i, src, dst, **where):
        return remote(src, dst, sems[0].at[i], sems[1].at[i], **where)

    def quarter(self, which):
        rows = pl.ds(pl.multiple_of(which * self.share, 16), self.share)
        return self.r.text_all.at[:, rows, :]

    def slab(self, there, origin):
        depth = self.r.text_all.shape[2]
        rows = pl.ds(pl.multiple_of(self.tp * self.share, 16), self.share)
        src = self.r.text.at[rows, pl.ds(pl.multiple_of(there * depth, 128), depth)]
        return src, self.r.text_all.at[origin, rows, :]

    def cond_out(self, i):
        there = self.peers[i]
        return self.send(self.cond, i, self.r.cond.at[there], self.r.conds.at[self.me], dp=there)

    def small_out(self, i):
        return self.send(self.small, i, self.r.small, self.r.smalls.at[self.me], dp=self.peers[i])

    def slab_out(self, i):
        return self.send(self.slabs, i, *self.slab(self.peers[i], self.me), dp=self.peers[i])

    def part_out(self, i):
        there = self.peers[i]
        return self.send(self.parts, i, self.r.part.at[there], self.r.parts.at[self.me], dp=there)

    def came(self, sems, i, ref):
        self.send(sems, i, ref, ref, dp=self.me).wait_recv()

    def begin(self):
        r, me = self.r, self.me
        for i in range(GRID - 1):
            self.cond_out(i).start()
            self.small_out(i).start()
        for i in range(GRID - 1):
            self.slab_out(i).start()
        pltpu.make_async_copy(*self.slab(me, me), self.own_s).start()
        r.conds[pl.ds(me, 1)] = r.cond[pl.ds(me, 1)]
        r.smalls[pl.ds(me, 1)] = r.small[...][None]

    def partial_rows(self):
        r, me = self.r, self.me
        for i, here in enumerate(self.sources):
            self.came(self.cond, i, r.conds.at[here])
        cond = jnp.concatenate([r.conds[i] for i in range(GRID)], axis=0)
        act = (cond * (1.0 / (1.0 + jnp.exp(-cond)))).astype(BF16)
        r.act[...] = act.astype(F32)
        width = r.w_ada.shape[1] // 4
        for i in range(4):
            cols = pl.ds(i * width, width)
            product = dot_nn(act, r.w_ada[:, cols])
            for j in range(GRID):
                r.part[j, :, cols] = product[j : j + 1, :]
        for i in range(GRID - 1):
            self.part_out(i).start()
        r.parts[pl.ds(me, 1)] = r.part[pl.ds(me, 1)]

    def spread(self):
        pltpu.make_async_copy(*self.slab(self.me, self.me), self.own_s).wait()
        for i, here in enumerate(self.sources):
            self.came(self.slabs, i, self.slab(here, here)[1])
        mine = self.quarter(self.tp)
        self.send(self.quarters, 0, mine, mine, tp=self.beside).start()
        self.send(self.quarters, 1, mine, mine, tp=self.far).start()

    def modulate(self):
        r = self.r
        for i, here in enumerate(self.sources):
            self.came(self.parts, i, r.parts.at[here])
            self.came(self.small, i, r.smalls.at[here])
        wide = r.rows.shape[1]
        bias = r.small.shape[1] - 2 * (wide // GRID)
        ends = r.small.shape[1]
        smalls = [r.smalls[i] for i in range(GRID)]
        mods = sum(r.parts[i] for i in range(GRID)) + jnp.concatenate([v[:, :bias] for v in smalls], axis=1)
        gain_one = jnp.concatenate([v[:, bias : bias + wide // GRID] for v in smalls], axis=1)
        gain_two = jnp.concatenate([v[:, bias + wide // GRID : ends] for v in smalls], axis=1)
        lift_one, lift_two = 1.0 + mods[:, :wide], 1.0 + mods[:, 2 * wide : 3 * wide]
        tanh_one, tanh_two = jnp.tanh(mods[:, wide : 2 * wide]), jnp.tanh(mods[:, 3 * wide :])
        values = (gain_one * lift_one, tanh_one, gain_two * lift_two, tanh_two, gain_one, lift_one, gain_two, lift_two)
        for i, value in enumerate(values):
            r.rows[i : i + 1, :] = value

    def pass_on(self):
        from_far = self.quarter(lax.rem(self.tp + 2, 4))
        self.send(self.quarters, 1, from_far, from_far, tp=self.far).wait_recv()
        self.send(self.quarters, 2, from_far, from_far, tp=self.beside).start()

    def collect(self):
        near = self.quarter(self.tp + 1 - 2 * lax.rem(self.tp, 2))
        self.send(self.quarters, 0, near, near, tp=self.beside).wait_recv()
        self.send(self.quarters, 2, near, near, tp=self.beside).wait_recv()

    def multiply(self, i):
        r = self.r
        cols = r.w_tk.shape[1]
        rows = r.text_all[i]
        line, y = lax.div(i, 2), lax.rem(i, 2)
        r.products[line, y, :, :cols] = dot_nn(rows, r.w_tk[...]).astype(BF16)
        r.products[line, y, :, cols:] = dot_nn(rows, r.w_tv[...]).astype(BF16)

    def drain(self):
        mine = self.quarter(self.tp)
        self.send(self.quarters, 0, mine, mine, tp=self.beside).wait_send()
        self.send(self.quarters, 1, mine, mine, tp=self.far).wait_send()
        self.send(self.quarters, 2, mine, mine, tp=self.beside).wait_send()
        for i in range(GRID - 1):
            self.cond_out(i).wait_send()
            self.small_out(i).wait_send()
            self.slab_out(i).wait_send()
            self.part_out(i).wait_send()


def forward_kernel(named, grid, cuts, *refs):
    r = named.take(refs)
    tok, weights, rows_ref, heads_ref = r.tok, r.weights, r.rows, r.heads
    cos_ref, sa_ref, sb_ref, seg_ref = r.cos, r.sa, r.sb, r.seg
    attn_sum, partial, mixed, ty = r.attn_sum, r.partial, r.mixed, r.ty
    sums = TpSum(partial, attn_sum, r.tp_set[:2], r.tp_set[2:8])
    mult, tanh_attn, mult_two = rows_ref.at[0:1], rows_ref.at[1:2], rows_ref.at[2:3]
    qgain, kgain, kygain, gate = (heads_ref.at[i : i + 1] for i in range(4))
    rows, cols = r.q_rot.shape
    step_rows = 256
    blocks_here = rows // step_rows
    pairs = cols // PAIR
    attn_engine = text_engine = engine = Idle()
    if grid:
        opening = Opening(r)
        attn_engine = GatherChain(cuts[0], r.attn_shard, weights, r.attn_set, A_A)
        text_engine = Scatter(cuts[1], r.products, ty, r.text_set, True, ahead=A_P)
        engine = GatherChain(cuts[2], r.ffn_shard, r.full_ffn, r.ffn_set)
        greet(dp_peers(), tp_peers())
        opening.begin()
        attn_engine.start()
        opening.partial_rows()
        paced(1, lambda i: None, (attn_engine, O_1))
        opening.spread()
        paced(1, lambda i: None, (attn_engine, O_2))
        opening.modulate()
        paced(1, lambda i: None, (attn_engine, O_3))
        opening.pass_on()
        paced(1, lambda i: None, (attn_engine, O_4))
        opening.collect()
        paced(GRID, opening.multiply, (attn_engine, 2))
        text_engine.start()
        engine.start()
        finish_pumps(attn_engine)
        attn_engine.arrive()
    else:
        greet([], tp_peers())

    def project(i):
        here = block_rows(i, step_rows)
        x = tok[here, :].astype(F32)
        inverse = lax.rsqrt(jnp.mean(x * x, axis=-1, keepdims=True) + EPS)
        h = (x * inverse * mult[...]).astype(BF16)
        r.h_one[here, :] = h
        cosines, sine_a, sine_b = thrice(cos_ref[here, :]), thrice(sa_ref[here, :]), thrice(sb_ref[here, :])
        q = dot_nn(h, weights[:, :cols])
        r.q_pre[here, :] = q
        qn = q * head_inverse(q, seg_ref[...]) * qgain[...]
        r.q_text[here, :] = (qn * SCALE).astype(BF16)
        r.q_rot[here, :] = (rope(qn, cosines, sine_a, sine_b) * SCALE).astype(BF16)
        k = dot_nn(h, weights[:, cols : 2 * cols])
        r.k_pre[here, :] = k
        kn = k * head_inverse(k, seg_ref[...]) * kgain[...]
        r.k_rot[here, :] = rope(kn, cosines, sine_a, sine_b).astype(BF16)
        v = dot_nn(h, weights[:, 2 * cols : 3 * cols]).astype(BF16)
        r.values[here, :] = v
        live = live_rows(r.frames, i * step_rows, step_rows, PAIR).astype(BF16)
        for pair in range(pairs):
            r.vaug[here, 2 * pair * PAIR : (2 * pair + 1) * PAIR] = v[:, pair * PAIR : (pair + 1) * PAIR] * live
            r.vaug[here, (2 * pair + 1) * PAIR : (2 * pair + 2) * PAIR] = live

    def attention(q_ref, k_ref, v_ref, inv_ref):
        def step(i):
            pair, block = lax.div(i, blocks_here), lax.rem(i, blocks_here)
            here, lanes = block_rows(block, step_rows), pair_lanes(pair)
            q = q_ref[here, lanes]
            keys = k_ref[:, lanes]
            values = v_ref[:, pair_lanes(pair, 2 * PAIR)]
            outs = jnp.zeros((step_rows, PAIR), F32)
            total = jnp.zeros((step_rows, PAIR), F32)
            for head in range(2):
                p = jnp.exp(dot_nt(q * half_mask(step_rows, head, BF16), keys)).astype(BF16)
                both = dot_nn(p, values)
                wide_mask = half_mask(step_rows, head, F32)
                outs = outs + both[:, :PAIR] * wide_mask
                total = total + both[:, PAIR:] * wide_mask
            inverse = 1.0 / total
            inv_ref[here, lanes] = inverse
            return here, lanes, outs * inverse

        return step

    self_attention = attention(r.q_rot, r.k_rot, r.vaug, r.inv_l)
    text_attention = attention(r.q_text, r.kyr, r.vyaug, r.inv_lt)

    def attend(i):
        here, lanes, out = self_attention(i)
        r.mixed_self[here, lanes] = out
        r.self_o[here, lanes] = out.astype(BF16)

    def attend_text(i):
        here, lanes, out = text_attention(i)
        r.text_o[here, lanes] = out.astype(BF16)
        mixed[here, lanes] = (r.mixed_self[here, lanes] + gate[:, lanes] * out).astype(BF16)

    half_blocks = blocks_here // 2
    parts_each = TP_PARTS // half_blocks

    def output(which):
        def step(i):
            block = which * half_blocks + i
            for pair in range(pairs):
                attend_text(pair * blocks_here + block)
            here = block_rows(block, step_rows)
            partial[here, :] = dot_nt(mixed[here, :], weights[:, 3 * cols :]).astype(BF16)

        return step

    def output_send(i):
        output(1 - sums.core)(i)
        loop(parts_each, lambda k: sums.stage_one(i * parts_each + k))

    def output_add(i):
        output(sums.core)(i)
        loop(parts_each, lambda k: sums.stage_two(i * parts_each + k))

    paced(blocks_here, project, (text_engine, 4), (engine, 2))
    paced(pairs * blocks_here, attend, (text_engine, 4), (engine, 3))
    finish_pumps(text_engine)

    ky = ty[:, :cols]
    r.ky_pre[...] = ky
    r.kyr[...] = (ky * head_inverse(ky, seg_ref[...]) * kygain[...]).astype(BF16)
    vy = ty[:, cols:].astype(BF16)
    r.vy[...] = vy
    for pair in range(pairs):
        r.vyaug[:, 2 * pair * PAIR : (2 * pair + 1) * PAIR] = vy[:, pair * PAIR : (pair + 1) * PAIR]
        r.vyaug[:, (2 * pair + 1) * PAIR : (2 * pair + 2) * PAIR] = jnp.ones((vy.shape[0], PAIR), BF16)
    paced(half_blocks, output_send, (engine, 2))
    paced(half_blocks, output_add, (engine, 2))

    def update(k, which):
        here = sums.spot(k, which)
        live = live_rows(r.frames, which * sums.half + k * sums.rows, sums.rows, tok.shape[1])
        state = tok[here, :].astype(F32) + live * tanh_attn[...] * attn_sum[here, :].astype(F32)
        inverse = lax.rsqrt(jnp.mean(state * state, axis=-1, keepdims=True) + EPS)
        r.h_two[here, :] = (state * inverse * mult_two[...]).astype(BF16)

    def three(k):
        sums.stage_three(k)
        update(k, sums.core)

    paced(TP_PARTS, three, (engine, 4))

    def four(k):
        sums.stage_four(k)
        update(k, 1 - sums.core)

    paced(TP_PARTS, four, (engine, 1))
    finish_pumps(engine)
    engine.arrive()
    sums.drain()
    if grid:
        opening.drain()
    attn_engine.drain()
    text_engine.drain()
    engine.drain()


def forward(clips, frames, tokens, heads_table, tables, seg, ffn_shard, start):
    rows, wide = tokens.shape
    cols = heads_table.shape[1]
    grid = clips == GRID
    depth, ffn_wide = ffn_shard.shape
    n = Named()
    n.ins.update(frames=(frames, IN_SMEM), tok=(tokens, IN_VMEM), heads=(heads_table, IN_VMEM))
    n.ins.update(cos=(tables[0], IN_VMEM), sa=(tables[1], IN_VMEM), sb=(tables[2], IN_VMEM), seg=(seg, IN_VMEM))
    cuts = None
    if grid:
        attn_shard, cond, small, w_ada, text, w_tk, w_tv = start
        rows_t, slab = text.shape[0], w_tk.shape[0]
        mods = w_ada.shape[1]
        n.ins.update(attn_shard=(attn_shard, ANY), cond=(cond, IN_VMEM), small=(small, IN_VMEM))
        n.ins.update(w_ada=(w_ada, IN_VMEM), text=(text, ANY), w_tk=(w_tk, IN_VMEM), w_tv=(w_tv, IN_VMEM))
        n.ins.update(ffn_shard=(ffn_shard, ANY))
        cuts = (
            Blocks(*attn_shard.shape, 96, 384),
            Blocks(rows_t, 2 * cols, 32, 2 * cols),
            Blocks(depth, ffn_wide, 96, 384),
        )
    else:
        weights, rows_table, ty = start
        rows_t = ty.shape[0]
        n.ins.update(weights=(weights, IN_VMEM), rows=(rows_table, IN_VMEM), ty=(ty, IN_VMEM))
    f, b = (shaped((rows, cols), F32), IN_VMEM), (shaped((rows, cols), BF16), IN_VMEM)
    ft, bt = (shaped((rows_t, cols), F32), IN_VMEM), (shaped((rows_t, cols), BF16), IN_VMEM)
    whole = (shaped((rows, wide), BF16), IN_VMEM)
    n.outs.update(q_pre=f, k_pre=f, q_rot=b, k_rot=b, q_text=b, values=b, self_o=b, inv_l=f, ky_pre=ft, kyr=bt, vy=bt)
    n.outs.update(text_o=b, inv_lt=f, h_one=whole, mixed=b, attn_sum=whole, h_two=whole)
    n.scratch.update(
        vaug=pltpu.VMEM((rows, 2 * cols), BF16),
        vyaug=pltpu.VMEM((rows_t, 2 * cols), BF16),
        partial=pltpu.VMEM((rows, wide), BF16),
        mixed_self=pltpu.VMEM((rows, cols), F32),
        tp_set=TpSum.scratch(rows, wide),
    )
    if grid:
        n.outs.update(
            weights=(shaped((GRID * attn_shard.shape[0], attn_shard.shape[1]), BF16), IN_VMEM),
            rows=(shaped((8, wide), F32), IN_VMEM),
            act=(shaped((GRID, cond.shape[2]), F32), IN_VMEM),
            text_all=(shaped((GRID, rows_t, slab), BF16), IN_VMEM),
            full_ffn=(shaped((GRID * depth, ffn_wide), BF16), ANY),
        )
        n.scratch.update(
            ty=pltpu.VMEM((rows_t, 2 * cols), F32),
            products=pltpu.VMEM((LINE, 2, rows_t, 2 * cols), BF16),
            smalls=pltpu.VMEM((GRID,) + small.shape, F32),
            conds=pltpu.VMEM((GRID, 1, cond.shape[2]), F32),
            part=pltpu.VMEM((GRID, 1, mods), F32),
            parts=pltpu.VMEM((GRID, 1, mods), F32),
            sems_set=[DMA((GRID - 1,))] * 8 + [DMA((3,))] * 2 + [DMA],
            attn_set=GatherChain.scratch(cuts[0].count),
            text_set=Scatter.scratch(cuts[1], True),
            ffn_set=GatherChain.scratch(cuts[2].count),
        )
    out = n.call(functools.partial(forward_kernel, n, grid, cuts), params(1))
    if not grid:
        out.weights, out.rows, out.text_all = weights, rows_table, jnp.zeros((1, 16, 128), BF16)
    return out


UNITS = 256
ONES = 3


def ffn_kernel(named, cut, cut_back, *refs):
    r = named.take(refs)
    engine, scatter = Idle(), Idle()
    if cut is not None:
        engine = GatherChain(cut, r.shard, r.w_two, r.gather_set)
        scatter = Scatter(cut_back, r.grads, r.out, r.scatter_set)
        greet(dp_peers(), [])
        engine.start()
    rows, wide = r.h_two.shape
    step_rows = 256
    count = rows // step_rows
    tall = wide // LINE
    tanh_two = r.rows[3:4, :]
    ones, twos = r.w_one.shape[1] // (3 * UNITS), r.w_two.shape[1] // (3 * UNITS)

    def start_rows(i):
        here = block_rows(i, step_rows)
        live = live_rows(r.frames, i * step_rows, step_rows, wide)
        r.grad_ffn[here, :] = (live * tanh_two * r.cot[here, :].astype(F32)).astype(BF16)

    def copy(b):
        place = r.grads.at[:, :, :, pl.ds(b * 3 * UNITS, 3 * UNITS)]
        return pltpu.make_async_copy(r.staged.at[b % 2], place, r.stage_s.at[b % 2])

    def block(b):
        w = r.w_one if b < ones else r.w_two
        first = (b if b < ones else b - ones) * 3 * UNITS
        last = b == ones + twos - 1
        dgu = r.dgu_last if last else r.dgu

        def units(i):
            here = block_rows(i, step_rows)
            both = dot_nn(r.h_two[here, :], w[:, first : first + 2 * UNITS])
            gate, up = both[:, :UNITS], both[:, UNITS:]
            back = dot_nn(r.grad_ffn[here, :], w[:, first + 2 * UNITS : first + 3 * UNITS])
            logistic = 1.0 / (1.0 + jnp.exp(-gate))
            swish = gate * logistic
            r.hid[here, b * UNITS : (b + 1) * UNITS] = (swish * up).astype(BF16)
            d_gate = (back * up * logistic * (1.0 + gate * (1.0 - logistic))).astype(BF16)
            d_both = jnp.concatenate([d_gate, (back * swish).astype(BF16)], axis=1)
            dgu[here, :] = d_both
            added = dot_nt(d_both, w[:, first : first + 2 * UNITS])
            if b == 0:
                r.total[here, :] = added
            elif not last:
                r.total[here, :] += added
            else:
                r.partial[here, :] = (r.total[here, :] + added).astype(BF16)

        def products(m):
            lanes = pl.ds(pl.multiple_of(m * tall, 128), tall)
            downs = dot_tn(r.grad_ffn[:, lanes], r.hid[:, b * UNITS : (b + 1) * UNITS]).astype(BF16)
            ins = dot_tn(r.h_two[:, lanes], dgu[...]).astype(BF16)
            for y in range(2):
                part = slice(y * tall // 2, (y + 1) * tall // 2)
                r.staged[b % 2, m, y, :, : 2 * UNITS] = ins[part]
                r.staged[b % 2, m, y, :, 2 * UNITS :] = downs[part]

        pumps = 1 if b < ones else 2
        paced(count, units, (engine, pumps), (scatter, 2 if b > 0 else 0))
        if not last:
            if b >= 2 and (b > 2 or cut is None):
                copy(b - 2).wait()
            paced(LINE, products, (engine, pumps), (scatter, 2 if b > 0 else 0))
            copy(b).start()
        if b == 0 and cut is not None:
            copy(0).wait()
            scatter.start()

    paced(count, start_rows, (engine, 1))
    each = cut.count // twos if cut is not None else 0
    for b in range(ones):
        block(b)
    for b in range(ones, ones + twos):
        if cut is not None:
            need = min(engine.ticks, (b - ones + 1) * each + 2)
            while engine.done < need:
                paced(1, lambda i: None, (engine, 1))
            engine.arrive((b - ones) * each, each)
        block(b)
    copy(ones + twos - 3).wait()
    copy(ones + twos - 2).wait()
    finish_pumps(scatter)
    scatter.drain()
    engine.drain()


def ffn(clips, frames, h_two, cotangent, rows_table, w_one, second):
    rows, wide = h_two.shape
    half_wide = second.shape[1]
    blocks = (w_one.shape[1] + half_wide) // (3 * UNITS)
    grid = clips == GRID
    depth = wide // GRID
    n = Named()
    n.ins.update(frames=(frames, IN_SMEM), h_two=(h_two, IN_VMEM), cot=(cotangent, IN_VMEM), rows=(rows_table, IN_VMEM))
    n.ins.update(w_one=(w_one, IN_VMEM))
    whole = (shaped((rows, wide), BF16), IN_VMEM)
    cut = Blocks(depth, half_wide, 96, 384) if grid else None
    cut_back = None
    if grid:
        n.ins.update(shard=(second, ANY))
        cut_back = Blocks(depth, 3 * UNITS, 96, 256)
        n.outs.update(w_two=(shaped((wide, half_wide), BF16), IN_VMEM), out=(shaped((depth, 3 * UNITS), F32), IN_VMEM))
        n.scratch.update(gather_set=GatherChain.scratch(cut.count), scatter_set=Scatter.scratch(cut_back))
    else:
        n.ins.update(w_two=(second, IN_VMEM))
    n.outs.update(partial=whole, grad_ffn=whole, hid=(shaped((rows, blocks * UNITS), BF16), IN_VMEM))
    n.outs.update(dgu_last=(shaped((rows, 2 * UNITS), BF16), IN_VMEM))
    n.outs.update(grads=(shaped((LINE, 2, depth, (blocks - 1) * 3 * UNITS), BF16), ANY))
    n.scratch.update(
        dgu=pltpu.VMEM((rows, 2 * UNITS), BF16),
        total=pltpu.VMEM((rows, wide), F32),
        staged=pltpu.VMEM((2, LINE, 2, depth, 3 * UNITS), BF16),
        stage_s=DMA((2,)),
    )
    out = n.call(functools.partial(ffn_kernel, n, cut, cut_back), params(5) if grid else plain_params())
    if not grid:
        out.w_two = second
    return out


def state_kernel(named, cut, *refs):
    r = named.take(refs)
    sums = TpSum(r.partial, r.grad_attn, r.tp_set[:2], r.tp_set[2:8], r.tp_set[8])
    tanh_attn, mult = r.rows.at[1:2], r.rows.at[2:3]
    engine = Idle()
    if cut is not None:
        engine = Scatter(cut, r.grads, r.out, r.scatter_set, ahead=A_S0)
        greet(dp_peers(), tp_peers())
        engine.start()
    else:
        greet([], tp_peers())
    loop(TP_PARTS, sums.stage_one)
    rows, wide = r.tok.shape
    step_rows = 256
    tall = wide // LINE
    blocks = r.hid.shape[1] // UNITS
    ones = r.w_one.shape[1] // (3 * UNITS)

    def down_copy(b):
        w = r.w_one if b < ones else r.w_two
        first = (b if b < ones else b - ones) * 3 * UNITS + 2 * UNITS
        place = r.down.at[:, pl.ds(b * UNITS, UNITS)]
        return pltpu.make_async_copy(w.at[:, pl.ds(first, UNITS)], place, r.down_s.at[b])

    for b in range(blocks):
        down_copy(b).start()
    r.colsums[...] = jnp.zeros_like(r.colsums)

    def products(m):
        lanes = pl.ds(pl.multiple_of(m * tall, 128), tall)
        downs = dot_tn(r.grad_ffn[:, lanes], r.hid[:, (blocks - 1) * UNITS :]).astype(BF16)
        ins = dot_tn(r.h_two[:, lanes], r.dgu[...]).astype(BF16)
        for y in range(2):
            part = slice(y * tall // 2, (y + 1) * tall // 2)
            r.g_last[m, y, :, : 2 * UNITS] = ins[part]
            r.g_last[m, y, :, 2 * UNITS :] = downs[part]

    def p_copy(i):
        place = r.p_ffn.at[block_rows(i, step_rows)]
        return pltpu.make_async_copy(r.p_staged.at[lax.rem(i, 2)], place, r.p_s.at[lax.rem(i, 2)])

    def p_block(i):
        pl.when(i >= 2)(lambda: p_copy(i - 2).wait())
        r.p_staged[lax.rem(i, 2)] = dot_nt(r.hid[block_rows(i, step_rows), :], r.down[...]).astype(BF16)
        p_copy(i).start()

    def update(k, which):
        here = sums.spot(k, which)
        live = live_rows(r.frames, which * sums.half + k * sums.rows, sums.rows, wide)
        added = r.attn_sum[here, :].astype(F32)
        state = r.tok[here, :].astype(F32) + live * tanh_attn[...] * added
        inverse = lax.rsqrt(jnp.mean(state * state, axis=-1, keepdims=True) + EPS)
        hat = state * inverse
        g = r.grad_attn[here, :].astype(F32)
        scaled = g * mult[...]
        g_hat = g * hat
        back = inverse * (scaled - hat * jnp.mean(scaled * hat, axis=-1, keepdims=True))
        total = r.cot[here, :].astype(F32) + back
        r.grad_state[here, :] = total.astype(BF16)
        live_total = live * total
        r.grad_attn[here, :] = (tanh_attn[...] * live_total).astype(BF16)
        r.colsums[0:1, :] += jnp.sum(g_hat, axis=0, keepdims=True)
        r.colsums[1:2, :] += jnp.sum(live_total * added, axis=0, keepdims=True)

    paced(TP_PARTS, sums.stage_two, (engine, 2))
    paced(LINE, products, (engine, 2))
    for b in range(blocks):
        down_copy(b).wait()
    paced(rows // step_rows, p_block, (engine, 2))

    def three(k):
        sums.stage_three(k)

        @pl.when(k > 0)
        def _():
            sums.sent(k - 1)
            update(k - 1, sums.core)

    paced(TP_PARTS, three, (engine, 8))
    sums.sent(TP_PARTS - 1)
    update(TP_PARTS - 1, sums.core)

    def four(k):
        sums.stage_four(k)
        update(k, 1 - sums.core)

    paced(TP_PARTS, four, (engine, 2))
    finish_pumps(engine)
    for i in (1, 2):
        p_copy(rows // step_rows - i).wait()
    sums.drain(True)
    engine.drain()


def state_backward(clips, frames, tokens, attn_sum, cotangent, rows_table, h_two, w_one, fed):
    rows, wide = tokens.shape
    grid = clips == GRID
    depth = wide // GRID
    units, scattered = fed.hid.shape[1], fed.grads.shape[-1]
    cut = Blocks(depth, scattered - 3 * UNITS, 96, 256, 3 * UNITS) if grid else None
    n = Named()
    n.ins.update(frames=(frames, IN_SMEM), tok=(tokens, IN_VMEM), attn_sum=(attn_sum, IN_VMEM), cot=(cotangent, IN_VMEM))
    n.ins.update(rows=(rows_table, IN_VMEM), h_two=(h_two, IN_VMEM), grad_ffn=(fed.grad_ffn, IN_VMEM))
    n.ins.update(hid=(fed.hid, IN_VMEM), dgu=(fed.dgu_last, IN_VMEM), w_one=(w_one, ANY), w_two=(fed.w_two, ANY))
    n.ins.update(partial=(fed.partial, ANY))
    whole = shaped((rows, wide), BF16)
    n.outs.update(grad_attn=(whole, IN_VMEM), grad_state=(whole, IN_VMEM), colsums=(shaped((8, wide), F32), IN_VMEM))
    n.outs.update(g_last=(shaped((LINE, 2, depth, 3 * UNITS), BF16), IN_VMEM), p_ffn=(whole, ANY))
    n.scratch.update(
        down=pltpu.VMEM((wide, units), BF16),
        down_s=DMA((units // UNITS,)),
        p_staged=pltpu.VMEM((2, 256, wide), BF16),
        p_s=DMA((2,)),
        tp_set=TpSum.scratch(rows, wide) + [DMA((TP_PARTS,))],
    )
    if grid:
        n.ins.update(grads=(fed.grads, ANY))
        n.outs.update(out=(shaped((depth, scattered - 3 * UNITS), F32), IN_VMEM))
        n.scratch.update(scatter_set=Scatter.scratch(cut))
    return n.call(functools.partial(state_kernel, n, cut), params(2))


def attn_back_kernel(blocks, blocks_t, *refs):
    frames, grad_attn, weights, heads_ref, cos_ref, sa_ref, sb_ref, seg_ref = refs[:8]
    (q_pre, k_pre, q_rot, k_rot, q_text, v_ref, self_o, inv_l) = refs[8:16]
    (ky_pre, kyr, vy, text_o, inv_lt, h_one, mixed, partial, grad) = refs[16:25]
    grad_qkv, grad_text, gains, ffn_sum, out, g_attn, all_text = refs[25:32]
    do_self, do_text, d_self, d_text, dqn, dk, dv, dky, dvy, klive, staged, stage_s = refs[32:44]
    sums = TpSum(partial, ffn_sum, refs[44:46], refs[46:52], refs[52])
    qgain, kgain, kygain, gate = (heads_ref.at[i : i + 1] for i in range(4))
    engine, text_engine = Idle(), Idle()
    if blocks is not None:
        engine = Scatter(blocks, grad, out, refs[53:61], ahead=A_S1)
        text_engine = GatherChain(blocks_t, grad_text, all_text, refs[61:], A_T)
        greet(dp_peers(), tp_peers())
        engine.start()
    else:
        greet([], tp_peers())
    loop(TP_PARTS, sums.stage_one)
    rows, cols = q_rot.shape
    wide = grad_attn.shape[1]
    step_rows = 256
    blocks_here = rows // step_rows
    pairs = cols // PAIR
    gains[...] = jnp.zeros_like(gains)
    dk[...] = jnp.zeros_like(dk)
    dv[...] = jnp.zeros_like(dv)
    dky[...] = jnp.zeros_like(dky)
    dvy[...] = jnp.zeros_like(dvy)

    def halves(value, first_head):
        lane = lax.broadcasted_iota(jnp.int32, (step_rows, PAIR), 1)
        out = jnp.zeros((step_rows, PAIR), F32)
        for head in range(2):
            total = jnp.sum(value * half_mask(step_rows, head, F32), axis=-1, keepdims=True)
            high = total.astype(BF16).astype(F32)
            spot = 2 * (first_head + head)
            out = out + jnp.where(lane == spot, high, jnp.where(lane == spot + 1, total - high, 0.0))
        return out

    def start_rows(i):
        here = block_rows(i, step_rows)
        g = dot_nn(grad_attn[here, :], weights[...])
        other = text_o[here, :].astype(F32)
        gains[3:4, :] += jnp.sum(g * other, axis=0, keepdims=True)
        first = (g * inv_l[here, :]).astype(BF16)
        do_self[here, :] = first
        second = (g * gate[...] * inv_lt[here, :]).astype(BF16)
        do_text[here, :] = second
        dot_self = first.astype(F32) * self_o[here, :].astype(F32)
        dot_text = second.astype(F32) * other
        each = [slice(pair * PAIR, (pair + 1) * PAIR) for pair in range(pairs)]
        d_self[here, :] = sum(halves(dot_self[:, lanes], 2 * pair) for pair, lanes in enumerate(each)).astype(BF16)
        d_text[here, :] = sum(halves(dot_text[:, lanes], 2 * pair) for pair, lanes in enumerate(each)).astype(BF16)
        klive[here, :] = k_rot[here, :] * live_rows(frames, i * step_rows, step_rows, cols).astype(BF16)

    def back(q_ref, k_ref, k_live, v_in, do_ref, d_ref, dk_ref, dv_ref, turned):
        def step(i):
            pair, block = lax.div(i, blocks_here), lax.rem(i, blocks_here)
            here, lanes = block_rows(block, step_rows), pair_lanes(pair)
            keys = k_ref[:, lanes]
            values = v_in[:, lanes]
            lane = lax.broadcasted_iota(jnp.int32, values.shape, 1)
            dq = jnp.zeros((step_rows, PAIR), F32)
            for head in range(2):
                mask = half_mask(step_rows, head, BF16)
                q = q_ref[here, lanes] * mask
                do = do_ref[here, lanes] * mask
                scores = dot_nt(keys, q)
                p = jnp.exp(scores)
                dv_ref[:, lanes] += dot_nn(p.astype(BF16), do)
                spot = 2 * (2 * pair + head)
                minus = jnp.where((lane == spot) | (lane == spot + 1), -1.0, 0.0).astype(BF16)
                left = jnp.concatenate([values, minus], axis=1)
                right = jnp.concatenate([do, d_ref[here, :]], axis=1)
                ds = (p * dot_nt(left, right)).astype(BF16)
                dk_ref[:, lanes] += dot_nn(ds, q)
                key_mask = half_mask(keys.shape[0], head, BF16)
                dq = dq + dot_tn(ds, k_live[:, lanes] * key_mask)
            dq = dq * SCALE
            if turned:
                dqn[here, lanes] += rope_back(dq, cos_ref[here, :], sa_ref[here, :], sb_ref[here, :])
            else:
                dqn[here, lanes] = dq

        return step

    paced(blocks_here, start_rows, (engine, 2))
    def norm_back(grad_normed, pre, gain, row):
        inverse = head_inverse(pre, seg_ref[...])
        hat = pre * inverse
        gains[row : row + 1, :] += jnp.sum(grad_normed * hat, axis=0, keepdims=True)
        scaled = grad_normed * gain
        average = segment_sum(scaled * hat, seg_ref[...]) * (1.0 / HEAD)
        return (inverse * (scaled - hat * average)).astype(BF16)

    def end_rows(i):
        here = block_rows(i, step_rows)
        cosines, sine_a, sine_b = thrice(cos_ref[here, :]), thrice(sa_ref[here, :]), thrice(sb_ref[here, :])
        live = live_rows(frames, i * step_rows, step_rows, cols)
        grad_qkv[here, :cols] = norm_back(dqn[here, :], q_pre[here, :], qgain[...], 0)
        dkn = rope_back(dk[here, :] * live, cosines, sine_a, sine_b)
        grad_qkv[here, cols : 2 * cols] = norm_back(dkn, k_pre[here, :], kgain[...], 1)
        grad_qkv[here, 2 * cols : 3 * cols] = (dv[here, :] * live).astype(BF16)
        for k in range(TP_PARTS // blocks_here):
            sums.stage_three(i * (TP_PARTS // blocks_here) + k)

    text_back = back(q_text, kyr, kyr, vy, do_text, d_text, dky, dvy, False)

    def text_step(i):
        text_back(i)
        pl.when(i < TP_PARTS)(lambda: sums.stage_two(i))

    paced(pairs * blocks_here, text_step, (engine, 3))
    grad_text[:, :cols] = norm_back(dky[...], ky_pre[...], kygain[...], 2)
    grad_text[:, cols:] = dvy[...].astype(BF16)
    text_engine.start()
    self_back = back(q_rot, k_rot, klive, v_ref, do_self, d_self, dk, dv, True)

    half = pairs * blocks_here // 2
    paced(half, self_back, (engine, 6), (text_engine, 2))
    paced(half, lambda i: self_back(i + half), (text_engine, 3))
    paced(blocks_here, end_rows, (text_engine, 2))
    tall = wide // LINE

    def copy(m):
        return pltpu.make_async_copy(staged.at[lax.rem(m, 2)], g_attn.at[m], stage_s.at[lax.rem(m, 2)])

    def products(m):
        lanes = pl.ds(pl.multiple_of(m * tall, 128), tall)
        pl.when(m >= 2)(lambda: copy(m - 2).wait())
        first = dot_tn(h_one[:, lanes], grad_qkv[...]).astype(BF16)
        second = dot_tn(grad_attn[:, lanes], mixed[...]).astype(BF16)
        for y in range(2):
            part = slice(y * tall // 2, (y + 1) * tall // 2)
            staged[lax.rem(m, 2), y, :, : 3 * cols] = first[part]
            staged[lax.rem(m, 2), y, :, 3 * cols :] = second[part]
        copy(m).start()

    paced(LINE, products, (text_engine, 4))
    finish_pumps(engine)
    finish_pumps(text_engine)
    text_engine.arrive()
    loop(TP_PARTS, sums.stage_four)
    copy(LINE - 2).wait()
    copy(LINE - 1).wait()
    sums.drain()
    engine.drain()
    text_engine.drain()


def attn_backward(clips, frames, grad_attn, w_out, heads_table, tables, seg, saved, partial, g_up):
    rows, wide = grad_attn.shape
    cols = heads_table.shape[1]
    rows_t = saved[8].shape[0]
    depth, units = wide // GRID, g_up.shape[-1]
    grid = clips == GRID
    parts = Blocks(depth, units, 96, 256) if grid else None
    blocks_t = Blocks(rows_t, 2 * cols, 32, 2 * cols) if grid else None
    f, b = pltpu.VMEM((rows, cols), F32), pltpu.VMEM((rows, cols), BF16)
    ft = pltpu.VMEM((rows_t, cols), F32)
    slim = pltpu.VMEM((rows, PAIR), BF16)
    return pl.pallas_call(
        functools.partial(attn_back_kernel, parts, blocks_t),
        out_shape=[
            shaped((rows, 3 * cols), BF16),
            shaped((rows_t, 2 * cols), BF16),
            shaped((8, cols), F32),
            shaped((rows, wide), BF16),
            shaped((depth, units), F32),
            shaped((LINE, 2, depth, 4 * cols), BF16),
            shaped((GRID * rows_t, 2 * cols), BF16),
        ],
        in_specs=[IN_SMEM] + [IN_VMEM] * 22 + [ANY] * 2,
        out_specs=[IN_VMEM] * 5 + [ANY] * 2,
        scratch_shapes=[b, b, slim, slim, f, f, f, ft, ft, b]
        + [pltpu.VMEM((2, 2, depth, 4 * cols), BF16), DMA((2,))]
        + TpSum.scratch(rows, wide)
        + [DMA((TP_PARTS,))]
        + (Scatter.scratch(parts) + GatherChain.scratch(blocks_t.count) if grid else []),
        compiler_params=params(3),
    )(frames, grad_attn, w_out, heads_table, *tables, seg, *saved, partial, g_up)


def last_kernel(parts, *refs):
    frames, grad_qkv, weights, tok, grad_state, rows_ref, sums_two, gains = refs[:8]
    ffn_sum, attn_sum, cot, text_all, all_text, grad_a = refs[8:14]
    result, grad_tokens, vecs, g_tk, g_tv, out_a = refs[14:20]
    partial, grad_n, colsum, outsum, vec = refs[20:25]
    sums = TpSum(partial, grad_n, refs[25:27], refs[27:33])
    me = lax.axis_index("dp")
    engine = Idle()
    peers = []
    if parts is not None:
        v_s, v_r = refs[33:35]
        peers = dp_peers()
        engine = Scatter(parts, grad_a, out_a, refs[35:], ahead=A_S2)
        greet(peers, tp_peers())
        engine.start()
    else:
        greet([], tp_peers())
    mult_one, tanh_one, _, tanh_two, gain_one, lift_one, gain_two, lift_two = (rows_ref[i : i + 1, :] for i in range(8))
    colsum[...] = jnp.zeros_like(colsum)
    outsum[...] = jnp.zeros_like(outsum)
    wide = tok.shape[1]
    cols = grad_qkv.shape[1] // 3
    step_rows = 256

    def project(which):
        def step(i):
            here = pl.ds(pl.multiple_of(which * sums.half + i * step_rows, 16), step_rows)
            partial[here, :] = dot_nt(grad_qkv[here, :], weights[:, : 3 * cols]).astype(BF16)

        return step

    parts_each = TP_PARTS // (sums.half // step_rows)

    def project_send(i):
        project(1 - sums.core)(i)
        loop(parts_each, lambda k: sums.stage_one(i * parts_each + k))

    paced(sums.half // step_rows, project_send)
    paced(sums.half // step_rows, project(sums.core), (engine, P_1))
    paced(TP_PARTS, sums.stage_two, (engine, P_2))

    def output(i):
        here = block_rows(i, 64)
        live = live_rows(frames, i * 64, 64, wide)
        added = live * ffn_sum[here, :].astype(F32)
        state = tok[here, :].astype(F32) + live * tanh_one * attn_sum[here, :].astype(F32)
        result[here, :] = (state + tanh_two * added).astype(BF16)
        outsum[...] += jnp.sum(added * cot[here, :].astype(F32), axis=0, keepdims=True)

    paced(tok.shape[0] // 64, output, (engine, P_3))
    if parts is not None:
        rows_t = text_all.shape[1]

        def text_products(i):
            here = block_rows(i, rows_t)
            g_tk[...] += dot_tn(text_all[i], all_text[here, :cols])
            g_tv[...] += dot_tn(text_all[i], all_text[here, cols:])

        g_tk[...] = jnp.zeros_like(g_tk)
        g_tv[...] = jnp.zeros_like(g_tv)
        paced(GRID, text_products, (engine, P_4))

    def update(k, which):
        here = sums.spot(k, which)
        x = tok[here, :].astype(F32)
        inverse = lax.rsqrt(jnp.mean(x * x, axis=-1, keepdims=True) + EPS)
        hat = x * inverse
        g = grad_n[here, :].astype(F32)
        scaled = g * mult_one
        back = inverse * (scaled - hat * jnp.mean(scaled * hat, axis=-1, keepdims=True))
        grad_tokens[here, :] = (grad_state[here, :].astype(F32) + back).astype(BF16)
        colsum[...] += jnp.sum(g * hat, axis=0, keepdims=True)

    def three(k):
        sums.stage_three(k)
        update(k, sums.core)

    paced(TP_PARTS, three, (engine, 4))

    def four(k):
        sums.stage_four(k)
        update(k, 1 - sums.core)

    paced(TP_PARTS, four, (engine, 2))
    pieces = (
        colsum[...] * gain_one,
        sums_two[1:2, :] * (1.0 - tanh_one * tanh_one),
        sums_two[0:1, :] * gain_two,
        outsum[...] * (1.0 - tanh_two * tanh_two),
        colsum[...] * lift_one,
        sums_two[0:1, :] * lift_two,
    )
    for i, piece in enumerate(pieces):
        vec[:, i * wide : (i + 1) * wide] = piece
    for i in range(4):
        vec[:, 6 * wide + i * cols : 6 * wide + (i + 1) * cols] = gains[i : i + 1, :]
    for i, there in enumerate(peers):
        remote(vec, vecs.at[me], v_s.at[i], v_r.at[i], dp=there).start()
    finish_pumps(engine)
    vecs[pl.ds(me if peers else 0, 1)] = vec[...][None]
    for i, there in enumerate(peers):
        here = lax.rem(me + GRID - 1 - i, GRID)
        remote(vec, vecs.at[here], v_s.at[i], v_r.at[i], dp=me).wait_recv()
        remote(vec, vecs.at[me], v_s.at[i], v_r.at[i], dp=there).wait_send()
    sums.drain()
    engine.drain()


def last_backward(
    clips, frames, grad_qkv, full_attn, tokens, grad_state, rows_table, sums_two, gains, ffn_sum, attn_sum, cotangent,
    text_all, all_text, g_attn
):
    rows, wide = tokens.shape
    grid = clips == GRID
    cols = gains.shape[1]
    depth, wide_a = g_attn.shape[-2:]
    slab = text_all.shape[-1]
    parts = Blocks(depth, wide_a, 96, 256) if grid else None
    whole = shaped((rows, wide), BF16)
    vec = (1, 6 * wide + 4 * cols)
    return pl.pallas_call(
        functools.partial(last_kernel, parts),
        out_shape=[
            whole,
            whole,
            shaped(((GRID if grid else 1),) + vec, F32),
            shaped((slab, cols), F32),
            shaped((slab, cols), F32),
            shaped((depth, wide_a), F32),
        ],
        in_specs=[IN_SMEM] + [IN_VMEM] * 12 + [ANY],
        out_specs=[IN_VMEM] * 6,
        scratch_shapes=[
            pltpu.VMEM((rows, wide), BF16),
            pltpu.VMEM((rows, wide), BF16),
            pltpu.VMEM((1, wide), F32),
            pltpu.VMEM((1, wide), F32),
            pltpu.VMEM(vec, F32),
        ]
        + TpSum.scratch(rows, wide)
        + ([DMA((GRID - 1,))] * 2 + Scatter.scratch(parts) if grid else []),
        compiler_params=params(4),
    )(
        frames, grad_qkv, full_attn, tokens, grad_state, rows_table, sums_two, gains, ffn_sum, attn_sum, cotangent,
        text_all, all_text, g_attn
    )


def gather_plain(shard):
    return lax.all_gather(shard, "dp", axis=0, tiled=True)


def scatter_plain(grad):
    return lax.psum_scatter(grad, "dp", scatter_dimension=0, tiled=True).astype(F32)


def first_plain(shard, cond, small, w_ada, text, w_tk, w_tv):
    act = jax.nn.silu(lax.all_to_all(cond[:, 0], "dp", 0, 0, tiled=True)).astype(BF16)
    parts = dot_nn(act, w_ada)
    mods = lax.psum_scatter(parts, "dp", scatter_dimension=0, tiled=True)[0]
    full_text = gather_plain(jnp.concatenate([w_tk, w_tv], axis=1))
    smalls = lax.all_gather(small, "dp", axis=0)[:, 0, :]
    wide = w_ada.shape[1] // 4
    bias, gain = 4 * wide // smalls.shape[0], wide // smalls.shape[0]
    scale_one, gate_one, scale_two, gate_two = jnp.split(mods + smalls[:, :bias].reshape(-1), 4)
    gain_one, gain_two = smalls[:, bias : bias + gain].reshape(-1), smalls[:, bias + gain :].reshape(-1)
    lift_one, lift_two = 1.0 + scale_one, 1.0 + scale_two
    values = (
        gain_one * lift_one,
        jnp.tanh(gate_one),
        gain_two * lift_two,
        jnp.tanh(gate_two),
        gain_one,
        lift_one,
        gain_two,
        lift_two,
    )
    return gather_plain(shard), jnp.stack(values), act.astype(F32), dot_nn(text, full_text)


def on_device(
    tokens,
    text,
    cond,
    frames,
    w_query,
    w_key,
    w_value,
    w_out,
    w_text_key,
    w_text_value,
    w_gate,
    w_up,
    w_down,
    w_ada,
    ada_bias,
    norm_one,
    norm_two,
    query_gain,
    key_gain,
    text_key_gain,
    cross_gate,
    cotangent,
):
    rows, wide = tokens.shape
    clips = lax.axis_size("dp")
    grid = clips == GRID
    cols, units = w_query.shape[1], w_gate.shape[1]
    heads_here = cols // HEAD
    bias_rows, gain_rows = ada_bias.shape[0], norm_one.shape[0]
    small = jnp.concatenate([ada_bias, norm_one, norm_two]).astype(F32)[None, :]
    cond_rows = cond.astype(F32).reshape(clips, 1, -1)
    attn_shard = jnp.concatenate([w_query, w_key, w_value, w_out.T], axis=1)
    turned = w_down.T
    pieces = [
        jnp.concatenate(
            [w[:, b * UNITS : (b + 1) * UNITS] for b in range(*ends) for w in (w_gate, w_up, turned)],
            axis=1,
        )
        for ends in ((0, ONES), (ONES, units // UNITS))
    ]
    opening = (attn_shard, cond_rows, small, w_ada, text, w_text_key, w_text_value)
    if not grid:
        full_attn, rows_table, act_rows, ty = first_plain(*opening)
        opening = (full_attn, rows_table, ty)
    gate_tanh = jnp.tanh(cross_gate.astype(F32))
    blank = jnp.zeros((cols,), F32)
    heads_table = jnp.stack(
        [query_gain.astype(F32), key_gain.astype(F32), text_key_gain.astype(F32), jnp.repeat(gate_tanh, HEAD)]
        + [blank] * 4
    )
    tables, seg = rope_tables(rows), segment_ones(cols)
    passed = forward(clips, frames, tokens, heads_table, tables, seg, pieces[0], opening)
    full_attn, rows_table = passed.weights, passed.rows
    if grid:
        act_rows, half_one, second = passed.act, passed.full_ffn, pieces[1]
    else:
        half_one, second = gather_plain(pieces[0]), gather_plain(pieces[1])
    p = passed
    saved = (p.q_pre, p.k_pre, p.q_rot, p.k_rot, p.q_text, p.values, p.self_o, p.inv_l)
    saved += (p.ky_pre, p.kyr, p.vy, p.text_o, p.inv_lt, p.h_one, p.mixed)
    fed = ffn(clips, frames, p.h_two, cotangent, rows_table, half_one, second)
    state = state_backward(clips, frames, tokens, p.attn_sum, cotangent, rows_table, p.h_two, half_one, fed)
    out_turned = full_attn[:, 3 * cols :]
    grad_qkv, grad_text, gains, ffn_sum, s_last, g_attn, all_text = attn_backward(
        clips, frames, state.grad_attn, out_turned, heads_table, tables, seg, saved, state.p_ffn, state.g_last
    )
    result, grad_tokens, vecs, s_text_key, s_text_value, s_attn = last_backward(
        clips,
        frames,
        grad_qkv,
        full_attn,
        tokens,
        state.grad_state,
        rows_table,
        state.colsums,
        gains,
        ffn_sum,
        p.attn_sum,
        cotangent,
        p.text_all,
        all_text if grid else grad_text,
        g_attn,
    )
    s_blocks = [fed.out, state.out] if grid else [scatter_plain(fed.grads.reshape(wide, -1))]
    if not grid:
        s_last, s_attn = (scatter_plain(g.reshape(wide, -1)) for g in (state.g_last, g_attn))
        s_text = scatter_plain(dot_tn(text, grad_text).astype(BF16))
        s_text_key, s_text_value = s_text[:, :cols], s_text[:, cols:]
        vecs = lax.all_gather(vecs[0], "dp", axis=0)
    s_ffn = [
        jnp.concatenate(
            [
                s[:, at + i * UNITS : at + (i + 1) * UNITS]
                for s in (*s_blocks, s_last)
                for at in range(0, s.shape[1], 3 * UNITS)
            ],
            axis=1,
        )
        for i in range(3)
    ]
    vecs = vecs[:, 0, :]
    mod_wide = 4 * wide
    g_ada = lax.dot_general(
        act_rows,
        vecs[:, :mod_wide],
        (((0,), (0,)), ((), ())),
        precision=lax.Precision.HIGHEST,
        preferred_element_type=F32,
    )
    sums = jnp.sum(vecs, axis=0)
    me = lax.axis_index("dp")
    g_bias = lax.dynamic_slice(sums, (me * bias_rows,), (bias_rows,))
    g_norm_one = lax.dynamic_slice(sums, (mod_wide + me * gain_rows,), (gain_rows,))
    g_norm_two = lax.dynamic_slice(sums, (mod_wide + wide + me * gain_rows,), (gain_rows,))
    rest = sums[mod_wide + 2 * wide :]
    g_cross_gate = jnp.sum(rest[3 * cols :].reshape(heads_here, HEAD), axis=1) * (1.0 - gate_tanh * gate_tanh)
    return (
        result,
        grad_tokens,
        s_attn[:, :cols],
        s_attn[:, cols : 2 * cols],
        s_attn[:, 2 * cols : 3 * cols],
        s_attn[:, 3 * cols :].T,
        s_text_key,
        s_text_value,
        s_ffn[0],
        s_ffn[1],
        s_ffn[2].T,
        g_ada,
        g_bias,
        g_norm_one,
        g_norm_two,
        rest[:cols],
        rest[cols : 2 * cols],
        rest[2 * cols : 3 * cols],
        g_cross_gate,
    )


def solution(mesh):
    placed = (
        P("dp", None),
        P("dp", None),
        P("dp", None),
        P("dp"),
        P("dp", "tp"),
        P("dp", "tp"),
        P("dp", "tp"),
        P("tp", "dp"),
        P("dp", "tp"),
        P("dp", "tp"),
        P("dp", "tp"),
        P("dp", "tp"),
        P("tp", "dp"),
        P("dp", None),
        P("dp"),
        P("dp"),
        P("dp"),
        P("tp"),
        P("tp"),
        P("tp"),
        P("tp"),
        P("dp", None),
    )
    return jax.shard_map(
        on_device,
        mesh=mesh,
        in_specs=placed,
        out_specs=(
            P("dp", None),
            P("dp", None),
            P("dp", "tp"),
            P("dp", "tp"),
            P("dp", "tp"),
            P("tp", "dp"),
            P("dp", "tp"),
            P("dp", "tp"),
            P("dp", "tp"),
            P("dp", "tp"),
            P("tp", "dp"),
            P("dp", None),
            P("dp"),
            P("dp"),
            P("dp"),
            P("tp"),
            P("tp"),
            P("tp"),
            P("tp"),
        ),
        check_vma=False,
    )
```

time: 594 us -> 560 us (0.943)
  matrix products: 31.5 us -> 4.31 us
  other arithmetic: 16.3 us -> 6.04 us
    dot_general x4 -> x0, matrix products: 27.2 us -> none  [the longest x3 19.1 us: dot_nn(): return jnp.dot(left, right, preferred_element_type=F32)]
    unnamed x45 -> x57, local copies, waits for them, and re-layouts: 5.5 us -> 14 us
    reduce_sum x2 -> x1, other arithmetic: 6.98 us -> 0.12 us  [on_device(): jnp.sum(rest[3 * cols:].reshape(heads_here, HEAD), axis=1)]
where the time goes in v4:
time: 560 us; the launch traced here: 550 us
  Pallas kernels  514 us (92%)
  local copies, waits for them, and re-layouts  23.4 us (4%)
  other arithmetic  6.04 us (1%)
    pallas_call x3, Pallas kernels, call(): pl.pallas_call(kernel, out_shape=[shape for shape, _ in self.outs.values(...  348 us
    pallas_call x1, Pallas kernels, attn_backward(): pl.pallas_call(functools.partial(attn_back_kernel, parts, blocks_t), out_...  84.4 us
    pallas_call x1, Pallas kernels, last_backward(): pl.pallas_call(functools.partial(last_kernel, parts), out_shape=[whole, w...  81.5 us
    unnamed x57, local copies, waits for them, and re-layouts  14 us

profile of v4, /device:TPU:0, one launch (start us, length us, event | category | flops | bytes accessed | tf_op | source)
XLA Modules:
  0.0 549.9 jit_solution(5591499398203376449)
XLA Ops:
  0.8 1.0 slice_dynamic-update-slice_fusion.8
  1.8 0.9 slice_dynamic-update-slice_fusion.7
  2.7 0.9 slice_dynamic-update-slice_fusion.2
  3.6 1.0 fusion.5
  4.6 1.0 fusion.6
  5.5 0.9 slice_dynamic-update-slice_fusion.1
  6.4 0.9 slice_dynamic-update-slice_fusion.4
  7.3 0.9 slice_dynamic-update-slice_fusion.3
  8.2 1.0 fusion.7
  12.9 199.5 %shard_map.393 = (f32[1024,384]{1,0:T(8,128)}, f32[1024,384]{1,0:T(8,128)}, bf16[1024,384]{1,0:T(8,128)(2,1)}, bf16[1024,384]{1,0:T(8,128)(2,1)}, bf16[1024,384]...) custom-call(s32[1]{0:T(128)S(6)} %copy.60.refs_0_, ...), custom_call_target="tpu_custom_call" | custom-call | tf_op jit(solution)/shard_map/pallas_call | solution.py:617
  213.2 76.6 %shard_map.394 = (bf16[1536,768]{1,0:T(8,128)(2,1)}, f32[192,768]{1,0:T(8,128)}, bf16[1024,1536]{1,0:T(8,128)(2,1)}, bf16[1024,1536]{1,0:T(8,128)(2,1)}, bf16[10...) custom-call(s32[1]{0:T(128)S(6)} %copy.60.refs_0_, ...), custom_call_target="tpu_custom_call" | custom-call | tf_op jit(solution)/shard_map/pallas_call | solution.py:617
  289.7 72.2 %shard_map.395 = (bf16[1024,1536]{1,0:T(8,128)(2,1)}, bf16[1024,1536]{1,0:T(8,128)(2,1)}, f32[8,1536]{1,0:T(8,128)}, bf16[4,2,192,768]{3,2,1,0:T(8,128)(2,1)}, b...) custom-call(s32[1]{0:T(128)S(6)} %copy.60.refs_0_, bf16[1024,1536]{1,0:T(8,128)(2,1)} %refs_3_.4, ...), custom_call_target="tpu_custom_call" | custom-call | tf_op jit(solution)/shard_map/pallas_call | solution.py:617
  362.0 2.4 slice.127.refs_2_
  364.4 84.4 %shard_map.396 = (bf16[1024,1152]{1,0:T(8,128)(2,1)}, bf16[256,768]{1,0:T(8,128)(2,1)}, f32[8,384]{1,0:T(8,128)}, bf16[1024,1536]{1,0:T(8,128)(2,1)}, f32[192,76...) custom-call(s32[1]{0:T(128)S(6)} %copy.60.refs_0_, ...), custom_call_target="tpu_custom_call" | custom-call | tf_op jit(solution)/shard_map/pallas_call | solution.py:1381
  448.8 81.5 %shard_map.397 = (bf16[1024,1536]{1,0:T(8,128)(2,1)}, bf16[1024,1536]{1,0:T(8,128)(2,1)}, f32[8,1,10752]{2,1,0:T(1,128)}, f32[512,384]{1,0:T(8,128)}, f32[512,384]{1,0:T(8,128)}, /*index=5*/f32[192,1536]{1,0:T(8,128)}) custom-call(s32[1]{0:T(128)S(6)} %copy.60.refs_0_, bf16[1024,1152]{1,0:T(8,128)(2,1)} %get-tuple-element.95.refs_1_, ...), custom_call_target="tpu_custom_call" | custom-call | tf_op jit(solution)/shard_map/pallas_call | solution.py:1523
  530.4 1.1 copy.47
  531.5 4.3 fusion
  535.9 0.9 copy-done.8
  536.9 1.0 maximum_bitcast_fusion
  537.9 1.4 pad_maximum_fusion
  539.2 1.0 slice_bitcast_fusion
  543.2 1.7 copy.61
  544.8 1.4 copy-done
  546.2 1.7 copy.62
  (72 shorter events, 8.6 us)
Async XLA Ops:
  0.7 9.2 %copy-start.22 = (bf16[6]{0:T(256)(128)(2,1)S(1)}, bf16[6]{0:T(256)(128)(2,1)}, u32[]{:S(2)}) copy-start(bf16[6]{0:T(256)(128)(2,1)} %param.46) | copy-start | bytes 40
  0.7 9.4 %copy-start.17 = (bf16[384]{0:T(512)(128)(2,1)S(1)}, bf16[384]{0:T(512)(128)(2,1)}, u32[]{:S(2)}) copy-start(bf16[384]{0:T(512)(128)(2,1)} %param.44) | copy-start | bytes 2308
  0.7 9.4 %copy-start.18 = (bf16[384]{0:T(512)(128)(2,1)S(1)}, bf16[384]{0:T(512)(128)(2,1)}, u32[]{:S(2)}) copy-start(bf16[384]{0:T(512)(128)(2,1)} %param.45) | copy-start | bytes 2308
  0.7 9.4 %copy-start.19 = (bf16[384]{0:T(512)(128)(2,1)S(1)}, bf16[384]{0:T(512)(128)(2,1)}, u32[]{:S(2)}) copy-start(bf16[384]{0:T(512)(128)(2,1)} %param.43) | copy-start | bytes 2308
  0.7 10.0 %copy-start.10 = (bf16[384,192]{0,1:T(8,128)(2,1)S(1)}, bf16[384,192]{0,1:T(8,128)(2,1)}, u32[]{:S(2)}) copy-start(bf16[384,192]{0,1:T(8,128)(2,1)} %param.33) | copy-start | bytes 442372
  0.7 10.0 %copy-start.13 = (bf16[192,384]{1,0:T(8,128)(2,1)S(1)}, bf16[192,384]{1,0:T(8,128)(2,1)}, u32[]{:S(2)}) copy-start(bf16[192,384]{1,0:T(8,128)(2,1)} %param.30) | copy-start | bytes 442372
  0.7 10.0 %copy-start.12 = (bf16[192,384]{1,0:T(8,128)(2,1)S(1)}, bf16[192,384]{1,0:T(8,128)(2,1)}, u32[]{:S(2)}) copy-start(bf16[192,384]{1,0:T(8,128)(2,1)} %param.31) | copy-start | bytes 442372
  0.7 10.0 %copy-start.11 = (bf16[192,384]{1,0:T(8,128)(2,1)S(1)}, bf16[192,384]{1,0:T(8,128)(2,1)}, u32[]{:S(2)}) copy-start(bf16[192,384]{1,0:T(8,128)(2,1)} %param.32) | copy-start | bytes 442372
  0.7 10.8 %copy-start.16 = (bf16[768]{0:T(1024)(128)(2,1)S(1)}, bf16[768]{0:T(1024)(128)(2,1)}, u32[]{:S(2)}) copy-start(bf16[768]{0:T(1024)(128)(2,1)} %param.40) | copy-start | bytes 4612
  0.8 10.8 %copy-start.20 = (bf16[192]{0:T(256)(128)(2,1)S(1)}, bf16[192]{0:T(256)(128)(2,1)}, u32[]{:S(2)}) copy-start(bf16[192]{0:T(256)(128)(2,1)} %param.41) | copy-start | bytes 1156
  0.8 10.9 %copy-start.21 = (bf16[192]{0:T(256)(128)(2,1)S(1)}, bf16[192]{0:T(256)(128)(2,1)}, u32[]{:S(2)}) copy-start(bf16[192]{0:T(256)(128)(2,1)} %param.42) | copy-start | bytes 1156
  0.8 11.6 %copy-start.15 = (bf16[1,1024]{1,0:T(2,128)(2,1)S(1)}, bf16[1,1024]{1,0:T(2,128)(2,1)}, u32[]{:S(2)}) copy-start(bf16[1,1024]{1,0:T(2,128)(2,1)} %param.28) | copy-start | bytes 6148
  9.2 3.7 copy-start.5
  448.8 82.6 %copy-start.14 = (f32[8,128]{1,0:T(8,128)S(1)}, f32[8,128]{1,0:T(8,128)}, u32[]{:S(2)}) copy-start(f32[8,128]{1,0:T(8,128)} %get-tuple-element.111) | copy-start | bytes 12292
  530.4 5.4 copy-start.9
  531.4 4.4 copy-start.3
  535.8 1.1 copy-start.8
  536.9 2.4 copy-start.4
  537.9 2.4 copy-start.2
  537.9 5.3 copy-start.1
  543.2 3.0 copy-start
  546.2 1.7 copy-start.7
  546.2 2.6 copy-start.6

commit v5 on v4

--- a/solution.py
+++ b/solution.py
@@ -597,7 +597,7 @@
 
 class Named:
     def __init__(self):
-        self.ins, self.outs, self.scratch = {}, {}, {}
+        self.ins, self.outs, self.scratch, self.late = {}, {}, {}, {}
 
     def take(self, refs):
         found, at = {}, 0
@@ -608,20 +608,38 @@
             many = isinstance(item, list)
             found[name] = refs[at : at + len(item)] if many else refs[at]
             at += len(item) if many else 1
-        return types.SimpleNamespace(**found)
+        count = len(self.late)
+        copies = []
+        for i, name in enumerate(self.late):
+            found[name] = refs[at + count + i]
+            copies.append(pltpu.make_async_copy(refs[at + i], found[name], refs[at + 2 * count + i]))
+        r = types.SimpleNamespace(**found)
+        r.fetch = types.SimpleNamespace(**dict(zip(self.late, copies)))
+        r.fetches = copies
+        return r
 
     def call(self, kernel, compiler_params):
         flat = []
         for item in self.scratch.values():
             flat += item if isinstance(item, list) else [item]
+        late = list(self.late.values())
+        flat += [pltpu.VMEM(value.shape, value.dtype) for value in late] + [DMA] * len(late)
+        ins, outs = list(self.ins.values()), list(self.outs.values())
+        first, many = len(ins) + len(outs), len(late)
+
+        def body(*refs):
+            own = refs[: len(ins)] + refs[len(ins) + many : first + many]
+            scratch = refs[first + many : len(refs) - 2 * many]
+            kernel(*own, *scratch, *refs[len(ins) : len(ins) + many], *refs[len(refs) - 2 * many :])
+
         results = pl.pallas_call(
-            kernel,
-            out_shape=[shape for shape, _ in self.outs.values()],
-            in_specs=[spec for _, spec in self.ins.values()],
-            out_specs=[spec for _, spec in self.outs.values()],
+            body,
+            out_shape=[shape for shape, _ in outs],
+            in_specs=[spec for _, spec in ins] + [ANY] * many,
+            out_specs=[spec for _, spec in outs],
             scratch_shapes=flat,
             compiler_params=compiler_params,
-        )(*[value for value, _ in self.ins.values()])
+        )(*[value for value, _ in ins], *late)
         return types.SimpleNamespace(**dict(zip(self.outs, results)))
 
 
@@ -749,6 +767,31 @@
             self.part_out(i).wait_send()
 
 
+def pack_kernel(q, k, v, out, gate, up, down, attn_ref, one_ref, two_ref):
+    cols = q.shape[1]
+    for i, w in enumerate((q, k, v)):
+        attn_ref[:, i * cols : (i + 1) * cols] = w[...]
+    attn_ref[:, 3 * cols :] = out[...]
+    for b in range(gate.shape[1] // UNITS):
+        ref, at = (one_ref, b) if b < ONES else (two_ref, b - ONES)
+        here = slice(b * UNITS, (b + 1) * UNITS)
+        for i, value in enumerate((gate[:, here], up[:, here], down[:, here])):
+            ref[:, (3 * at + i) * UNITS : (3 * at + i + 1) * UNITS] = value
+
+
+def pack(q, k, v, out, gate, up, down):
+    depth, cols = q.shape
+    blocks = gate.shape[1] // UNITS
+    widths = (4 * cols, 3 * UNITS * ONES, 3 * UNITS * (blocks - ONES))
+    return pl.pallas_call(
+        pack_kernel,
+        out_shape=[shaped((depth, wide), BF16) for wide in widths],
+        in_specs=[IN_VMEM] * 7,
+        out_specs=[IN_VMEM] * 3,
+        compiler_params=plain_params(),
+    )(q, k, v, out, gate, up, down)
+
+
 def forward_kernel(named, grid, cuts, *refs):
     r = named.take(refs)
     tok, weights, rows_ref, heads_ref = r.tok, r.weights, r.rows, r.heads
@@ -762,6 +805,8 @@
     blocks_here = rows // step_rows
     pairs = cols // PAIR
     attn_engine = text_engine = engine = Idle()
+    for fetch in r.fetches:
+        fetch.start()
     if grid:
         opening = Opening(r)
         attn_engine = GatherChain(cuts[0], r.attn_shard, weights, r.attn_set, A_A)
@@ -779,6 +824,8 @@
         opening.pass_on()
         paced(1, lambda i: None, (attn_engine, O_4))
         opening.collect()
+        r.fetch.w_tk.wait()
+        r.fetch.w_tv.wait()
         paced(GRID, opening.multiply, (attn_engine, 2))
         text_engine.start()
         engine.start()
@@ -865,6 +912,8 @@
         output(sums.core)(i)
         loop(parts_each, lambda k: sums.stage_two(i * parts_each + k))
 
+    for fetch in (r.fetch.tok, r.fetch.cos, r.fetch.sa, r.fetch.sb, r.fetch.seg):
+        fetch.wait()
     paced(blocks_here, project, (text_engine, 4), (engine, 2))
     paced(pairs * blocks_here, attend, (text_engine, 4), (engine, 3))
     finish_pumps(text_engine)
@@ -914,15 +963,15 @@
     grid = clips == GRID
     depth, ffn_wide = ffn_shard.shape
     n = Named()
-    n.ins.update(frames=(frames, IN_SMEM), tok=(tokens, IN_VMEM), heads=(heads_table, IN_VMEM))
-    n.ins.update(cos=(tables[0], IN_VMEM), sa=(tables[1], IN_VMEM), sb=(tables[2], IN_VMEM), seg=(seg, IN_VMEM))
+    n.ins.update(frames=(frames, IN_SMEM), heads=(heads_table, IN_VMEM))
     cuts = None
     if grid:
         attn_shard, cond, small, w_ada, text, w_tk, w_tv = start
         rows_t, slab = text.shape[0], w_tk.shape[0]
         mods = w_ada.shape[1]
         n.ins.update(attn_shard=(attn_shard, ANY), cond=(cond, IN_VMEM), small=(small, IN_VMEM))
-        n.ins.update(w_ada=(w_ada, IN_VMEM), text=(text, ANY), w_tk=(w_tk, IN_VMEM), w_tv=(w_tv, IN_VMEM))
+        n.ins.update(w_ada=(w_ada, IN_VMEM), text=(text, ANY))
+        n.late.update(w_tk=w_tk, w_tv=w_tv)
         n.ins.update(ffn_shard=(ffn_shard, ANY))
         cuts = (
             Blocks(*attn_shard.shape, 96, 384),
@@ -965,6 +1014,7 @@
             text_set=Scatter.scratch(cuts[1], True),
             ffn_set=GatherChain.scratch(cuts[2].count),
         )
+    n.late.update(tok=tokens, cos=tables[0], sa=tables[1], sb=tables[2], seg=seg)
     out = n.call(functools.partial(forward_kernel, n, grid, cuts), params(1))
     if not grid:
         out.weights, out.rows, out.text_all = weights, rows_table, jnp.zeros((1, 16, 128), BF16)
@@ -973,11 +1023,14 @@
 
 UNITS = 256
 ONES = 3
+SP = ((0, 0), (2, 2), (2, 2), (2, 0))
 
 
 def ffn_kernel(named, cut, cut_back, *refs):
     r = named.take(refs)
     engine, scatter = Idle(), Idle()
+    for fetch in r.fetches:
+        fetch.start()
     if cut is not None:
         engine = GatherChain(cut, r.shard, r.w_two, r.gather_set)
         scatter = Scatter(cut_back, r.grads, r.out, r.scatter_set)
@@ -1034,17 +1087,19 @@
                 r.staged[b % 2, m, y, :, 2 * UNITS :] = downs[part]
 
         pumps = 1 if b < ones else 2
-        paced(count, units, (engine, pumps), (scatter, 2 if b > 0 else 0))
+        paced(count, units, (engine, pumps), (scatter, SP[b][0]))
         if not last:
             if b >= 2 and (b > 2 or cut is None):
                 copy(b - 2).wait()
-            paced(LINE, products, (engine, pumps), (scatter, 2 if b > 0 else 0))
+            paced(LINE, products, (engine, pumps), (scatter, SP[b][1]))
             copy(b).start()
         if b == 0 and cut is not None:
             copy(0).wait()
             scatter.start()
 
     paced(count, start_rows, (engine, 1))
+    r.fetch.h_two.wait()
+    r.fetch.w_one.wait()
     each = cut.count // twos if cut is not None else 0
     for b in range(ones):
         block(b)
@@ -1069,8 +1124,8 @@
     grid = clips == GRID
     depth = wide // GRID
     n = Named()
-    n.ins.update(frames=(frames, IN_SMEM), h_two=(h_two, IN_VMEM), cot=(cotangent, IN_VMEM), rows=(rows_table, IN_VMEM))
-    n.ins.update(w_one=(w_one, IN_VMEM))
+    n.ins.update(frames=(frames, IN_SMEM), cot=(cotangent, IN_VMEM), rows=(rows_table, IN_VMEM))
+    n.late.update(h_two=h_two, w_one=w_one)
     whole = (shaped((rows, wide), BF16), IN_VMEM)
     cut = Blocks(depth, half_wide, 96, 384) if grid else None
     cut_back = None
@@ -1120,6 +1175,8 @@
         place = r.down.at[:, pl.ds(b * UNITS, UNITS)]
         return pltpu.make_async_copy(w.at[:, pl.ds(first, UNITS)], place, r.down_s.at[b])
 
+    for fetch in r.fetches:
+        fetch.start()
     for b in range(blocks):
         down_copy(b).start()
     r.colsums[...] = jnp.zeros_like(r.colsums)
@@ -1161,10 +1218,15 @@
         r.colsums[1:2, :] += jnp.sum(live_total * added, axis=0, keepdims=True)
 
     paced(TP_PARTS, sums.stage_two, (engine, 2))
+    for fetch in (r.fetch.h_two, r.fetch.grad_ffn, r.fetch.hid, r.fetch.dgu):
+        fetch.wait()
     paced(LINE, products, (engine, 2))
     for b in range(blocks):
         down_copy(b).wait()
     paced(rows // step_rows, p_block, (engine, 2))
+
+    for fetch in (r.fetch.tok, r.fetch.attn_sum, r.fetch.cot):
+        fetch.wait()
 
     def three(k):
         sums.stage_three(k)
@@ -1197,10 +1259,10 @@
     units, scattered = fed.hid.shape[1], fed.grads.shape[-1]
     cut = Blocks(depth, scattered - 3 * UNITS, 96, 256, 3 * UNITS) if grid else None
     n = Named()
-    n.ins.update(frames=(frames, IN_SMEM), tok=(tokens, IN_VMEM), attn_sum=(attn_sum, IN_VMEM), cot=(cotangent, IN_VMEM))
-    n.ins.update(rows=(rows_table, IN_VMEM), h_two=(h_two, IN_VMEM), grad_ffn=(fed.grad_ffn, IN_VMEM))
-    n.ins.update(hid=(fed.hid, IN_VMEM), dgu=(fed.dgu_last, IN_VMEM), w_one=(w_one, ANY), w_two=(fed.w_two, ANY))
+    n.ins.update(frames=(frames, IN_SMEM), rows=(rows_table, IN_VMEM), w_one=(w_one, ANY), w_two=(fed.w_two, ANY))
     n.ins.update(partial=(fed.partial, ANY))
+    n.late.update(h_two=h_two, grad_ffn=fed.grad_ffn, hid=fed.hid, dgu=fed.dgu_last)
+    n.late.update(tok=tokens, attn_sum=attn_sum, cot=cotangent)
     whole = shaped((rows, wide), BF16)
     n.outs.update(grad_attn=(whole, IN_VMEM), grad_state=(whole, IN_VMEM), colsums=(shaped((8, wide), F32), IN_VMEM))
     n.outs.update(g_last=(shaped((LINE, 2, depth, 3 * UNITS), BF16), IN_VMEM), p_ffn=(whole, ANY))
@@ -1218,18 +1280,27 @@
     return n.call(functools.partial(state_kernel, n, cut), params(2))
 
 
-def attn_back_kernel(blocks, blocks_t, *refs):
-    frames, grad_attn, weights, heads_ref, cos_ref, sa_ref, sb_ref, seg_ref = refs[:8]
-    (q_pre, k_pre, q_rot, k_rot, q_text, v_ref, self_o, inv_l) = refs[8:16]
-    (ky_pre, kyr, vy, text_o, inv_lt, h_one, mixed, partial, grad) = refs[16:25]
-    grad_qkv, grad_text, gains, ffn_sum, out, g_attn, all_text = refs[25:32]
-    do_self, do_text, d_self, d_text, dqn, dk, dv, dky, dvy, klive, staged, stage_s = refs[32:44]
-    sums = TpSum(partial, ffn_sum, refs[44:46], refs[46:52], refs[52])
+def attn_back_kernel(named, blocks, blocks_t, *refs):
+    r = named.take(refs)
+    out_cols = r.full.shape[1] * 3 // 4
+    out_fetch = pltpu.make_async_copy(r.full.at[:, out_cols:], r.weights, r.weights_s)
+    out_fetch.start()
+    frames, grad_attn, weights, heads_ref, seg_ref = r.frames, r.grad_attn, r.weights, r.heads, r.seg
+    cos_ref, sa_ref, sb_ref = r.cos, r.sa, r.sb
+    q_pre, k_pre, q_rot, k_rot, q_text, v_ref, self_o, inv_l = (
+        r.q_pre, r.k_pre, r.q_rot, r.k_rot, r.q_text, r.values, r.self_o, r.inv_l
+    )
+    ky_pre, kyr, vy, text_o, inv_lt, h_one, mixed = r.ky_pre, r.kyr, r.vy, r.text_o, r.inv_lt, r.h_one, r.mixed
+    grad_qkv, grad_text, gains, g_attn = r.grad_qkv, r.grad_text, r.gains, r.g_attn
+    do_self, do_text, d_self, d_text, dqn, dk, dv, dky, dvy, klive, staged, stage_s = r.work_set
+    sums = TpSum(r.partial, r.ffn_sum, r.tp_set[:2], r.tp_set[2:8], r.tp_set[8])
+    for fetch in r.fetches:
+        fetch.start()
     qgain, kgain, kygain, gate = (heads_ref.at[i : i + 1] for i in range(4))
     engine, text_engine = Idle(), Idle()
     if blocks is not None:
-        engine = Scatter(blocks, grad, out, refs[53:61], ahead=A_S1)
-        text_engine = GatherChain(blocks_t, grad_text, all_text, refs[61:], A_T)
+        engine = Scatter(blocks, r.grad, r.out, r.scatter_set, ahead=A_S1)
+        text_engine = GatherChain(blocks_t, grad_text, r.all_text, r.gather_set, A_T)
         greet(dp_peers(), tp_peers())
         engine.start()
     else:
@@ -1303,6 +1374,7 @@
 
         return step
 
+    out_fetch.wait()
     paced(blocks_here, start_rows, (engine, 2))
     def norm_back(grad_normed, pre, gain, row):
         inverse = head_inverse(pre, seg_ref[...])
@@ -1323,6 +1395,8 @@
         for k in range(TP_PARTS // blocks_here):
             sums.stage_three(i * (TP_PARTS // blocks_here) + k)
 
+    for fetch in (r.fetch.q_text, r.fetch.kyr, r.fetch.vy):
+        fetch.wait()
     text_back = back(q_text, kyr, kyr, vy, do_text, d_text, dky, dvy, False)
 
     def text_step(i):
@@ -1330,6 +1404,8 @@
         pl.when(i < TP_PARTS)(lambda: sums.stage_two(i))
 
     paced(pairs * blocks_here, text_step, (engine, 3))
+    for fetch in (r.fetch.seg, r.fetch.ky_pre, r.fetch.q_rot, r.fetch.values, r.fetch.cos, r.fetch.sa, r.fetch.sb):
+        fetch.wait()
     grad_text[:, :cols] = norm_back(dky[...], ky_pre[...], kygain[...], 2)
     grad_text[:, cols:] = dvy[...].astype(BF16)
     text_engine.start()
@@ -1338,6 +1414,8 @@
     half = pairs * blocks_here // 2
     paced(half, self_back, (engine, 6), (text_engine, 2))
     paced(half, lambda i: self_back(i + half), (text_engine, 3))
+    for fetch in (r.fetch.q_pre, r.fetch.k_pre, r.fetch.h_one, r.fetch.mixed):
+        fetch.wait()
     paced(blocks_here, end_rows, (text_engine, 2))
     tall = wide // LINE
 
@@ -1367,52 +1445,63 @@
     text_engine.drain()
 
 
-def attn_backward(clips, frames, grad_attn, w_out, heads_table, tables, seg, saved, partial, g_up):
+def attn_backward(clips, frames, grad_attn, full_attn, heads_table, tables, seg, p, partial, g_last):
     rows, wide = grad_attn.shape
     cols = heads_table.shape[1]
-    rows_t = saved[8].shape[0]
-    depth, units = wide // GRID, g_up.shape[-1]
+    rows_t = p.kyr.shape[0]
+    depth, last_wide = wide // GRID, g_last.shape[-1]
     grid = clips == GRID
-    parts = Blocks(depth, units, 96, 256) if grid else None
-    blocks_t = Blocks(rows_t, 2 * cols, 32, 2 * cols) if grid else None
     f, b = pltpu.VMEM((rows, cols), F32), pltpu.VMEM((rows, cols), BF16)
     ft = pltpu.VMEM((rows_t, cols), F32)
     slim = pltpu.VMEM((rows, PAIR), BF16)
-    return pl.pallas_call(
-        functools.partial(attn_back_kernel, parts, blocks_t),
-        out_shape=[
-            shaped((rows, 3 * cols), BF16),
-            shaped((rows_t, 2 * cols), BF16),
-            shaped((8, cols), F32),
-            shaped((rows, wide), BF16),
-            shaped((depth, units), F32),
-            shaped((LINE, 2, depth, 4 * cols), BF16),
-            shaped((GRID * rows_t, 2 * cols), BF16),
-        ],
-        in_specs=[IN_SMEM] + [IN_VMEM] * 22 + [ANY] * 2,
-        out_specs=[IN_VMEM] * 5 + [ANY] * 2,
-        scratch_shapes=[b, b, slim, slim, f, f, f, ft, ft, b]
-        + [pltpu.VMEM((2, 2, depth, 4 * cols), BF16), DMA((2,))]
-        + TpSum.scratch(rows, wide)
-        + [DMA((TP_PARTS,))]
-        + (Scatter.scratch(parts) + GatherChain.scratch(blocks_t.count) if grid else []),
-        compiler_params=params(3),
-    )(frames, grad_attn, w_out, heads_table, *tables, seg, *saved, partial, g_up)
-
-
-def last_kernel(parts, *refs):
-    frames, grad_qkv, weights, tok, grad_state, rows_ref, sums_two, gains = refs[:8]
-    ffn_sum, attn_sum, cot, text_all, all_text, grad_a = refs[8:14]
-    result, grad_tokens, vecs, g_tk, g_tv, out_a = refs[14:20]
-    partial, grad_n, colsum, outsum, vec = refs[20:25]
-    sums = TpSum(partial, grad_n, refs[25:27], refs[27:33])
+    n = Named()
+    n.ins.update(frames=(frames, IN_SMEM), grad_attn=(grad_attn, IN_VMEM), full=(full_attn, ANY))
+    n.ins.update(heads=(heads_table, IN_VMEM), k_rot=(p.k_rot, IN_VMEM), self_o=(p.self_o, IN_VMEM))
+    n.ins.update(inv_l=(p.inv_l, IN_VMEM), text_o=(p.text_o, IN_VMEM), inv_lt=(p.inv_lt, IN_VMEM), partial=(partial, ANY))
+    n.late.update(q_text=p.q_text, kyr=p.kyr, vy=p.vy, seg=seg, ky_pre=p.ky_pre, q_rot=p.q_rot, values=p.values)
+    n.late.update(cos=tables[0], sa=tables[1], sb=tables[2], q_pre=p.q_pre, k_pre=p.k_pre, h_one=p.h_one, mixed=p.mixed)
+    n.outs.update(
+        grad_qkv=(shaped((rows, 3 * cols), BF16), IN_VMEM),
+        grad_text=(shaped((rows_t, 2 * cols), BF16), IN_VMEM),
+        gains=(shaped((8, cols), F32), IN_VMEM),
+        ffn_sum=(shaped((rows, wide), BF16), IN_VMEM),
+        g_attn=(shaped((LINE, 2, depth, 4 * cols), BF16), ANY),
+    )
+    n.scratch.update(
+        work_set=[b, b, slim, slim, f, f, f, ft, ft, b, pltpu.VMEM((2, 2, depth, 4 * cols), BF16), DMA((2,))],
+        tp_set=TpSum.scratch(rows, wide) + [DMA((TP_PARTS,))],
+        weights=pltpu.VMEM((wide, cols), BF16),
+        weights_s=DMA,
+    )
+    parts = blocks_t = None
+    if grid:
+        parts = Blocks(depth, last_wide, 96, 256)
+        blocks_t = Blocks(rows_t, 2 * cols, 32, 2 * cols)
+        n.ins.update(grad=(g_last, ANY))
+        n.outs.update(
+            out=(shaped((depth, last_wide), F32), IN_VMEM), all_text=(shaped((GRID * rows_t, 2 * cols), BF16), ANY)
+        )
+        n.scratch.update(scatter_set=Scatter.scratch(parts), gather_set=GatherChain.scratch(blocks_t.count))
+    return n.call(functools.partial(attn_back_kernel, n, parts, blocks_t), params(3))
+
+
+def last_kernel(named, parts, *refs):
+    r = named.take(refs)
+    frames, grad_qkv, weights, tok, grad_state = r.frames, r.grad_qkv, r.weights, r.tok, r.grad_state
+    rows_ref, sums_two, gains, ffn_sum, attn_sum, cot = r.rows, r.sums_two, r.gains, r.ffn_sum, r.attn_sum, r.cot
+    result, grad_tokens, vecs = r.result, r.grad_tokens, r.vecs
+    partial, grad_n, colsum, outsum, vec = r.work_set
+    sums = TpSum(partial, grad_n, r.tp_set[:2], r.tp_set[2:8])
     me = lax.axis_index("dp")
     engine = Idle()
     peers = []
+    for fetch in r.fetches:
+        fetch.start()
     if parts is not None:
-        v_s, v_r = refs[33:35]
+        v_s, v_r = r.sems_set
+        text_all, all_text, g_tk, g_tv = r.text_all, r.all_text, r.g_tk, r.g_tv
         peers = dp_peers()
-        engine = Scatter(parts, grad_a, out_a, refs[35:], ahead=A_S2)
+        engine = Scatter(parts, r.grad_a, r.out_a, r.scatter_set, ahead=A_S2)
         greet(peers, tp_peers())
         engine.start()
     else:
@@ -1449,6 +1538,8 @@
         result[here, :] = (state + tanh_two * added).astype(BF16)
         outsum[...] += jnp.sum(added * cot[here, :].astype(F32), axis=0, keepdims=True)
 
+    for fetch in (r.fetch.tok, r.fetch.ffn_sum, r.fetch.attn_sum, r.fetch.cot):
+        fetch.wait()
     paced(tok.shape[0] // 64, output, (engine, P_3))
     if parts is not None:
         rows_t = text_all.shape[1]
@@ -1460,6 +1551,8 @@
 
         g_tk[...] = jnp.zeros_like(g_tk)
         g_tv[...] = jnp.zeros_like(g_tv)
+        r.fetch.text_all.wait()
+        r.fetch.all_text.wait()
         paced(GRID, text_products, (engine, P_4))
 
     def update(k, which):
@@ -1477,6 +1570,7 @@
         sums.stage_three(k)
         update(k, sums.core)
 
+    r.fetch.grad_state.wait()
     paced(TP_PARTS, three, (engine, 4))
 
     def four(k):
@@ -1508,44 +1602,38 @@
     engine.drain()
 
 
-def last_backward(
-    clips, frames, grad_qkv, full_attn, tokens, grad_state, rows_table, sums_two, gains, ffn_sum, attn_sum, cotangent,
-    text_all, all_text, g_attn
-):
+def last_backward(clips, frames, tokens, cotangent, p, state, back, qkv_weights):
     rows, wide = tokens.shape
     grid = clips == GRID
-    cols = gains.shape[1]
-    depth, wide_a = g_attn.shape[-2:]
-    slab = text_all.shape[-1]
-    parts = Blocks(depth, wide_a, 96, 256) if grid else None
-    whole = shaped((rows, wide), BF16)
+    cols = back.gains.shape[1]
+    depth, wide_a = back.g_attn.shape[-2:]
+    whole = (shaped((rows, wide), BF16), IN_VMEM)
     vec = (1, 6 * wide + 4 * cols)
-    return pl.pallas_call(
-        functools.partial(last_kernel, parts),
-        out_shape=[
-            whole,
-            whole,
-            shaped(((GRID if grid else 1),) + vec, F32),
-            shaped((slab, cols), F32),
-            shaped((slab, cols), F32),
-            shaped((depth, wide_a), F32),
-        ],
-        in_specs=[IN_SMEM] + [IN_VMEM] * 12 + [ANY],
-        out_specs=[IN_VMEM] * 6,
-        scratch_shapes=[
+    n = Named()
+    n.ins.update(frames=(frames, IN_SMEM), grad_qkv=(back.grad_qkv, IN_VMEM), weights=(qkv_weights, IN_VMEM))
+    n.ins.update(rows=(p.rows, IN_VMEM), sums_two=(state.colsums, IN_VMEM), gains=(back.gains, IN_VMEM))
+    n.late.update(tok=tokens, ffn_sum=back.ffn_sum, attn_sum=p.attn_sum, cot=cotangent)
+    n.outs.update(result=whole, grad_tokens=whole, vecs=(shaped(((GRID if grid else 1),) + vec, F32), IN_VMEM))
+    n.scratch.update(
+        work_set=[
             pltpu.VMEM((rows, wide), BF16),
             pltpu.VMEM((rows, wide), BF16),
             pltpu.VMEM((1, wide), F32),
             pltpu.VMEM((1, wide), F32),
             pltpu.VMEM(vec, F32),
-        ]
-        + TpSum.scratch(rows, wide)
-        + ([DMA((GRID - 1,))] * 2 + Scatter.scratch(parts) if grid else []),
-        compiler_params=params(4),
-    )(
-        frames, grad_qkv, full_attn, tokens, grad_state, rows_table, sums_two, gains, ffn_sum, attn_sum, cotangent,
-        text_all, all_text, g_attn
+        ],
+        tp_set=TpSum.scratch(rows, wide),
     )
+    parts = None
+    if grid:
+        parts = Blocks(depth, wide_a, 96, 256)
+        g_text = (shaped((p.text_all.shape[-1], cols), F32), IN_VMEM)
+        n.ins.update(grad_a=(back.g_attn, ANY))
+        n.late.update(text_all=p.text_all, all_text=back.all_text)
+        n.outs.update(g_tk=g_text, g_tv=g_text, out_a=(shaped((depth, wide_a), F32), IN_VMEM))
+        n.scratch.update(sems_set=[DMA((GRID - 1,))] * 2, scatter_set=Scatter.scratch(parts))
+    n.late.update(grad_state=state.grad_state)
+    return n.call(functools.partial(last_kernel, n, parts), params(4))
 
 
 def gather_plain(shard):
@@ -1578,6 +1666,56 @@
         lift_two,
     )
     return gather_plain(shard), jnp.stack(values), act.astype(F32), dot_nn(text, full_text)
+
+
+def unpack_kernel(count, *refs):
+    blocks, (attn, vecs, act) = refs[:count], refs[count : count + 3]
+    q, k, v, out, gate, up, down, g_ada, bias, g_one, g_two, rest = refs[count + 3 :]
+    cols = q.shape[1]
+    for i, ref in enumerate((q, k, v, out)):
+        ref[...] = attn[:, i * cols : (i + 1) * cols]
+    b = 0
+    for ref in blocks:
+        for at in range(0, ref.shape[1], 3 * UNITS):
+            for i, place in enumerate((gate, up, down)):
+                place[:, b * UNITS : (b + 1) * UNITS] = ref[:, at + i * UNITS : at + (i + 1) * UNITS]
+            b += 1
+    total = vecs[0]
+    for i in range(1, vecs.shape[0]):
+        total = total + vecs[i]
+    wide = g_ada.shape[1] // 4
+    rest[...] = total[:, 6 * wide :]
+    me = lax.axis_index("dp")
+    for i in range(vecs.shape[0]):
+
+        @pl.when(me == i)
+        def _():
+            bias[...] = total[:, i * bias.shape[1] : (i + 1) * bias.shape[1]]
+            gain = g_one.shape[1]
+            g_one[...] = total[:, 4 * wide + i * gain : 4 * wide + (i + 1) * gain]
+            g_two[...] = total[:, 5 * wide + i * gain : 5 * wide + (i + 1) * gain]
+
+    clips = jnp.concatenate([vecs[i][:, : 4 * wide] for i in range(vecs.shape[0])], axis=0)
+    turned = act[...].T
+    for at in range(0, 4 * wide, 512):
+        part = turned[:, 0:1] * clips[0:1, at : at + 512]
+        for i in range(1, clips.shape[0]):
+            part = part + turned[:, i : i + 1] * clips[i : i + 1, at : at + 512]
+        g_ada[:, at : at + 512] = part
+
+
+def unpack(blocks, attn, vecs, act, units, bias_rows, gain_rows):
+    depth, cols = attn.shape[0], attn.shape[1] // 4
+    wide = (vecs.shape[2] - 4 * cols) // 6
+    shapes = [(depth, cols)] * 4 + [(depth, units)] * 3
+    shapes += [(act.shape[1], 4 * wide), (1, bias_rows), (1, gain_rows), (1, gain_rows), (1, 4 * cols)]
+    return pl.pallas_call(
+        functools.partial(unpack_kernel, len(blocks)),
+        out_shape=[shaped(shape, F32) for shape in shapes],
+        in_specs=[IN_VMEM] * (len(blocks) + 3),
+        out_specs=[IN_VMEM] * len(shapes),
+        compiler_params=plain_params(),
+    )(*blocks, attn, vecs, act)
 
 
 def on_device(
@@ -1612,15 +1750,7 @@
     bias_rows, gain_rows = ada_bias.shape[0], norm_one.shape[0]
     small = jnp.concatenate([ada_bias, norm_one, norm_two]).astype(F32)[None, :]
     cond_rows = cond.astype(F32).reshape(clips, 1, -1)
-    attn_shard = jnp.concatenate([w_query, w_key, w_value, w_out.T], axis=1)
-    turned = w_down.T
-    pieces = [
-        jnp.concatenate(
-            [w[:, b * UNITS : (b + 1) * UNITS] for b in range(*ends) for w in (w_gate, w_up, turned)],
-            axis=1,
-        )
-        for ends in ((0, ONES), (ONES, units // UNITS))
-    ]
+    attn_shard, *pieces = pack(w_query, w_key, w_value, w_out.T, w_gate, w_up, w_down.T)
     opening = (attn_shard, cond_rows, small, w_ada, text, w_text_key, w_text_value)
     if not grid:
         full_attn, rows_table, act_rows, ty = first_plain(*opening)
@@ -1639,80 +1769,42 @@
     else:
         half_one, second = gather_plain(pieces[0]), gather_plain(pieces[1])
     p = passed
-    saved = (p.q_pre, p.k_pre, p.q_rot, p.k_rot, p.q_text, p.values, p.self_o, p.inv_l)
-    saved += (p.ky_pre, p.kyr, p.vy, p.text_o, p.inv_lt, p.h_one, p.mixed)
-    fed = ffn(clips, frames, p.h_two, cotangent, rows_table, half_one, second)
-    state = state_backward(clips, frames, tokens, p.attn_sum, cotangent, rows_table, p.h_two, half_one, fed)
-    out_turned = full_attn[:, 3 * cols :]
-    grad_qkv, grad_text, gains, ffn_sum, s_last, g_attn, all_text = attn_backward(
-        clips, frames, state.grad_attn, out_turned, heads_table, tables, seg, saved, state.p_ffn, state.g_last
+    fed = ffn(clips, frames, p.h_two, cotangent, p.rows, half_one, second)
+    state = state_backward(clips, frames, tokens, p.attn_sum, cotangent, p.rows, p.h_two, half_one, fed)
+    back = attn_backward(
+        clips, frames, state.grad_attn, full_attn, heads_table, tables, seg, p, state.p_ffn, state.g_last
     )
-    result, grad_tokens, vecs, s_text_key, s_text_value, s_attn = last_backward(
-        clips,
-        frames,
-        grad_qkv,
-        full_attn,
-        tokens,
-        state.grad_state,
-        rows_table,
-        state.colsums,
-        gains,
-        ffn_sum,
-        p.attn_sum,
-        cotangent,
-        p.text_all,
-        all_text if grid else grad_text,
-        g_attn,
-    )
+    last = last_backward(clips, frames, tokens, cotangent, p, state, back, full_attn)
+    vecs = last.vecs
     s_blocks = [fed.out, state.out] if grid else [scatter_plain(fed.grads.reshape(wide, -1))]
+    if grid:
+        s_last, s_attn, s_text_key, s_text_value = back.out, last.out_a, last.g_tk, last.g_tv
     if not grid:
-        s_last, s_attn = (scatter_plain(g.reshape(wide, -1)) for g in (state.g_last, g_attn))
-        s_text = scatter_plain(dot_tn(text, grad_text).astype(BF16))
+        s_last, s_attn = (scatter_plain(g.reshape(wide, -1)) for g in (state.g_last, back.g_attn))
+        s_text = scatter_plain(dot_tn(text, back.grad_text).astype(BF16))
         s_text_key, s_text_value = s_text[:, :cols], s_text[:, cols:]
         vecs = lax.all_gather(vecs[0], "dp", axis=0)
-    s_ffn = [
-        jnp.concatenate(
-            [
-                s[:, at + i * UNITS : at + (i + 1) * UNITS]
-                for s in (*s_blocks, s_last)
-                for at in range(0, s.shape[1], 3 * UNITS)
-            ],
-            axis=1,
-        )
-        for i in range(3)
-    ]
-    vecs = vecs[:, 0, :]
-    mod_wide = 4 * wide
-    g_ada = lax.dot_general(
-        act_rows,
-        vecs[:, :mod_wide],
-        (((0,), (0,)), ((), ())),
-        precision=lax.Precision.HIGHEST,
-        preferred_element_type=F32,
+    g_query, g_key, g_value, g_out, g_gate, g_up, g_down, g_ada, g_bias, g_one, g_two, rest = unpack(
+        (*s_blocks, s_last), s_attn, vecs, act_rows, units, bias_rows, gain_rows
     )
-    sums = jnp.sum(vecs, axis=0)
-    me = lax.axis_index("dp")
-    g_bias = lax.dynamic_slice(sums, (me * bias_rows,), (bias_rows,))
-    g_norm_one = lax.dynamic_slice(sums, (mod_wide + me * gain_rows,), (gain_rows,))
-    g_norm_two = lax.dynamic_slice(sums, (mod_wide + wide + me * gain_rows,), (gain_rows,))
-    rest = sums[mod_wide + 2 * wide :]
+    rest = rest[0]
     g_cross_gate = jnp.sum(rest[3 * cols :].reshape(heads_here, HEAD), axis=1) * (1.0 - gate_tanh * gate_tanh)
     return (
-        result,
-        grad_tokens,
-        s_attn[:, :cols],
-        s_attn[:, cols : 2 * cols],
-        s_attn[:, 2 * cols : 3 * cols],
-        s_attn[:, 3 * cols :].T,
+        last.result,
+        last.grad_tokens,
+        g_query,
+        g_key,
+        g_value,
+        g_out.T,
         s_text_key,
         s_text_value,
-        s_ffn[0],
-        s_ffn[1],
-        s_ffn[2].T,
+        g_gate,
+        g_up,
+        g_down.T,
         g_ada,
-        g_bias,
-        g_norm_one,
-        g_norm_two,
+        g_bias[0],
+        g_one[0],
+        g_two[0],
         rest[:cols],
         rest[cols : 2 * cols],
         rest[2 * cols : 3 * cols],

time: 560 us -> 532 us (0.950)
  local copies, waits for them, and re-layouts: 23.4 us -> 12.8 us
  Pallas kernels: 514 us -> 504 us
    pallas_call x5 -> x7, Pallas kernels: 514 us -> 504 us  [the longest x5 494 us: call(): pl.pallas_call(body, out_shape=[shape for shape, _ in outs], in_specs=[sp...]
    unnamed x57 -> x14, local copies, waits for them, and re-layouts: 14 us -> 6.47 us
where the time goes in v5:
time: 532 us; the launch traced here: 522 us
  Pallas kernels  504 us (95%)
  local copies, waits for them, and re-layouts  12.8 us (2%)
    pallas_call x5, Pallas kernels, call(): pl.pallas_call(body, out_shape=[shape for shape, _ in outs], in_specs=[sp...  494 us

profile of v5, /device:TPU:0, one launch (start us, length us, event | category | flops | bytes accessed | tf_op | source)
XLA Modules:
  0.0 522.4 jit_solution(11325866408566462043)
XLA Ops:
  1.3 0.7 convert_tanh_fusion
  2.0 0.7 concatenate.17
  2.6 0.7 concatenate.18
  3.3 0.7 reshape.96
  4.0 0.7 reshape.97
  4.6 0.7 reshape.98
  5.3 0.7 concatenate.16
  6.1 0.6 convert_element_type.21.refs_4_
  6.9 1.3 bitcast_convert_fusion.refs_3_
  8.2 0.6 stack.31.refs_1_.refs_3_
  8.8 2.7 shard_map.393
  11.5 197.8 %shard_map.394 = (f32[1024,384]{1,0:T(8,128)}, f32[1024,384]{1,0:T(8,128)}, bf16[1024,384]{1,0:T(8,128)(2,1)}, bf16[1024,384]{1,0:T(8,128)(2,1)}, bf16[1024,384]...) custom-call(s32[1]{0:T(128)S(6)} %copy.49.refs_0_, ...), custom_call_target="tpu_custom_call" | custom-call | tf_op jit(solution)/shard_map/pallas_call | solution.py:635
  209.4 73.6 %shard_map.395 = (bf16[1536,768]{1,0:T(8,128)(2,1)}, f32[192,768]{1,0:T(8,128)}, bf16[1024,1536]{1,0:T(8,128)(2,1)}, bf16[1024,1536]{1,0:T(8,128)(2,1)}, bf16[10...) custom-call(s32[1]{0:T(128)S(6)} %copy.49.refs_0_, bf16[1024,1536]{1,0:T(8,128)(2,1)} %refs_10_.5, ...), custom_call_target="tpu_custom_call" | custom-call | tf_op jit(solution)/shard_map/pallas_call | solution.py:635
  283.0 66.6 %shard_map.396 = (bf16[1024,1536]{1,0:T(8,128)(2,1)}, bf16[1024,1536]{1,0:T(8,128)(2,1)}, f32[8,1536]{1,0:T(8,128)}, bf16[4,2,192,768]{3,2,1,0:T(8,128)(2,1)}, b...) custom-call(s32[1]{0:T(128)S(6)} %copy.49.refs_0_, f32[8,1536]{1,0:T(8,128)} %get-tuple-element.83.refs_2_.refs_1_.refs_3_, ...), custom_call_target="tpu_custom_call" | custom-call | tf_op jit(solution)/shard_map/pallas_call | solution.py:635
  349.6 81.5 %shard_map.397 = (bf16[1024,1152]{1,0:T(8,128)(2,1)}, bf16[256,768]{1,0:T(8,128)(2,1)}, f32[8,384]{1,0:T(8,128)}, bf16[1024,1536]{1,0:T(8,128)(2,1)}, bf16[4,2,1...) custom-call(s32[1]{0:T(128)S(6)} %copy.49.refs_0_, ...), custom_call_target="tpu_custom_call" | custom-call | tf_op jit(solution)/shard_map/pallas_call | solution.py:635
  431.1 74.7 %shard_map.398 = (bf16[1024,1536]{1,0:T(8,128)(2,1)}, bf16[1024,1536]{1,0:T(8,128)(2,1)}, f32[8,1,10752]{2,1,0:T(1,128)}, f32[512,384]{1,0:T(8,128)}, f32[512,384]{1,0:T(8,128)}, /*index=5*/f32[192,1536]{1,0:T(8,128)}) custom-call(s32[1]{0:T(128)S(6)} %copy.49.refs_0_, bf16[1024,1152]{1,0:T(8,128)(2,1)} %get-tuple-element.113.refs_1_, ...), custom_call_target="tpu_custom_call" | custom-call | tf_op jit(solution)/shard_map/pallas_call | solution.py:635
  505.9 6.5 %shard_map.399 = (f32[192,384]{1,0:T(8,128)}, f32[192,384]{1,0:T(8,128)}, f32[192,384]{1,0:T(8,128)}, f32[192,384]{1,0:T(8,128)}, f32[192,1024]{1,0:T(8,128)}, /...) custom-call(f32[192,768]{1,0:T(8,128)} %get-tuple-element.123.refs_0, ...), custom_call_target="tpu_custom_call" | custom-call | tf_op jit(solution)/shard_map/pallas_call | solution.py:1712
  512.4 1.3 reduce
  513.6 1.3 slice_reduce_fusion
  515.7 1.7 copy.50
  517.4 1.4 copy-done
  518.7 1.7 copy.51
  520.4 0.9 copy.52
  521.3 0.9 copy.53
  (16 shorter events, 1.0 us)
Async XLA Ops:
  505.8 9.3 %copy-start.4 = (bf16[6]{0:T(256)(128)(2,1)S(1)}, bf16[6]{0:T(256)(128)(2,1)}, u32[]{:S(2)}) copy-start(bf16[6]{0:T(256)(128)(2,1)} %param.46) | copy-start | bytes 40
  505.9 9.9 %copy-start.1 = (bf16[1024,1536]{1,0:T(8,128)(2,1)S(1)}, bf16[1024,1536]{1,0:T(8,128)(2,1)}, u32[]{:S(2)}) copy-start(bf16[1024,1536]{1,0:T(8,128)(2,1)} %get-tuple-element.166) | copy-start | bytes 9437188
  515.7 3.0 copy-start
  518.7 1.7 copy-start.3
  518.7 2.6 copy-start.2

commit v6 on v5

--- a/solution.py
+++ b/solution.py
@@ -767,8 +767,17 @@
             self.part_out(i).wait_send()
 
 
-def pack_kernel(q, k, v, out, gate, up, down, attn_ref, one_ref, two_ref):
+def pack_kernel(q, k, v, out, gate, up, down, *refs):
+    vectors, (attn_ref, one_ref, two_ref, small_ref, heads_ref) = refs[:7], refs[7:]
     cols = q.shape[1]
+    at = 0
+    for vector in vectors[:3]:
+        count = vector.shape[0]
+        small_ref[:, at : at + count] = vector[...].astype(F32).reshape(1, count)
+        at += count
+    heads_ref[...] = jnp.zeros_like(heads_ref)
+    for i, vector in enumerate(vectors[3:]):
+        heads_ref[i : i + 1, :] = vector[...].astype(F32).reshape(1, cols)
     for i, w in enumerate((q, k, v)):
         attn_ref[:, i * cols : (i + 1) * cols] = w[...]
     attn_ref[:, 3 * cols :] = out[...]
@@ -779,17 +788,18 @@
             ref[:, (3 * at + i) * UNITS : (3 * at + i + 1) * UNITS] = value
 
 
-def pack(q, k, v, out, gate, up, down):
+def pack(q, k, v, out, gate, up, down, vectors):
     depth, cols = q.shape
     blocks = gate.shape[1] // UNITS
     widths = (4 * cols, 3 * UNITS * ONES, 3 * UNITS * (blocks - ONES))
     return pl.pallas_call(
         pack_kernel,
-        out_shape=[shaped((depth, wide), BF16) for wide in widths],
-        in_specs=[IN_VMEM] * 7,
-        out_specs=[IN_VMEM] * 3,
+        out_shape=[shaped((depth, wide), BF16) for wide in widths]
+        + [shaped((1, sum(vector.shape[0] for vector in vectors[:3])), F32), shaped((8, cols), F32)],
+        in_specs=[IN_VMEM] * 14,
+        out_specs=[IN_VMEM] * 5,
         compiler_params=plain_params(),
-    )(q, k, v, out, gate, up, down)
+    )(q, k, v, out, gate, up, down, *vectors)
 
 
 def forward_kernel(named, grid, cuts, *refs):
@@ -1748,19 +1758,15 @@
     cols, units = w_query.shape[1], w_gate.shape[1]
     heads_here = cols // HEAD
     bias_rows, gain_rows = ada_bias.shape[0], norm_one.shape[0]
-    small = jnp.concatenate([ada_bias, norm_one, norm_two]).astype(F32)[None, :]
+    gate_tanh = jnp.tanh(cross_gate.astype(F32))
+    vectors = (ada_bias, norm_one, norm_two, query_gain, key_gain, text_key_gain, jnp.repeat(gate_tanh, HEAD))
     cond_rows = cond.astype(F32).reshape(clips, 1, -1)
-    attn_shard, *pieces = pack(w_query, w_key, w_value, w_out.T, w_gate, w_up, w_down.T)
+    packed = pack(w_query, w_key, w_value, w_out.T, w_gate, w_up, w_down.T, vectors)
+    attn_shard, *pieces, small, heads_table = packed
     opening = (attn_shard, cond_rows, small, w_ada, text, w_text_key, w_text_value)
     if not grid:
         full_attn, rows_table, act_rows, ty = first_plain(*opening)
         opening = (full_attn, rows_table, ty)
-    gate_tanh = jnp.tanh(cross_gate.astype(F32))
-    blank = jnp.zeros((cols,), F32)
-    heads_table = jnp.stack(
-        [query_gain.astype(F32), key_gain.astype(F32), text_key_gain.astype(F32), jnp.repeat(gate_tanh, HEAD)]
-        + [blank] * 4
-    )
     tables, seg = rope_tables(rows), segment_ones(cols)
     passed = forward(clips, frames, tokens, heads_table, tables, seg, pieces[0], opening)
     full_attn, rows_table = passed.weights, passed.rows

time: 532 us -> 527 us (level)
  no operation moved by 1% of the time
where the time goes in v6:
time: 527 us; the launch traced here: 518 us
  Pallas kernels  503 us (95%)
  local copies, waits for them, and re-layouts  8.62 us (2%)
    pallas_call x5, Pallas kernels, call(): pl.pallas_call(body, out_shape=[shape for shape, _ in outs], in_specs=[sp...  494 us

profile of v6, /device:TPU:0, one launch (start us, length us, event | category | flops | bytes accessed | tf_op | source)
XLA Modules:
  0.0 517.6 jit_solution(8315785647365800916)
XLA Ops:
  1.3 0.7 convert_tanh_fusion
  2.0 0.1 broadcast_in_dim.3
  2.0 0.7 reshape.54.refs_6_
  2.7 1.3 bitcast_convert_fusion.refs_3_
  4.0 2.8 shard_map.393
  6.8 197.8 %shard_map.394 = (f32[1024,384]{1,0:T(8,128)}, f32[1024,384]{1,0:T(8,128)}, bf16[1024,384]{1,0:T(8,128)(2,1)}, bf16[1024,384]{1,0:T(8,128)(2,1)}, bf16[1024,384]...) custom-call(s32[1]{0:T(128)S(6)} %copy.49.refs_0_, ...), custom_call_target="tpu_custom_call" | custom-call | tf_op jit(solution)/shard_map/pallas_call | solution.py:635
  204.6 73.6 %shard_map.395 = (bf16[1536,768]{1,0:T(8,128)(2,1)}, f32[192,768]{1,0:T(8,128)}, bf16[1024,1536]{1,0:T(8,128)(2,1)}, bf16[1024,1536]{1,0:T(8,128)(2,1)}, bf16[10...) custom-call(s32[1]{0:T(128)S(6)} %copy.49.refs_0_, bf16[1024,1536]{1,0:T(8,128)(2,1)} %refs_10_.5, ...), custom_call_target="tpu_custom_call" | custom-call | tf_op jit(solution)/shard_map/pallas_call | solution.py:635
  278.2 66.6 %shard_map.396 = (bf16[1024,1536]{1,0:T(8,128)(2,1)}, bf16[1024,1536]{1,0:T(8,128)(2,1)}, f32[8,1536]{1,0:T(8,128)}, bf16[4,2,192,768]{3,2,1,0:T(8,128)(2,1)}, b...) custom-call(s32[1]{0:T(128)S(6)} %copy.49.refs_0_, f32[8,1536]{1,0:T(8,128)} %get-tuple-element.87.refs_2_.refs_1_.refs_3_, ...), custom_call_target="tpu_custom_call" | custom-call | tf_op jit(solution)/shard_map/pallas_call | solution.py:635
  344.8 81.5 %shard_map.397 = (bf16[1024,1152]{1,0:T(8,128)(2,1)}, bf16[256,768]{1,0:T(8,128)(2,1)}, f32[8,384]{1,0:T(8,128)}, bf16[1024,1536]{1,0:T(8,128)(2,1)}, bf16[4,2,1...) custom-call(s32[1]{0:T(128)S(6)} %copy.49.refs_0_, ...), custom_call_target="tpu_custom_call" | custom-call | tf_op jit(solution)/shard_map/pallas_call | solution.py:635
  426.4 74.6 %shard_map.398 = (bf16[1024,1536]{1,0:T(8,128)(2,1)}, bf16[1024,1536]{1,0:T(8,128)(2,1)}, f32[8,1,10752]{2,1,0:T(1,128)}, f32[512,384]{1,0:T(8,128)}, f32[512,384]{1,0:T(8,128)}, /*index=5*/f32[192,1536]{1,0:T(8,128)}) custom-call(s32[1]{0:T(128)S(6)} %copy.49.refs_0_, bf16[1024,1152]{1,0:T(8,128)(2,1)} %get-tuple-element.117.refs_1_, ...), custom_call_target="tpu_custom_call" | custom-call | tf_op jit(solution)/shard_map/pallas_call | solution.py:635
  501.0 0.0 copy-start.4
  501.0 0.0 copy-start.1
  501.0 6.5 %shard_map.399 = (f32[192,384]{1,0:T(8,128)}, f32[192,384]{1,0:T(8,128)}, f32[192,384]{1,0:T(8,128)}, f32[192,384]{1,0:T(8,128)}, f32[192,1024]{1,0:T(8,128)}, /...) custom-call(f32[192,768]{1,0:T(8,128)} %get-tuple-element.127.refs_0, ...), custom_call_target="tpu_custom_call" | custom-call | tf_op jit(solution)/shard_map/pallas_call | solution.py:1722
  507.5 1.3 reduce
  508.8 1.3 slice_reduce_fusion
  510.2 0.1 reshape.57
  510.2 0.1 reduce_sum.9
  510.4 0.5 subtract_multiply_fusion
  510.9 1.7 copy.50
  512.5 1.4 copy-done
  513.9 1.7 copy.51
  515.6 0.0 copy-done.3
  515.6 0.9 copy.52
  516.5 0.9 copy.53
  (6 shorter events, 0.0 us)
Async XLA Ops:
  501.0 9.3 %copy-start.4 = (bf16[6]{0:T(256)(128)(2,1)S(1)}, bf16[6]{0:T(256)(128)(2,1)}, u32[]{:S(2)}) copy-start(bf16[6]{0:T(256)(128)(2,1)} %param.46) | copy-start | bytes 40
  501.0 9.9 %copy-start.1 = (bf16[1024,1536]{1,0:T(8,128)(2,1)S(1)}, bf16[1024,1536]{1,0:T(8,128)(2,1)}, u32[]{:S(2)}) copy-start(bf16[1024,1536]{1,0:T(8,128)(2,1)} %get-tuple-element.170) | copy-start | bytes 9437188
  510.9 3.0 copy-start
  513.9 1.7 copy-start.3
  513.9 2.6 copy-start.2

commit v7 on v6

--- a/solution.py
+++ b/solution.py
@@ -838,9 +838,9 @@
         r.fetch.w_tv.wait()
         paced(GRID, opening.multiply, (attn_engine, 2))
         text_engine.start()
-        engine.start()
         finish_pumps(attn_engine)
         attn_engine.arrive()
+        engine.start()
     else:
         greet([], tp_peers())
 

time: 527 us -> 525 us (level)
  no operation moved by 1% of the time
where the time goes in v7:
time: 525 us; the launch traced here: 515 us
  Pallas kernels  501 us (95%)
  local copies, waits for them, and re-layouts  8.62 us (2%)
    pallas_call x5, Pallas kernels, call(): pl.pallas_call(body, out_shape=[shape for shape, _ in outs], in_specs=[sp...  492 us

profile of v7, /device:TPU:0, one launch (start us, length us, event | category | flops | bytes accessed | tf_op | source)
XLA Modules:
  0.0 515.4 jit_solution(11523534843996859921)
XLA Ops:
  1.3 0.7 convert_tanh_fusion
  2.0 0.1 broadcast_in_dim.3
  2.0 0.7 reshape.54.refs_6_
  2.7 1.3 bitcast_convert_fusion.refs_3_
  4.0 2.8 shard_map.393
  6.8 196.2 %shard_map.394 = (f32[1024,384]{1,0:T(8,128)}, f32[1024,384]{1,0:T(8,128)}, bf16[1024,384]{1,0:T(8,128)(2,1)}, bf16[1024,384]{1,0:T(8,128)(2,1)}, bf16[1024,384]...) custom-call(s32[1]{0:T(128)S(6)} %copy.49.refs_0_, ...), custom_call_target="tpu_custom_call" | custom-call | tf_op jit(solution)/shard_map/pallas_call | solution.py:635
  202.9 73.1 %shard_map.395 = (bf16[1536,768]{1,0:T(8,128)(2,1)}, f32[192,768]{1,0:T(8,128)}, bf16[1024,1536]{1,0:T(8,128)(2,1)}, bf16[1024,1536]{1,0:T(8,128)(2,1)}, bf16[10...) custom-call(s32[1]{0:T(128)S(6)} %copy.49.refs_0_, bf16[1024,1536]{1,0:T(8,128)(2,1)} %refs_10_.5, ...), custom_call_target="tpu_custom_call" | custom-call | tf_op jit(solution)/shard_map/pallas_call | solution.py:635
  276.0 66.6 %shard_map.396 = (bf16[1024,1536]{1,0:T(8,128)(2,1)}, bf16[1024,1536]{1,0:T(8,128)(2,1)}, f32[8,1536]{1,0:T(8,128)}, bf16[4,2,192,768]{3,2,1,0:T(8,128)(2,1)}, b...) custom-call(s32[1]{0:T(128)S(6)} %copy.49.refs_0_, f32[8,1536]{1,0:T(8,128)} %get-tuple-element.87.refs_2_.refs_1_.refs_3_, ...), custom_call_target="tpu_custom_call" | custom-call | tf_op jit(solution)/shard_map/pallas_call | solution.py:635
  342.6 81.7 %shard_map.397 = (bf16[1024,1152]{1,0:T(8,128)(2,1)}, bf16[256,768]{1,0:T(8,128)(2,1)}, f32[8,384]{1,0:T(8,128)}, bf16[1024,1536]{1,0:T(8,128)(2,1)}, bf16[4,2,1...) custom-call(s32[1]{0:T(128)S(6)} %copy.49.refs_0_, ...), custom_call_target="tpu_custom_call" | custom-call | tf_op jit(solution)/shard_map/pallas_call | solution.py:635
  424.3 74.5 %shard_map.398 = (bf16[1024,1536]{1,0:T(8,128)(2,1)}, bf16[1024,1536]{1,0:T(8,128)(2,1)}, f32[8,1,10752]{2,1,0:T(1,128)}, f32[512,384]{1,0:T(8,128)}, f32[512,384]{1,0:T(8,128)}, /*index=5*/f32[192,1536]{1,0:T(8,128)}) custom-call(s32[1]{0:T(128)S(6)} %copy.49.refs_0_, bf16[1024,1152]{1,0:T(8,128)(2,1)} %get-tuple-element.117.refs_1_, ...), custom_call_target="tpu_custom_call" | custom-call | tf_op jit(solution)/shard_map/pallas_call | solution.py:635
  498.8 0.0 copy-start.4
  498.8 6.5 %shard_map.399 = (f32[192,384]{1,0:T(8,128)}, f32[192,384]{1,0:T(8,128)}, f32[192,384]{1,0:T(8,128)}, f32[192,384]{1,0:T(8,128)}, f32[192,1024]{1,0:T(8,128)}, /...) custom-call(f32[192,768]{1,0:T(8,128)} %get-tuple-element.127.refs_0, ...), custom_call_target="tpu_custom_call" | custom-call | tf_op jit(solution)/shard_map/pallas_call | solution.py:1722
  505.3 1.3 reduce
  506.6 1.3 slice_reduce_fusion
  508.0 0.1 reshape.57
  508.0 0.1 reduce_sum.9
  508.2 0.5 subtract_multiply_fusion
  508.7 0.0 copy-done.1
  508.7 1.7 copy.50
  510.4 1.4 copy-done
  511.7 1.7 copy.51
  513.4 0.0 copy-done.3
  513.4 0.9 copy.52
  514.3 0.9 copy.53
  (6 shorter events, 0.0 us)
Async XLA Ops:
  498.8 9.3 %copy-start.4 = (bf16[6]{0:T(256)(128)(2,1)S(1)}, bf16[6]{0:T(256)(128)(2,1)}, u32[]{:S(2)}) copy-start(bf16[6]{0:T(256)(128)(2,1)} %param.46) | copy-start | bytes 40
  498.8 9.9 %copy-start.1 = (bf16[1024,1536]{1,0:T(8,128)(2,1)S(1)}, bf16[1024,1536]{1,0:T(8,128)(2,1)}, u32[]{:S(2)}) copy-start(bf16[1024,1536]{1,0:T(8,128)(2,1)} %get-tuple-element.170) | copy-start | bytes 9437188
  508.7 3.0 copy-start
  511.7 1.7 copy-start.3
  511.7 2.6 copy-start.2
